TPU v7x, 32 devices: a whole 2x2x4 slice. The times are simulated.
32 devices in a mesh: head: 4 (over y, x), tok: 8 (over z, core).
Axes of the slice: x: 2, y: 2, z: 4, core: 2. Of those that a mesh axis runs over, the one named last changes fastest.
Arguments:
- tokens: bfloat16 [4096, 8192], P('tok', 'head'), may hold values from -20 to 20
- qkv_maps: bfloat16 [16, 512, 1536], P('head'), may hold values from -0.26516504 to 0.26516504
- rate_map: bfloat16 [8192, 16], P('head'), may hold values from -0.09375 to 0.09375
- fast_init: bfloat16 [16, 3, 512, 512], P('head'), may hold values from -0.25 to 0.25
Outputs:
- layer_out: bfloat16 [4096, 8192], P('tok', 'head')
All inputs are finite; a program needn't handle non-finite values.
Results may differ from a plain program's by a relative error of at most 0.04.
Values may be sent and summed in bfloat16 or wider, within the bound.
No kernel may reach another device: no remote copies, remote signals or barrier semaphores. Data moves between devices by JAX's collectives and lax.ppermute only.
A program may use at most 128 MiB of HBM per device.

v0:
```python
import jax
import jax.numpy as jnp
from jax import lax
from jax.sharding import PartitionSpec as P

WINDOW = 512


rate_base = 0.003
epsilon = 1e-06


def from_behind(block, axis, distance):
    devices = range(lax.axis_size(axis))
    route = [(i - distance, i) for i in devices if i - distance in devices]
    return lax.ppermute(block, axis, route)


def rms_rows(matrix):
    matrix = matrix.astype(jnp.float32)
    return matrix / jnp.sqrt(jnp.mean(matrix * matrix, axis=-1, keepdims=True) + epsilon)


def renorm(updated, initial):
    target = jnp.sqrt(jnp.mean(initial * initial, axis=-1, keepdims=True) + epsilon)
    current = jnp.sqrt(jnp.mean(updated * updated, axis=-1, keepdims=True) + epsilon)
    return (updated * (target / current)).astype(jnp.bfloat16)


def band_attention(queries, key_rows, value_rows, query_pos, key_pos, score_scale):
    scores = (
        jnp.einsum("qhd,khd->hqk", queries, key_rows, preferred_element_type=jnp.float32)
        * score_scale
    )
    key_mask = (
        (key_pos[None, :] <= query_pos[:, None])
        & (key_pos[None, :] > query_pos[:, None] - WINDOW)
        & (key_pos[None, :] >= 0)
    )
    key_mask = key_mask[None]
    row_max = jnp.max(jnp.where(key_mask, scores, -1e30), axis=2, keepdims=True)
    raised = jnp.where(key_mask, jnp.exp(scores - row_max), 0.0)
    probs = (raised / jnp.sum(raised, axis=2, keepdims=True)).astype(jnp.bfloat16)
    return jnp.einsum("hqk,khd->qhd", probs, value_rows, preferred_element_type=jnp.float32)


def fast_gradient(weights, key_part, value_part, rate_part):
    pre_gate = jnp.einsum(
        "rhd,hde->rhe", key_part, weights[:, 0], preferred_element_type=jnp.float32
    )
    pre_up = jnp.einsum("rhd,hde->rhe", key_part, weights[:, 1], preferred_element_type=jnp.float32)
    sigma = jax.nn.sigmoid(pre_gate)
    gated = pre_gate * sigma
    hidden = (gated * pre_up).astype(jnp.bfloat16)
    target = (rate_part.astype(jnp.float32)[:, :, None] * value_part.astype(jnp.float32)).astype(
        jnp.bfloat16
    )
    grad_down = jnp.einsum("rhe,rhd->hed", hidden, target, preferred_element_type=jnp.float32)
    back_hidden = jnp.einsum(
        "rhd,hed->rhe", target, weights[:, 2], preferred_element_type=jnp.float32
    )
    gate_delta = (back_hidden * pre_up * sigma * (1.0 + pre_gate * (1.0 - sigma))).astype(
        jnp.bfloat16
    )
    up_delta = (back_hidden * gated).astype(jnp.bfloat16)
    grad_gate = jnp.einsum("rhd,rhe->hde", key_part, gate_delta, preferred_element_type=jnp.float32)
    grad_up = jnp.einsum("rhd,rhe->hde", key_part, up_delta, preferred_element_type=jnp.float32)
    return jnp.stack([grad_gate, grad_up, grad_down], 1)


def fast_apply(weights, query_part):
    app_gate = jnp.einsum(
        "rhd,hde->rhe", query_part, weights[:, 0], preferred_element_type=jnp.float32
    )
    app_up = jnp.einsum(
        "rhd,hde->rhe", query_part, weights[:, 1], preferred_element_type=jnp.float32
    )
    app_hidden = (app_gate * jax.nn.sigmoid(app_gate) * app_up).astype(jnp.bfloat16)
    result = jnp.einsum(
        "rhe,hed->rhd", app_hidden, weights[:, 2], preferred_element_type=jnp.float32
    )
    return result.astype(jnp.bfloat16)


def update_weights(weights, partial_value, initial):
    total = lax.psum(partial_value.astype(jnp.bfloat16), "tok").astype(jnp.float32)
    return renorm(weights.astype(jnp.float32) + total, initial)


def body(tokens, qkv_maps, rate_map, fast_init):
    tok_rows = tokens.shape[0]
    head_count = qkv_maps.shape[0]
    head_width = qkv_maps.shape[1]
    groups = lax.axis_size("tok")
    logit_terms = jnp.dot(tokens, rate_map, preferred_element_type=jnp.float32)
    logits = lax.psum_scatter(
        logit_terms.astype(jnp.bfloat16), "head", scatter_dimension=1, tiled=True
    ).astype(jnp.float32)
    rate = (rate_base * jax.nn.softplus(logits)).astype(jnp.bfloat16)
    inputs = tokens.reshape(tok_rows, head_count, head_width)
    projected = jnp.einsum("rhd,hde->rhe", inputs, qkv_maps, preferred_element_type=jnp.float32)
    queries = projected[:, :, :head_width].astype(jnp.bfloat16)
    key_rows = projected[:, :, head_width : 2 * head_width].astype(jnp.bfloat16)
    value_rows = projected[:, :, 2 * head_width :].astype(jnp.bfloat16)
    tail_rows = min(WINDOW, tok_rows)
    edge = jnp.stack([key_rows, value_rows], 0)
    distance = 0
    received = [from_behind(edge, "tok", distance + 1)]
    anchor = lax.axis_index("tok") * tok_rows
    offsets = jnp.arange(tail_rows, dtype=jnp.int32)
    distance = 1
    arrived = received[distance - 1]
    key_parts = [arrived[0]]
    value_parts = [arrived[1]]
    position_parts = [anchor - distance * tok_rows + tok_rows - tail_rows + offsets]
    local_pos = anchor + jnp.arange(tok_rows, dtype=jnp.int32)
    all_keys = jnp.concatenate(key_parts + [key_rows], 0)
    all_values = jnp.concatenate(value_parts + [value_rows], 0)
    all_pos = jnp.concatenate(position_parts + [local_pos], 0)
    attended = band_attention(
        queries, all_keys, all_values, local_pos, all_pos, head_width ** (-0.5)
    )
    q_norm = rms_rows(queries).astype(jnp.bfloat16)
    k_norm = rms_rows(key_rows).astype(jnp.bfloat16)
    initial = fast_init.astype(jnp.float32)
    weights = fast_init
    own_block = lax.axis_index("tok") // (groups // 2)
    fast_out = jnp.zeros_like(q_norm)
    for half_index in range(2):
        partial_value = fast_gradient(weights, k_norm, value_rows, rate)
        partial_value = jnp.where(own_block == half_index, partial_value, 0.0)
        weights = update_weights(weights, partial_value, initial)
        applied = fast_apply(weights, q_norm)
        fast_out = jnp.where(own_block == half_index, applied, fast_out)
    combined = (attended + fast_out.astype(jnp.float32)).astype(jnp.bfloat16)
    return combined.reshape(tok_rows, head_count * head_width)


def solution(mesh):
    in_specs = (
        P("tok", "head"),
        P("head", None, None),
        P("head", None),
        P("head", None, None, None),
    )
    out_specs = P("tok", "head")
    return jax.shard_map(body, mesh=mesh, in_specs=in_specs, out_specs=out_specs, check_vma=False)
```

profile of v0, /device:TPU:8, one launch (start us, length us, event | category | flops | bytes accessed | tf_op | source)
XLA Modules:
  0.0 457.4 jit_solution(3486646701272989900)
XLA Ops:
  6.5 10.2 %convert_bitcast_fusion = bf16[512,4,1536]{0,2,1:T(8,128)(2,1)} fusion(bf16[4,512,1536]{2,1,0:T(8,128)(2,1)} %param.5, bf16[64,4,8,512]{3,2,1,0:T(8,128)(2,1)} %bitcast.203), kind=kOutput, calls=%fused_computation.18 | convolution fusion | flops 3224371200 | bytes 14680064 | tf_op jit(solution)/shard_map/rhd,hde->rhe/dot_general | solution.py:101
  19.8 5.0 %fusion.57 = f32[4,512,512]{2,1,0:T(8,128)} fusion(f32[512,4]{0,1:T(4,128)S(1)} %add_sqrt_fusion.2, bf16[512,4,1536]{0,2,1:T(8,128)(2,1)} %convert_bitcast_fusion, bf16[4,3,512,512]{3,2,1,0:T(8,128)(2,1)S(1)} %copy-done.3), kind=kOutput, calls=%fused_computation.102 | convolution fusion | flops 1076887552 | bytes 8396800 | tf_op jit(solution)/shard_map/rhd,hde->rhe/dot_general | solution.py:48
  24.8 5.1 %fusion.58 = f32[4,512,512]{2,1,0:T(8,128)} fusion(f32[512,4]{0,1:T(4,128)S(1)} %add_sqrt_fusion.2, bf16[512,4,1536]{0,2,1:T(8,128)(2,1)} %convert_bitcast_fusion, bf16[4,3,512,512]{3,2,1,0:T(8,128)(2,1)S(1)} %copy-done.3), kind=kOutput, calls=%fused_computation.104 | convolution fusion | flops 1076887552 | bytes 8396800 | tf_op jit(solution)/shard_map/rhd,hde->rhe/dot_general | solution.py:51
  30.5 16.3 %all-reduce = bf16[512,16]{0,1:T(8,128)(2,1)S(1)} all-reduce(bf16[512,16]{0,1:T(8,128)(2,1)S(1)} %convolution_convert_fusion), channel_id=2, replica_groups=mesh['head'=4,'tok'=8] {'head'}, use_global_device_ids=true, to_apply=%region_3.4.clone | all-reduce | flops 8192 | bytes 32768
  52.9 5.9 %convolution_bitcast_fusion.3 = bf16[4,1,512,512]{3,2,0,1:T(8,128)(2,1)} fusion(f32[4,512,512]{2,1,0:T(8,128)} %fusion.58, f32[512,4]{0,1:T(4,128)S(1)} %fusion.76, f32[4,512,512]{2,1,0:T(8,128)S(1)} %copy-done.9, bf16[512,4,1536]{0,2,1:T(8,128)(2,1)S(1)} %bitcast.200), kind=kOutput, calls=%fused_computation.88 | convolution fusion | flops 1083179008 | bytes 12591104 | tf_op jit(solution)/shard_map/rhe,rhd->hed/dot_general | solution.py:58
  65.3 6.8 %fusion.2 = bf16[4,3,512,512]{3,2,0,1:T(8,128)(2,1)} fusion(bf16[4,1,512,512]{3,2,0,1:T(8,128)(2,1)} %convolution_bitcast_fusion.3, bf16[4,1,512,512]{3,2,0,1:T(8,128)(2,1)} %convolution_bitcast_fusion.4, bf16[4,1,512,512]{3,2,0,1:T(8,128)(2,1)} %convolution_bitcast_fusion.5, pred[]{:T(512)S(6)} %eq.9), kind=kLoop, calls=%fused_computation.5 | loop fusion | flops 22020096 | bytes 12582913 | tf_op jit(solution)/shard_map/convert_element_type | solution.py:86
  72.2 4.4 fusion.107
  81.9 159.3 %all-reduce.4.cloned.1.call-done = bf16[4,3,512,512]{3,2,0,1:T(8,128)(2,1)} async-done(((bf16[4,3,512,512]{3,2,0,1:T(8,128)(2,1)}), bf16[4,3,512,512]{3,2,0,1:T(8,128)(2,1)}) %all-reduce.4.cloned.1.call-update) | async-done | bytes 6291472 | tf_op jit(solution)/shard_map/psum | solution.py:86
  241.2 8.3 %fusion.1 = (f32[4,3,512]{2,0,1:T(4,128)S(1)}, f32[4,3,512]{2,0,1:T(4,128)S(1)}) fusion(bf16[4,3,512,512]{3,2,1,0:T(8,128)(2,1)} %param.7, bf16[4,3,512,512]{3,2,0,1:T(8,128)(2,1)} %all-reduce.4.cloned.1.call-done), kind=kLoop, calls=%fused_computation.3 | loop fusion | flops 22007808 | bytes 12632064 | tf_op jit(solution)/shard_map/reduce_sum | solution.py:25
  249.6 4.6 %multiply_convert_fusion.1 = bf16[4,3,512,512]{3,2,0,1:T(8,128)(2,1)S(1)} fusion(bf16[4,3,512,512]{3,2,0,1:T(8,128)(2,1)S(1)} %copy-done.4, f32[4,3,512]{2,0,1:T(4,128)S(1)} %rsqrt_multiply_fusion.1, bf16[4,3,512,512]{3,2,1,0:T(8,128)(2,1)} %param.7), kind=kLoop, calls=%fused_computation.11 | loop fusion | flops 15728640 | bytes 18898944 | tf_op jit(solution)/shard_map/convert_element_type | solution.py:27
  260.1 4.5 convolution_bitcast_fusion
  264.6 4.6 convolution_bitcast_fusion.2
  271.2 3.9 fusion.3
  275.1 5.5 %fusion.65 = f32[4,512,512]{1,2,0:T(8,128)} fusion(bf16[4,3,512,512]{3,2,0,1:T(8,128)(2,1)} %copy-done.2, f32[512,4]{0,1:T(4,128)S(1)} %add_sqrt_fusion.1, bf16[512,4,1536]{0,2,1:T(8,128)(2,1)} %convert_bitcast_fusion), kind=kOutput, calls=%fused_computation.113 | convolution fusion | flops 1076887552 | bytes 8396800 | tf_op jit(solution)/shard_map/rhd,hde->rhe/dot_general | solution.py:72
  280.6 8.9 %fusion.62 = bf16[4,512,512]{2,1,0:T(8,128)(2,1)} fusion(bf16[4,3,512,512]{3,2,0,1:T(8,128)(2,1)} %copy-done.2, f32[4,512,512]{1,2,0:T(8,128)} %fusion.65, f32[512,4]{0,1:T(4,128)S(1)} %add_sqrt_fusion.1, bf16[512,4,1536]{0,2,1:T(8,128)(2,1)} %convert_bitcast_fusion), kind=kOutput, calls=%fused_computation.110 | convolution fusion | flops 2156920832 | bytes 12591104 | tf_op jit(solution)/shard_map/rhe,hed->rhd/dot_general | solution.py:79
  289.5 3.8 slice_bitcast_fusion.16
  293.3 4.0 fusion.16
  297.3 6.1 %fusion.108 = (f32[4,512]{1,0:T(4,128)S(1)}, f32[4,512,1024]{2,1,0:T(8,128)}) fusion(f32[4,512,1024]{2,1,0:T(8,128)S(1)} %fusion.16, pred[512,1024]{1,0:T(8,128)(4,1)S(1)} %and_and_fusion), kind=kOutput, calls=%fused_computation.156 | output fusion | flops 12583935 | bytes 17309696 | tf_op jit(solution)/shard_map/sub | solution.py:42
  303.4 109.1 %all-reduce.6.cloned.1.call-done = bf16[4,3,512,512]{3,2,0,1:T(8,128)(2,1)} async-done(((bf16[4,3,512,512]{3,2,0,1:T(8,128)(2,1)}), bf16[4,3,512,512]{3,2,0,1:T(8,128)(2,1)}) %all-reduce.6.cloned.1.call-update) | async-done | bytes 6291472 | tf_op jit(solution)/shard_map/psum | solution.py:86
  412.5 6.9 %multiply_reduce_fusion = f32[4,3,512]{2,0,1:T(4,128)S(1)} fusion(bf16[4,3,512,512]{3,2,0,1:T(8,128)(2,1)} %all-reduce.6.cloned.1.call-done, bf16[4,3,512,512]{3,2,0,1:T(8,128)(2,1)} %copy-done.2), kind=kLoop, calls=%fused_computation.9 | loop fusion | flops 15722496 | bytes 12607488 | tf_op jit(solution)/shard_map/reduce_sum | solution.py:26
  419.5 4.7 %multiply_convert_fusion = bf16[4,3,512,512]{3,2,0,1:T(8,128)(2,1)S(1)} fusion(bf16[4,3,512,512]{3,2,0,1:T(8,128)(2,1)S(1)} %copy-done.5, bf16[4,3,512,512]{3,2,0,1:T(8,128)(2,1)} %copy-done.2, f32[4,3,512]{2,0,1:T(4,128)S(1)} %rsqrt_multiply_fusion), kind=kLoop, calls=%fused_computation.8 | loop fusion | flops 15728640 | bytes 18898944 | tf_op jit(solution)/shard_map/convert_element_type | solution.py:27
  426.9 5.0 %fusion.55 = f32[4,512,512]{1,2,0:T(8,128)} fusion(bf16[4,3,512,512]{3,2,0,1:T(8,128)(2,1)S(1)} %multiply_convert_fusion, f32[512,4]{0,1:T(4,128)S(1)} %add_sqrt_fusion.1, bf16[512,4,1536]{0,2,1:T(8,128)(2,1)} %convert_bitcast_fusion), kind=kOutput, calls=%fused_computation.95 | convolution fusion | flops 1076887552 | bytes 8396800 | tf_op jit(solution)/shard_map/rhd,hde->rhe/dot_general | solution.py:72
  431.9 8.3 %fusion.56 = bf16[4,512,512]{2,1,0:T(8,128)(2,1)} fusion(bf16[4,3,512,512]{3,2,0,1:T(8,128)(2,1)} %copy-done.6, f32[4,512,512]{1,2,0:T(8,128)} %fusion.55, f32[512,4]{0,1:T(4,128)S(1)} %add_sqrt_fusion.1, bf16[512,4,1536]{0,2,1:T(8,128)(2,1)} %convert_bitcast_fusion), kind=kOutput, calls=%fused_computation.97 | convolution fusion | flops 2156920832 | bytes 12591104 | tf_op jit(solution)/shard_map/rhe,hed->rhd/dot_general | solution.py:79
  440.2 7.8 %add_convert_fusion = bf16[4,512,512]{2,1,0:T(8,128)(2,1)S(1)} fusion(bf16[4,512,512]{2,1,0:T(8,128)(2,1)} %fusion.62, bf16[4,512,512]{2,1,0:T(8,128)(2,1)} %fusion.56, pred[]{:T(512)S(6)} %eq.9, pred[]{:T(512)S(6)} %eq.8, f32[4,512,1024]{2,1,0:T(8,128)} %get-tuple-element.16, f32[4,512]{1,0:T(4,128)S(1)} %get-tuple-element.15, ...), kind=kOutput, calls=%fused_computation.80 | convolution fusion | flops 2165309440 | bytes 18882562 | tf_op jit(solution)/shard_map/hqk,khd->qhd/dot_general | solution.py:44
  (60 shorter events, 33.9 us)
Async XLA Ops:
  6.5 23.3 %copy-start = (bf16[2048,16]{0,1:T(8,128)(2,1)S(1)}, bf16[2048,16]{0,1:T(8,128)(2,1)}, u32[]{:S(2)}) copy-start(bf16[2048,16]{0,1:T(8,128)(2,1)} %param.6) | copy-start | bytes 196612
  6.5 234.6 %all-reduce.4.cloned.1.call-start = ((), (), s32[]{:S(2)}) async-start(), calls=%async_computation | async-start | bytes 12582912 | tf_op jit(solution)/shard_map/psum | solution.py:86
  6.5 13.3 %copy-start.3 = (bf16[4,3,512,512]{3,2,1,0:T(8,128)(2,1)S(1)}, bf16[4,3,512,512]{3,2,1,0:T(8,128)(2,1)}, u32[]{:S(2)}) copy-start(bf16[4,3,512,512]{3,2,1,0:T(8,128)(2,1)} %param.7) | copy-start | bytes 18874372
  24.8 5.1 %copy-start.7 = (bf16[512,2048]{1,0:T(8,128)(2,1)S(1)}, bf16[512,2048]{1,0:T(8,128)(2,1)}, u32[]{:S(2)}) copy-start(bf16[512,2048]{1,0:T(8,128)(2,1)} %param.4) | copy-start | bytes 6291460
  24.8 22.1 %copy-start.8 = (u32[32]{0:T(128)S(1)}, u32[32]{0:T(128)}, u32[]{:S(2)}) copy-start(u32[32]{0:T(128)} %constant.60) | copy-start | bytes 388
  29.9 22.1 %slice-start = ((s8[6291456]{0:T(1024)(128)(4,1)}), s8[2097152]{0:T(1024)(128)(4,1)S(1)}, s32[]{:S(2)}) async-start(s8[6291456]{0:T(1024)(128)(4,1)} %bitcast.199), calls=%async_computation.2 | async-start | bytes 4194304
  48.1 3.9 slice-start.1
  48.1 4.7 %copy-start.9 = (f32[4,512,512]{2,1,0:T(8,128)S(1)}, f32[4,512,512]{2,1,0:T(8,128)}, u32[]{:S(2)}) copy-start(f32[4,512,512]{2,1,0:T(8,128)} %fusion.57) | copy-start | bytes 12582916
  52.9 5.9 %copy-start.10 = (f32[4,512,512]{2,1,0:T(8,128)S(1)}, f32[4,512,512]{2,1,0:T(8,128)}, u32[]{:S(2)}) copy-start(f32[4,512,512]{2,1,0:T(8,128)} %fusion.58) | copy-start | bytes 12582916
  72.1 340.4 %all-reduce.6.cloned.1.call-start = ((), (), s32[]{:S(2)}) async-start(), calls=%async_computation.1 | async-start | bytes 12582912 | tf_op jit(solution)/shard_map/psum | solution.py:86
  78.9 210.5 %collective-permute-start = (bf16[2,512,4,512]{1,3,2,0:T(8,128)(2,1)}, bf16[2,512,4,512]{1,3,2,0:T(8,128)(2,1)}, u32[]{:S(2)}, u32[]{:S(2)}) collective-permute-start(bf16[2,512,4,512]{1,3,2,0:T(8,128)(2,1)} %pad_maximum_fusion), channel_id=1, source_target_pairs={{0,1},{1,2},{2,3},{3,4},{4,5},{5,6},{6,7},{8,9},{9,10},{10,11},{11... | collective-permute-start | bytes 12582920 | tf_op jit(solution)/shard_map/ppermute | solution.py:16
  241.2 8.4 %copy-start.4 = (bf16[4,3,512,512]{3,2,0,1:T(8,128)(2,1)S(1)}, bf16[4,3,512,512]{3,2,0,1:T(8,128)(2,1)}, u32[]{:S(2)}) copy-start(bf16[4,3,512,512]{3,2,0,1:T(8,128)(2,1)} %all-reduce.4.cloned.1.call-done) | copy-start | bytes 18874372
  241.2 13.0 %slice-start.2 = ((s8[6291456]{0:T(1024)(128)(4,1)}), s8[4194304]{0:T(1024)(128)(4,1)S(1)}, s32[]{:S(2)}) async-start(s8[6291456]{0:T(1024)(128)(4,1)} %bitcast.201), calls=%async_computation.4 | async-start | bytes 8388608
  249.5 4.6 %slice-start.3 = ((s8[6291456]{0:T(1024)(128)(4,1)}), s8[2097152]{0:T(1024)(128)(4,1)S(1)}, s32[]{:S(2)}) async-start(s8[6291456]{0:T(1024)(128)(4,1)} %bitcast.201), calls=%async_computation.5 | async-start | bytes 4194304
  254.2 4.6 %copy-start.2 = (bf16[4,3,512,512]{3,2,0,1:T(8,128)(2,1)}, bf16[4,3,512,512]{3,2,0,1:T(8,128)(2,1)S(1)}, u32[]{:S(2)}) copy-start(bf16[4,3,512,512]{3,2,0,1:T(8,128)(2,1)S(1)} %multiply_convert_fusion.1) | copy-start | bytes 18874372
  412.5 6.9 %copy-start.5 = (bf16[4,3,512,512]{3,2,0,1:T(8,128)(2,1)S(1)}, bf16[4,3,512,512]{3,2,0,1:T(8,128)(2,1)}, u32[]{:S(2)}) copy-start(bf16[4,3,512,512]{3,2,0,1:T(8,128)(2,1)} %all-reduce.6.cloned.1.call-done) | copy-start | bytes 18874372
  424.2 2.7 copy-start.6
  440.2 10.2 %copy-start.1 = (bf16[2048,16]{0,1:T(8,128)(2,1)S(1)}, bf16[2048,16]{0,1:T(8,128)(2,1)}, u32[]{:S(2)}) copy-start(bf16[2048,16]{0,1:T(8,128)(2,1)} %param.6) | copy-start | bytes 196612
Sparse Core Ops, SparseCore 0:
  72.2 168.8 all-reduce.3
  275.3 137.2 all-reduce.5
where the time goes:
time: 466 us; the launch traced here: 457 us
  waiting for transfers between devices  268 us (58%)
  matrix products  93.5 us (20%)
  other arithmetic  47.3 us (10%)
  blocking collectives  16.3 us (3%)
  local copies, waits for them, and re-layouts  14.8 us (3%)
  between operations  14.6 us (3%)
    psum x2, waiting for transfers between devices, update_weights(): lax.psum(partial_value.astype(jnp.bfloat16), 'tok').astype(jnp.float32)  268 us
    dot_general x2, matrix products, fast_apply(): jnp.einsum('rhe,hed->rhd', app_hidden, weights[:, 2], preferred_element_t...  17.2 us
    unnamed x1, blocking collectives  16.3 us
    convert_element_type x2, other arithmetic, update_weights(): partial_value.astype(jnp.bfloat16)  10.7 us
    dot_general x2, matrix products, fast_apply(): jnp.einsum('rhd,hde->rhe', query_part, weights[:, 0], preferred_element_t...  10.4 us
    dot_general x2, matrix products, fast_gradient(): jnp.einsum('rhe,rhd->hed', hidden, target, preferred_element_type=jnp.flo...  10.4 us
    dot_general x1, matrix products, body(): jnp.einsum('rhd,hde->rhe', inputs, qkv_maps, preferred_element_type=jnp.f...  10.2 us
    convert_element_type x2, other arithmetic, renorm(): return (updated * (target / current)).astype(jnp.bfloat16)  9.32 us
  transfers between devices with their start and end apart: 3, of which 2 were waited for; matrix products, arithmetic and copies ran while one was open for 15% of the time, Pallas kernels for 0%

commit v1 on v0

--- a/solution.py
+++ b/solution.py
@@ -1,6 +1,10 @@
+import functools
+
 import jax
 import jax.numpy as jnp
 from jax import lax
+from jax.experimental import pallas as pl
+from jax.experimental.pallas import tpu as pltpu
 from jax.sharding import PartitionSpec as P
 
 WINDOW = 512
@@ -8,6 +12,7 @@
 
 rate_base = 0.003
 epsilon = 1e-06
+VMEM_LIMIT = 48 * 1024 * 1024
 
 
 def from_behind(block, axis, distance):
@@ -87,7 +92,7 @@
     return renorm(weights.astype(jnp.float32) + total, initial)
 
 
-def body(tokens, qkv_maps, rate_map, fast_init):
+def general_body(tokens, qkv_maps, rate_map, fast_init):
     tok_rows = tokens.shape[0]
     head_count = qkv_maps.shape[0]
     head_width = qkv_maps.shape[1]
@@ -136,6 +141,280 @@
     return combined.reshape(tok_rows, head_count * head_width)
 
 
+def matmul(left, right):
+    return jnp.dot(left, right, preferred_element_type=jnp.float32)
+
+
+def matmul_nt(left, right):
+    return lax.dot_general(left, right, (((1,), (1,)), ((), ())), preferred_element_type=jnp.float32)
+
+
+def matmul_tn(left, right):
+    return lax.dot_general(left, right, (((0,), (0,)), ((), ())), preferred_element_type=jnp.float32)
+
+
+def unit_rows(rows):
+    rows = rows.astype(jnp.float32)
+    scale = lax.rsqrt(jnp.mean(rows * rows, axis=-1, keepdims=True) + epsilon)
+    return (rows * scale).astype(jnp.bfloat16)
+
+
+def logistic(a):
+    return 0.5 * jnp.tanh(0.5 * a) + 0.5
+
+
+def project_kernel(width, table, x0, x1, x2, x3, maps, q_out, k_out, v_out):
+    step = pl.program_id(0)
+
+    def block(x_ref, own):
+        x = x_ref[...]
+        if own:
+            q_out[0] = matmul(x, maps[0, :, :width]).astype(jnp.bfloat16)
+        k_out[0] = matmul(x, maps[0, :, width : 2 * width]).astype(jnp.bfloat16)
+        v_out[0] = matmul(x, maps[0, :, 2 * width :]).astype(jnp.bfloat16)
+
+    for at, x_ref in enumerate((x0, x1, x2, x3)):
+        pl.when(step == at)(functools.partial(block, x_ref, at % 2 == 0))
+
+
+def project(table, blocks, maps):
+    rows, width = blocks[0].shape
+    count = len(blocks)
+    whole = pl.BlockSpec((rows, width), lambda i, t: (0, 0))
+    out = functools.partial(pl.BlockSpec, (1, rows, width))
+    return pl.pallas_call(
+        functools.partial(project_kernel, width),
+        grid_spec=pltpu.PrefetchScalarGridSpec(
+            num_scalar_prefetch=1,
+            grid=(count,),
+            in_specs=[whole] * count + [pl.BlockSpec((1, width, 3 * width), lambda i, t: (t[0], 0, 0))],
+            out_specs=[
+                out(lambda i, t: (i // 2, 0, 0)),
+                out(lambda i, t: (i, 0, 0)),
+                out(lambda i, t: (i, 0, 0)),
+            ],
+        ),
+        out_shape=[
+            jax.ShapeDtypeStruct((count // 2, rows, width), jnp.bfloat16),
+            jax.ShapeDtypeStruct((count, rows, width), jnp.bfloat16),
+            jax.ShapeDtypeStruct((count, rows, width), jnp.bfloat16),
+        ],
+        compiler_params=pltpu.CompilerParams(vmem_limit_bytes=VMEM_LIMIT),
+        name="project",
+    )(table, *blocks, maps)
+
+
+def attend_kernel(slots, table, q, k_now, v_now, k_near, v_near, k_far, v_far, out):
+    step = pl.program_id(0)
+    rows, width = q.shape[1:]
+    part = rows // 2
+    place = table[1 + step]
+    is_far = place >= slots
+    bound = jnp.where(table[1 + slots + step] > 0, 0, rows)
+    row = lax.broadcasted_iota(jnp.int32, (part, rows + part), 0)
+    column = lax.broadcasted_iota(jnp.int32, (part, rows + part), 1)
+
+    def block(k_before, v_before):
+        for at in range(2):
+            first = at * part
+            queries = q[0, first : first + part]
+            keys = jnp.concatenate([k_before[0, first:], k_now[0, : first + part]], 0)
+            values = jnp.concatenate([v_before[0, first:], v_now[0, : first + part]], 0)
+            scores = matmul_nt(queries, keys) * (width ** -0.5)
+            mask = (column > row) & (column <= row + rows) & (column >= bound - first)
+            scores = jnp.where(mask, scores, -1e30)
+            raised = jnp.exp(scores - jnp.max(scores, axis=1, keepdims=True))
+            total = jnp.sum(raised, axis=1, keepdims=True)
+            out[0, first : first + part] = matmul(raised.astype(jnp.bfloat16), values) / total
+
+    pl.when(jnp.logical_not(is_far))(lambda: block(k_near, v_near))
+    pl.when(is_far)(lambda: block(k_far, v_far))
+
+
+def attend(table, q, k_now, v_now, k_near, v_near, k_far, v_far):
+    slots, rows, width = q.shape
+    block = functools.partial(pl.BlockSpec, (1, rows, width))
+    now = block(lambda i, t: (2 * i, 0, 0))
+    near = block(lambda i, t: (2 * jnp.minimum(t[1 + i], slots - 1) + 1, 0, 0))
+    far = block(lambda i, t: (2 * jnp.maximum(t[1 + i] - slots, 0) + 1, 0, 0))
+    each = block(lambda i, t: (i, 0, 0))
+    return pl.pallas_call(
+        functools.partial(attend_kernel, slots),
+        grid_spec=pltpu.PrefetchScalarGridSpec(
+            num_scalar_prefetch=1,
+            grid=(slots,),
+            in_specs=[each, now, now, near, near, far, far],
+            out_specs=each,
+        ),
+        out_shape=jax.ShapeDtypeStruct((slots, rows, width), jnp.float32),
+        compiler_params=pltpu.CompilerParams(vmem_limit_bytes=VMEM_LIMIT),
+        name="attend",
+    )(table, q, k_now, v_now, k_near, v_near, k_far, v_far)
+
+
+def fast_kernel(count, table, k, v, rate, weights, initial, q, attended, out, new, grads):
+    step = pl.program_id(0)
+    active = table[1] > 0
+    width = k.shape[2]
+
+    @pl.when(active & (step == 0))
+    def _():
+        grads[...] = jnp.zeros_like(grads)
+
+    @pl.when(active & (step < count))
+    def _():
+        keys = unit_rows(k[0])
+        spread = jnp.concatenate([rate[0]] * (width // rate.shape[2]), 1).astype(jnp.float32)
+        target = (spread * v[0].astype(jnp.float32)).astype(jnp.bfloat16)
+        gate = matmul(keys, weights[0, 0])
+        up = matmul(keys, weights[0, 1])
+        back = matmul_nt(target, weights[0, 2])
+        sigma = logistic(gate)
+        gated = gate * sigma
+        hidden = (gated * up).astype(jnp.bfloat16)
+        gate_delta = (back * up * sigma * (1.0 + gate * (1.0 - sigma))).astype(jnp.bfloat16)
+        up_delta = (back * gated).astype(jnp.bfloat16)
+        grads[0] += matmul_tn(keys, gate_delta)
+        grads[1] += matmul_tn(keys, up_delta)
+        grads[2] += matmul_tn(hidden, target)
+
+    @pl.when(active & (step == count - 1))
+    def _():
+        for at in range(3):
+            start = initial[0, at].astype(jnp.float32)
+            updated = weights[0, at].astype(jnp.float32) + grads[at]
+            wanted = jnp.mean(start * start, axis=-1, keepdims=True) + epsilon
+            held = jnp.mean(updated * updated, axis=-1, keepdims=True) + epsilon
+            new[0, at] = (updated * (jnp.sqrt(wanted) / jnp.sqrt(held))).astype(jnp.bfloat16)
+
+    @pl.when(jnp.logical_not(active) & (step == 0))
+    def _():
+        new[...] = weights[...]
+
+    @pl.when(active & (step >= count))
+    def _():
+        queries = unit_rows(q[0])
+        gate = matmul(queries, new[0, 0])
+        hidden = (gate * logistic(gate) * matmul(queries, new[0, 1])).astype(jnp.bfloat16)
+        fast = matmul(hidden, new[0, 2]).astype(jnp.bfloat16).astype(jnp.float32)
+        out[0] = (attended[0] + fast).astype(jnp.bfloat16)
+
+
+def fast_stretch(table, k, v, rate, weights, initial, q, attended):
+    count, rows, width = k.shape
+    own = q.shape[0]
+    held = weights.shape[0] - 1
+    block = functools.partial(pl.BlockSpec, (1, rows, width))
+    token = block(lambda i, t: (jnp.minimum(i, count - 1), 0, 0))
+    query = block(lambda i, t: (jnp.maximum(i - count, 0), 0, 0))
+    matrices = functools.partial(pl.BlockSpec, (1,) + weights.shape[1:])
+    return pl.pallas_call(
+        functools.partial(fast_kernel, count),
+        grid_spec=pltpu.PrefetchScalarGridSpec(
+            num_scalar_prefetch=1,
+            grid=(count + own,),
+            in_specs=[
+                token,
+                token,
+                pl.BlockSpec((1,) + rate.shape[1:], lambda i, t: (t[2 + jnp.minimum(i, count - 1)], 0, 0)),
+                matrices(lambda i, t: (jnp.minimum(t[0], held), 0, 0, 0)),
+                matrices(lambda i, t: (t[0], 0, 0, 0)),
+                query,
+                query,
+            ],
+            out_specs=[query, matrices(lambda i, t: (0, 0, 0, 0))],
+            scratch_shapes=[pltpu.VMEM(weights.shape[1:], jnp.float32)],
+        ),
+        out_shape=[
+            jax.ShapeDtypeStruct((own, rows, width), jnp.bfloat16),
+            jax.ShapeDtypeStruct((1,) + weights.shape[1:], jnp.bfloat16),
+        ],
+        compiler_params=pltpu.CompilerParams(vmem_limit_bytes=VMEM_LIMIT),
+        name="fast_stretch",
+    )(table, k, v, rate, weights, initial, q, attended)
+
+
+def head_body(tokens, qkv_maps, rate_map, fast_init):
+    rows = tokens.shape[0]
+    heads, width = qkv_maps.shape[:2]
+    groups = lax.axis_size("tok")
+    chips = groups // 2
+    slots = chips // 2
+    me = lax.axis_index("tok")
+    chip, core = me // 2, me % 2
+
+    def swap(block, bits):
+        return lax.ppermute(block, "tok", [(i, i ^ bits) for i in range(groups)])
+
+    def piece(slot):
+        return lax.dynamic_slice_in_dim(tokens, (chip ^ slot) * width, width, 1)
+
+    pieces = [piece(slot) for slot in range(chips)]
+    same = [pieces[0]] + [swap(pieces[slot], 2 * slot) for slot in range(1, chips)]
+    other = [swap(block, 1) for block in same]
+
+    terms = lax.dot_general(
+        rate_map, tokens, (((0,), (1,)), ((), ())), preferred_element_type=jnp.float32
+    )
+    terms = lax.all_to_all(terms.reshape(-1, heads, rows), "head", 0, 0)
+    rate = (rate_base * jax.nn.softplus(jnp.sum(terms, 0))).astype(jnp.bfloat16)
+    rate = lax.all_to_all(jnp.repeat(rate, 2, axis=0), "tok", 0, 0, tiled=True)
+    rate = jnp.broadcast_to(rate[:, :, None], (groups, rows, 128))
+
+    def mixed(first):
+        return [part for slot in range(first, first + slots) for part in (same[slot], other[slot])]
+
+    head = jnp.asarray(chip, jnp.int32)
+    q_near, k_near, v_near = project(head[None], mixed(0), qkv_maps)
+    q_far, k_far, v_far = project(head[None], mixed(slots), qkv_maps)
+
+    def attend_table(first):
+        at = chip ^ jnp.arange(first, first + slots, dtype=jnp.int32)
+        before = jnp.where(core == 1, at, at - 1)
+        there = (before >= 0).astype(jnp.int32)
+        return jnp.concatenate([head[None], chip ^ jnp.maximum(before, 0), there])
+
+    attended_near = attend(
+        attend_table(0), q_near, k_near, v_near, k_near, v_near, k_far, v_far
+    )
+    attended_far = attend(
+        attend_table(slots), q_far, k_far, v_far, k_near, v_near, k_far, v_far
+    )
+
+    def fast_table(first, active):
+        at = chip ^ jnp.arange(first, first + slots, dtype=jnp.int32)
+        blocks = (2 * at[:, None] + (core ^ jnp.arange(2, dtype=jnp.int32))[None]).reshape(-1)
+        return jnp.concatenate([head[None], jnp.asarray(active, jnp.int32)[None], blocks])
+
+    is_first = chip < slots
+    initial = lax.dynamic_slice_in_dim(fast_init, chip, 1, 0)
+    out_early, weights = fast_stretch(
+        fast_table(0, is_first), k_near, v_near, rate, initial, fast_init, q_near, attended_near
+    )
+    out_far, weights = fast_stretch(
+        fast_table(slots, True), k_far, v_far, rate, weights, fast_init, q_far, attended_far
+    )
+    out_late, weights = fast_stretch(
+        fast_table(0, ~is_first), k_near, v_near, rate, weights, fast_init, q_near, attended_near
+    )
+    out_near = jnp.where(is_first, out_early, out_late)
+    results = [out_near[slot] for slot in range(slots)] + [out_far[slot] for slot in range(slots)]
+    results = [results[0]] + [swap(results[slot], 2 * slot) for slot in range(1, chips)]
+    combined = jnp.zeros_like(tokens)
+    for slot in range(chips):
+        combined = lax.dynamic_update_slice_in_dim(combined, results[slot], (chip ^ slot) * width, 1)
+    return combined
+
+
+def body(tokens, qkv_maps, rate_map, fast_init):
+    groups = lax.axis_size("tok")
+    heads = qkv_maps.shape[0]
+    powers = groups & (groups - 1) == 0
+    if powers and groups == 2 * heads and tokens.shape[0] == WINDOW:
+        return head_body(tokens, qkv_maps, rate_map, fast_init)
+    return general_body(tokens, qkv_maps, rate_map, fast_init)
+
+
 def solution(mesh):
     in_specs = (
         P("tok", "head"),

time: 466 us -> 183 us (0.39); the launches traced: 457 us -> 182 us
  waiting for transfers between devices: 268 us -> 83.9 us
  matrix products: 93.5 us -> 0.64 us
  Pallas kernels: 0 us -> 62.8 us
  other arithmetic: 47.3 us -> 1.24 us
  blocking collectives: 16.3 us -> 0 us
  starting transfers between devices: 2.36 us -> 17.3 us
  between operations: 14.6 us -> 0.22 us
    psum x2 -> x0, waiting for transfers between devices: 268 us -> none  [update_weights(): lax.psum(partial_value.astype(jnp.bfloat16), 'tok').astype(jnp.float32)]
    dot_general x20 -> x1, matrix products: 93.5 us -> 0.64 us  [head_body(): lax.dot_general(rate_map, tokens, (((0,), (1,)), ((), ())), preferred_ele...]
    ppermute x1 -> x10, waiting for transfers between devices: 0.01 us -> 79.8 us  [swap(): return lax.ppermute(block, 'tok', [(i, i ^ bits) for i in range(groups)])]
    pallas_call x0 -> x7, Pallas kernels: none -> 62.8 us  [the longest x3 39.5 us: fast_stretch(): pl.pallas_call(functools.partial(fast_kernel, count), grid_spec=pltpu.Pre...]
    convert_element_type x5 -> x2, other arithmetic: 20 us -> 0.03 us  [the longest x1 0.02 us: head_body(): rate = (rate_base * jax.nn.softplus(jnp.sum(terms, 0))).astype(jnp.bfloat16)]
    reduce_sum x3 -> x1, other arithmetic: 18.3 us -> 0.02 us  [head_body(): rate = (rate_base * jax.nn.softplus(jnp.sum(terms, 0))).astype(jnp.bfloat16)]
    unnamed x1 -> x0, blocking collectives: 16.3 us -> none
    all_to_all x0 -> x2, starting transfers between devices: none -> 8.83 us  [the longest x1 5.11 us: head_body(): rate = lax.all_to_all(jnp.repeat(rate, 2, axis=0), 'tok', 0, 0, tiled=True)]
  transfers between devices with their start and end apart: 3 -> 12, of which waited for: 2 -> 6; matrix products, arithmetic and copies ran while one was open for 15% -> 4% of each run, Pallas kernels for 0% -> 3%
where the time goes in v1:
time: 183 us; the launch traced here: 182 us
  waiting for transfers between devices  83.9 us (46%)
  Pallas kernels  62.8 us (34%)
  starting transfers between devices  17.3 us (9%)
  local copies, waits for them, and re-layouts  15.8 us (9%)
    ppermute x10, waiting for transfers between devices, swap(): return lax.ppermute(block, 'tok', [(i, i ^ bits) for i in range(groups)])  79.8 us
    pallas_call x3, Pallas kernels, fast_stretch(): pl.pallas_call(functools.partial(fast_kernel, count), grid_spec=pltpu.Pre...  39.5 us
    pallas_call x2, Pallas kernels, project(): pl.pallas_call(functools.partial(project_kernel, width), grid_spec=pltpu....  12.6 us
    pallas_call x2, Pallas kernels, attend(): pl.pallas_call(functools.partial(attend_kernel, slots), grid_spec=pltpu.P...  10.7 us
    ppermute x10, starting transfers between devices, swap(): return lax.ppermute(block, 'tok', [(i, i ^ bits) for i in range(groups)])  8.52 us
    unnamed x23, local copies, waits for them, and re-layouts  6.98 us
    all_to_all x1, starting transfers between devices, head_body(): rate = lax.all_to_all(jnp.repeat(rate, 2, axis=0), 'tok', 0, 0, tiled=True)  5.11 us
    all_to_all x1, waiting for transfers between devices, head_body(): rate = lax.all_to_all(jnp.repeat(rate, 2, axis=0), 'tok', 0, 0, tiled=True)  4.09 us
  transfers between devices with their start and end apart: 12, of which 6 were waited for; matrix products, arithmetic and copies ran while one was open for 4% of the time, Pallas kernels for 3%

profile of v1, /device:TPU:8, one launch (start us, length us, event | category | flops | bytes accessed | tf_op | source)
XLA Modules:
  0.0 182.0 jit_solution(17403716762739923588)
XLA Ops:
  0.0 2.9 %constant_dynamic-slice_fusion = (bf16[512,512]{1,0:T(8,128)(2,1)}, bf16[512,512]{1,0:T(8,128)(2,1)}, bf16[512,512]{1,0:T(8,128)(2,1)S(1)}, bf16[512,512]{1,0:T(8,128)(2,1)S(1)}) fusion(bf16[512,2048]{1,0:T(8,128)(2,1)} %param.4, s32[]{:T(128)S(6)} %select_n.64, s32[]{:T(128)S(6)} %select_n.58, s32[]{:T(128)S(6)} %select_n.57, s32[]{:T(128)S(6)} %select_n.63), kind=kLoop, calls=%fused_computation.13 | loop fusion | bytes 4194320 | tf_op jit(solution)/shard_map/dynamic_slice | solution.py:350
  2.9 2.6 %collective-permute-start.3 = (bf16[512,512]{1,0:T(8,128)(2,1)S(1)}, bf16[512,512]{1,0:T(8,128)(2,1)S(1)}, u32[]{:S(2)}, u32[]{:S(2)}) collective-permute-start(bf16[512,512]{1,0:T(8,128)(2,1)S(1)} %get-tuple-element.30), channel_id=1, source_target_pairs={{0,4},{1,5},{2,6},{3,7},{4,0},{5,1},{6,2},{7,3},{8,12},{9,13},{10,... | collective-permute-start | bytes 1572872 | tf_op jit(solution)/shard_map/ppermute | solution.py:347
  5.5 1.8 collective-permute-start.1
  8.6 3.7 %all-to-all-start = ((f32[4,4,512]{2,1,0:T(4,128)}), f32[4,4,512]{2,1,0:T(4,128)S(1)}, u32[]{:S(2)}, u32[]{:S(2)}) async-start(f32[4,4,512]{2,1,0:T(4,128)} %reshape.35), calls=%async_computation | async-start | bytes 65536 | tf_op jit(solution)/shard_map/all_to_all | solution.py:359
  12.5 2.6 %constant_dynamic-slice_fusion.2.weights = bf16[1,3,512,512]{3,2,1,0:T(8,128)(2,1)} fusion(bf16[4,3,512,512]{3,2,1,0:T(8,128)(2,1)} %initial.5, s32[]{:T(128)S(6)} %select_n.60), kind=kLoop, calls=%fused_computation.15 | loop fusion | bytes 3145732 | tf_op jit(solution)/shard_map/dynamic_slice | solution.py:390
  15.2 24.0 %collective-permute-done.3.x0 = bf16[512,512]{1,0:T(8,128)(2,1)S(1)} collective-permute-done((bf16[512,512]{1,0:T(8,128)(2,1)S(1)}, bf16[512,512]{1,0:T(8,128)(2,1)S(1)}, u32[]{:S(2)}, u32[]{:S(2)}) %collective-permute-start.3) | collective-permute-done | bytes 524320 | tf_op jit(solution)/shard_map/ppermute | solution.py:347
  39.1 11.2 %collective-permute-done.5.x2 = bf16[512,512]{1,0:T(8,128)(2,1)S(1)} collective-permute-done((bf16[512,512]{1,0:T(8,128)(2,1)}, bf16[512,512]{1,0:T(8,128)(2,1)S(1)}, u32[]{:S(2)}, u32[]{:S(2)}) %collective-permute-start.5) | collective-permute-done | bytes 524320 | tf_op jit(solution)/shard_map/ppermute | solution.py:347
  53.0 5.1 %all-to-all-start.1 = ((bf16[8,2,256]{2,1,0:T(2,128)(2,1)}), bf16[8,2,256]{2,1,0:T(2,128)(2,1)S(1)}, u32[]{:S(2)}, u32[]{:S(2)}) async-start(bf16[8,2,256]{2,1,0:T(2,128)(2,1)} %reshape.38), calls=%async_computation.1 | async-start | bytes 16384 | tf_op jit(solution)/shard_map/all_to_all | solution.py:361
  58.2 4.1 %all-to-all-done.1 = bf16[8,2,256]{2,1,0:T(2,128)(2,1)S(1)} async-done(((bf16[8,2,256]{2,1,0:T(2,128)(2,1)}), bf16[8,2,256]{2,1,0:T(2,128)(2,1)S(1)}, u32[]{:S(2)}, u32[]{:S(2)}) %all-to-all-start.1) | async-done | bytes 8224 | tf_op jit(solution)/shard_map/all_to_all | solution.py:361
  62.4 6.0 %project.3 = (bf16[2,512,512]{2,1,0:T(8,128)(2,1)S(1)}, bf16[4,512,512]{2,1,0:T(8,128)(2,1)S(1)}, bf16[4,512,512]{2,1,0:T(8,128)(2,1)}) custom-call(s32[1]{0:T(128)} %bitcast.table, bf16[512,512]{1,0:T(8,128)(2,1)S(1)} %collective-permute-done.3.x0, bf16[512,512]{1,0:T(8,128)(2,1)S(1)} %collective-permute-done.4.x1, ...), custom_call_target="tpu_custom_call" | custom-call | tf_op jit(solution)/shard_map/project/pallas_call | solution.py:185
  68.4 6.6 %project.2 = (bf16[2,512,512]{2,1,0:T(8,128)(2,1)S(1)}, bf16[4,512,512]{2,1,0:T(8,128)(2,1)S(1)}, bf16[4,512,512]{2,1,0:T(8,128)(2,1)}) custom-call(s32[1]{0:T(128)} %bitcast.table, bf16[512,512]{1,0:T(8,128)(2,1)S(1)} %get-tuple-element.29.x0, bf16[512,512]{1,0:T(8,128)(2,1)S(1)} %collective-permute-done.x1, ...), custom_call_target="tpu_custom_call" | custom-call | tf_op jit(solution)/shard_map/project/pallas_call | solution.py:185
  75.0 1.4 copy-done.1
  76.4 5.4 %attend.3.attended = f32[2,512,512]{2,1,0:T(8,128)S(1)} custom-call(s32[5]{0:T(128)S(1)} %pad_add_fusion.2.table, bf16[2,512,512]{2,1,0:T(8,128)(2,1)S(1)} %get-tuple-element.23.q, bf16[4,512,512]{2,1,0:T(8,128)(2,1)S(1)} %get-tuple-element.19.k_far.k_now.k, bf16[4,512,512]{2,1,0:T(8,128)(2,1)} %get-tuple-element.20.v_far.v_now.v, ...), custom_call_target="tpu_custom_call" | custom-call | tf_op jit(solution)/shard_map/attend/pallas_call | solution.py:241
  81.8 1.4 copy-done.5
  83.1 5.3 %attend.2.attended = f32[2,512,512]{2,1,0:T(8,128)S(1)} custom-call(s32[5]{0:T(128)S(1)} %pad_add_fusion.table, bf16[2,512,512]{2,1,0:T(8,128)(2,1)S(1)} %get-tuple-element.18.q, bf16[4,512,512]{2,1,0:T(8,128)(2,1)S(1)} %copy-done.2, bf16[4,512,512]{2,1,0:T(8,128)(2,1)} %get-tuple-element.17.v_now.v_near.v, bf16[4,512,512]{2,1,0:T(8,128)(2,1)S(1)} %copy-done.2, ...), custom_call_target="tpu_custom_call" | custom-call | tf_op jit(solution)/shard_map/attend/pallas_call | solution.py:241
  88.5 1.4 copy-done.4
  90.5 16.1 %fast_stretch.3 = (bf16[2,512,512]{2,1,0:T(8,128)(2,1)S(1)}, bf16[1,3,512,512]{3,2,1,0:T(8,128)(2,1)S(1)}) custom-call(s32[6]{0:T(128)S(1)} %get-tuple-element.36.table, bf16[4,512,512]{2,1,0:T(8,128)(2,1)} %copy-done.1, bf16[4,512,512]{2,1,0:T(8,128)(2,1)} %get-tuple-element.17.v_now.v_near.v, bf16[8,512,128]{2,1,0:T(8,128)(2,1)S(1)} %broadcast_in_dim.47.rate, ...), custom_call_target="tpu_custom_call" | custom-call | tf_op jit(solution)/shard_map/fast_stretch/pallas_call | solution.py:311
  107.7 15.9 %fast_stretch.4 = (bf16[2,512,512]{2,1,0:T(8,128)(2,1)S(1)}, bf16[1,3,512,512]{3,2,1,0:T(8,128)(2,1)S(1)}) custom-call(s32[6]{0:T(128)S(1)} %pad_add_fusion.1.table, bf16[4,512,512]{2,1,0:T(8,128)(2,1)} %copy-done.3, bf16[4,512,512]{2,1,0:T(8,128)(2,1)} %get-tuple-element.20.v_far.v_now.v, bf16[8,512,128]{2,1,0:T(8,128)(2,1)S(1)} %broadcast_in_dim.47.rate, ...), custom_call_target="tpu_custom_call" | custom-call | tf_op jit(solution)/shard_map/fast_stretch/pallas_call | solution.py:311
  124.7 7.5 %fast_stretch.5 = (bf16[2,512,512]{2,1,0:T(8,128)(2,1)S(1)}, bf16[1,3,512,512]{3,2,1,0:T(8,128)(2,1)}) custom-call(s32[6]{0:T(128)S(1)} %get-tuple-element.35.table, bf16[4,512,512]{2,1,0:T(8,128)(2,1)} %copy-done.1, bf16[4,512,512]{2,1,0:T(8,128)(2,1)} %get-tuple-element.17.v_now.v_near.v, bf16[8,512,128]{2,1,0:T(8,128)(2,1)S(1)} %broadcast_in_dim.47.rate, ...), custom_call_target="tpu_custom_call" | custom-call | tf_op jit(solution)/shard_map/fast_stretch/pallas_call | solution.py:311
  132.4 1.5 collective-permute-start.7
  134.6 1.5 collective-permute-start.9
  136.4 18.5 %collective-permute-done.7 = bf16[512,512]{1,0:T(8,128)(2,1)S(1)} collective-permute-done((bf16[512,512]{1,0:T(8,128)(2,1)S(1)}, bf16[512,512]{1,0:T(8,128)(2,1)S(1)}, u32[]{:S(2)}, u32[]{:S(2)}) %collective-permute-start.7) | collective-permute-done | bytes 524320 | tf_op jit(solution)/shard_map/ppermute | solution.py:347
  155.0 14.5 %collective-permute-done.8 = bf16[512,512]{1,0:T(8,128)(2,1)S(1)} collective-permute-done((bf16[512,512]{1,0:T(8,128)(2,1)S(1)}, bf16[512,512]{1,0:T(8,128)(2,1)S(1)}, u32[]{:S(2)}, u32[]{:S(2)}) %collective-permute-start.8) | collective-permute-done | bytes 524320 | tf_op jit(solution)/shard_map/ppermute | solution.py:347
  169.5 11.7 %collective-permute-done.9 = bf16[512,512]{1,0:T(8,128)(2,1)S(1)} collective-permute-done((bf16[512,512]{1,0:T(8,128)(2,1)S(1)}, bf16[512,512]{1,0:T(8,128)(2,1)S(1)}, u32[]{:S(2)}, u32[]{:S(2)}) %collective-permute-start.9) | collective-permute-done | bytes 524320 | tf_op jit(solution)/shard_map/ppermute | solution.py:347
  (60 shorter events, 9.2 us)
Async XLA Ops:
  0.0 7.3 %copy-start = (bf16[2048,16]{0,1:T(8,128)(2,1)S(1)}, bf16[2048,16]{0,1:T(8,128)(2,1)}, u32[]{:S(2)}) copy-start(bf16[2048,16]{0,1:T(8,128)(2,1)} %param.6) | copy-start | bytes 196612
  0.0 7.3 %copy-start.8 = (bf16[512,2048]{1,0:T(8,128)(2,1)S(1)}, bf16[512,2048]{1,0:T(8,128)(2,1)}, u32[]{:S(2)}) copy-start(bf16[512,2048]{1,0:T(8,128)(2,1)} %param.4) | copy-start | bytes 6291460
  2.9 36.3 %collective-permute-start.3 = (bf16[512,512]{1,0:T(8,128)(2,1)S(1)}, bf16[512,512]{1,0:T(8,128)(2,1)S(1)}, u32[]{:S(2)}, u32[]{:S(2)}) collective-permute-start(bf16[512,512]{1,0:T(8,128)(2,1)S(1)} %get-tuple-element.30), channel_id=1, source_target_pairs={{0,4},{1,5},{2,6},{3,7},{4,0},{5,1},{6,2},{7,3},{8,12},{9,13},{10,... | collective-permute-start | bytes 1572872 | tf_op jit(solution)/shard_map/ppermute | solution.py:347
  5.5 44.9 %collective-permute-start.5 = (bf16[512,512]{1,0:T(8,128)(2,1)}, bf16[512,512]{1,0:T(8,128)(2,1)S(1)}, u32[]{:S(2)}, u32[]{:S(2)}) collective-permute-start(bf16[512,512]{1,0:T(8,128)(2,1)} %get-tuple-element.27), channel_id=1, source_target_pairs={{0,6},{1,7},{2,4},{3,5},{4,2},{5,3},{6,0},{7,1},{8,14},{9,15},{10,... | collective-permute-start | bytes 1572872 | tf_op jit(solution)/shard_map/ppermute | solution.py:347
  5.5 44.9 %collective-permute-start.1 = (bf16[512,512]{1,0:T(8,128)(2,1)}, bf16[512,512]{1,0:T(8,128)(2,1)S(1)}, u32[]{:S(2)}, u32[]{:S(2)}) collective-permute-start(bf16[512,512]{1,0:T(8,128)(2,1)} %get-tuple-element.28), channel_id=1, source_target_pairs={{0,2},{1,3},{2,0},{3,1},{4,6},{5,7},{6,4},{7,5},{8,10},{9,11},{10,... | collective-permute-start | bytes 1572872 | tf_op jit(solution)/shard_map/ppermute | solution.py:347
  7.3 61.1 %collective-permute-start = (bf16[512,512]{1,0:T(8,128)(2,1)S(1)}, bf16[512,512]{1,0:T(8,128)(2,1)S(1)}, u32[]{:S(2)}, u32[]{:S(2)}) collective-permute-start(bf16[512,512]{1,0:T(8,128)(2,1)S(1)} %get-tuple-element.29.x0), channel_id=1, source_target_pairs={{0,1},{1,0},{2,3},{3,2},{4,5},{5,4},{6,7},{7,6},{8,9},{9,8},{10,11... | collective-permute-start | bytes 1572872 | tf_op jit(solution)/shard_map/ppermute | solution.py:347
  8.6 42.6 %all-to-all-start = ((f32[4,4,512]{2,1,0:T(4,128)}), f32[4,4,512]{2,1,0:T(4,128)S(1)}, u32[]{:S(2)}, u32[]{:S(2)}) async-start(f32[4,4,512]{2,1,0:T(4,128)} %reshape.35), calls=%async_computation | async-start | bytes 65536 | tf_op jit(solution)/shard_map/all_to_all | solution.py:359
  39.1 23.2 %collective-permute-start.4 = (bf16[512,512]{1,0:T(8,128)(2,1)S(1)}, bf16[512,512]{1,0:T(8,128)(2,1)S(1)}, u32[]{:S(2)}, u32[]{:S(2)}) collective-permute-start(bf16[512,512]{1,0:T(8,128)(2,1)S(1)} %collective-permute-done.3.x0), channel_id=1, source_target_pairs={{0,1},{1,0},{2,3},{3,2},{4,5},{5,4},{6,7},{7,6},{8,9},{9,8},{10,11... | collective-permute-start | bytes 1572872 | tf_op jit(solution)/shard_map/ppermute | solution.py:347
  50.4 12.0 %collective-permute-start.6 = (bf16[512,512]{1,0:T(8,128)(2,1)S(1)}, bf16[512,512]{1,0:T(8,128)(2,1)}, u32[]{:S(2)}, u32[]{:S(2)}) collective-permute-start(bf16[512,512]{1,0:T(8,128)(2,1)S(1)} %collective-permute-done.5.x2), channel_id=1, source_target_pairs={{0,1},{1,0},{2,3},{3,2},{4,5},{5,4},{6,7},{7,6},{8,9},{9,8},{10,11... | collective-permute-start | bytes 1572872 | tf_op jit(solution)/shard_map/ppermute | solution.py:347
  50.4 17.9 %collective-permute-start.2 = (bf16[512,512]{1,0:T(8,128)(2,1)S(1)}, bf16[512,512]{1,0:T(8,128)(2,1)}, u32[]{:S(2)}, u32[]{:S(2)}) collective-permute-start(bf16[512,512]{1,0:T(8,128)(2,1)S(1)} %collective-permute-done.1.x2), channel_id=1, source_target_pairs={{0,1},{1,0},{2,3},{3,2},{4,5},{5,4},{6,7},{7,6},{8,9},{9,8},{10,11... | collective-permute-start | bytes 1572872 | tf_op jit(solution)/shard_map/ppermute | solution.py:347
  53.0 9.3 %all-to-all-start.1 = ((bf16[8,2,256]{2,1,0:T(2,128)(2,1)}), bf16[8,2,256]{2,1,0:T(2,128)(2,1)S(1)}, u32[]{:S(2)}, u32[]{:S(2)}) async-start(bf16[8,2,256]{2,1,0:T(2,128)(2,1)} %reshape.38), calls=%async_computation.1 | async-start | bytes 16384 | tf_op jit(solution)/shard_map/all_to_all | solution.py:361
  68.3 8.0 %copy-start.3 = (bf16[4,512,512]{2,1,0:T(8,128)(2,1)}, bf16[4,512,512]{2,1,0:T(8,128)(2,1)S(1)}, u32[]{:S(2)}) copy-start(bf16[4,512,512]{2,1,0:T(8,128)(2,1)S(1)} %get-tuple-element.19.k_far.k_now.k) | copy-start | bytes 6291460
  75.0 1.4 copy-start.1
  76.4 6.8 %copy-start.2 = (bf16[4,512,512]{2,1,0:T(8,128)(2,1)S(1)}, bf16[4,512,512]{2,1,0:T(8,128)(2,1)}, u32[]{:S(2)}) copy-start(bf16[4,512,512]{2,1,0:T(8,128)(2,1)} %copy-done.1) | copy-start | bytes 6291460
  81.8 1.4 copy-start.5
  88.5 1.4 copy-start.4
  106.6 1.1 copy-start.7
  123.6 1.1 copy-start.6
  132.4 22.5 %collective-permute-start.7 = (bf16[512,512]{1,0:T(8,128)(2,1)S(1)}, bf16[512,512]{1,0:T(8,128)(2,1)S(1)}, u32[]{:S(2)}, u32[]{:S(2)}) collective-permute-start(bf16[512,512]{1,0:T(8,128)(2,1)S(1)} %slice_bitcast_fusion), channel_id=1, source_target_pairs={{0,2},{1,3},{2,0},{3,1},{4,6},{5,7},{6,4},{7,5},{8,10},{9,11},{10,... | collective-permute-start | bytes 1572872 | tf_op jit(solution)/shard_map/ppermute | solution.py:347
  134.0 35.5 %collective-permute-start.8 = (bf16[512,512]{1,0:T(8,128)(2,1)S(1)}, bf16[512,512]{1,0:T(8,128)(2,1)S(1)}, u32[]{:S(2)}, u32[]{:S(2)}) collective-permute-start(bf16[512,512]{1,0:T(8,128)(2,1)S(1)} %get-tuple-element.32), channel_id=1, source_target_pairs={{0,4},{1,5},{2,6},{3,7},{4,0},{5,1},{6,2},{7,3},{8,12},{9,13},{10,... | collective-permute-start | bytes 1572872 | tf_op jit(solution)/shard_map/ppermute | solution.py:347
  134.6 46.6 %collective-permute-start.9 = (bf16[512,512]{1,0:T(8,128)(2,1)S(1)}, bf16[512,512]{1,0:T(8,128)(2,1)S(1)}, u32[]{:S(2)}, u32[]{:S(2)}) collective-permute-start(bf16[512,512]{1,0:T(8,128)(2,1)S(1)} %get-tuple-element.31), channel_id=1, source_target_pairs={{0,6},{1,7},{2,4},{3,5},{4,2},{5,3},{6,0},{7,1},{8,14},{9,15},{10,... | collective-permute-start | bytes 1572872 | tf_op jit(solution)/shard_map/ppermute | solution.py:347
  169.5 11.7 %copy-start.9 = (bf16[512,2048]{1,0:T(8,128)(2,1)}, bf16[512,2048]{1,0:T(8,128)(2,1)S(1)}, u32[]{:S(2)}) copy-start(bf16[512,2048]{1,0:T(8,128)(2,1)S(1)} %constant_dynamic-update-slice_fusion.1) | copy-start | bytes 6291460

commit v2 on v0

--- a/solution.py
+++ b/solution.py
@@ -1,6 +1,10 @@
+import functools
+
 import jax
 import jax.numpy as jnp
 from jax import lax
+from jax.experimental import pallas as pl
+from jax.experimental.pallas import tpu as pltpu
 from jax.sharding import PartitionSpec as P
 
 WINDOW = 512
@@ -8,6 +12,8 @@
 
 rate_base = 0.003
 epsilon = 1e-06
+VMEM_LIMIT = 33 * 1024 * 1024
+BEGIN_LIMIT = 33 * 1024 * 1024
 
 
 def from_behind(block, axis, distance):
@@ -87,7 +93,7 @@
     return renorm(weights.astype(jnp.float32) + total, initial)
 
 
-def body(tokens, qkv_maps, rate_map, fast_init):
+def general_body(tokens, qkv_maps, rate_map, fast_init):
     tok_rows = tokens.shape[0]
     head_count = qkv_maps.shape[0]
     head_width = qkv_maps.shape[1]
@@ -136,6 +142,324 @@
     return combined.reshape(tok_rows, head_count * head_width)
 
 
+def matmul(left, right):
+    return jnp.dot(left, right, preferred_element_type=jnp.float32)
+
+
+def matmul_nt(left, right):
+    return lax.dot_general(left, right, (((1,), (1,)), ((), ())), preferred_element_type=jnp.float32)
+
+
+def matmul_tn(left, right):
+    return lax.dot_general(left, right, (((0,), (0,)), ((), ())), preferred_element_type=jnp.float32)
+
+
+def unit_rows(rows):
+    rows = rows.astype(jnp.float32)
+    scale = lax.rsqrt(jnp.mean(rows * rows, axis=-1, keepdims=True) + epsilon)
+    return (rows * scale).astype(jnp.bfloat16)
+
+
+def logistic(a):
+    return 0.5 * jnp.tanh(0.5 * a) + 0.5
+
+
+def fetch(source, target, sem, when=None):
+    copy = pltpu.make_async_copy(source, target, sem)
+    if when is None:
+        copy.start()
+    else:
+        pl.when(when)(copy.start)
+
+
+def fetched(target, sem):
+    pltpu.make_async_copy(target, target, sem).wait()
+
+
+def learn(at, x, m, rate_row, pool, put_query, put_key_value):
+    rows, width = x.shape[1:]
+    here = pl.ds(pl.multiple_of(rows * at, rows), rows)
+    key_rows = matmul(x[at], m[:, width : 2 * width]).astype(jnp.bfloat16)
+    value_rows = matmul(x[at], m[:, 2 * width :]).astype(jnp.bfloat16)
+    put_key_value(key_rows, value_rows)
+    pool[0, here] = unit_rows(key_rows)
+    spread = jnp.broadcast_to(rate_row, (128, rows)).T
+    spread = jnp.concatenate([spread] * (width // 128), 1)
+    pool[2, here] = (spread * value_rows.astype(jnp.float32)).astype(jnp.bfloat16)
+
+    @pl.when(at % 2 == 0)
+    def _():
+        put_query(matmul(x[at], m[:, :width]).astype(jnp.bfloat16))
+
+
+def deltas(at, rows, w, pool):
+    here = pl.ds(pl.multiple_of(rows * at, rows), rows)
+    gate = matmul(pool[0, here], w[0])
+    up = matmul(pool[0, here], w[1])
+    back = matmul_nt(pool[2, here], w[2])
+    sigma = logistic(gate)
+    gated = gate * sigma
+    pool[1, here] = (gated * up).astype(jnp.bfloat16)
+    pool[3, here] = (back * up * sigma * (1.0 + gate * (1.0 - sigma))).astype(jnp.bfloat16)
+    pool[4, here] = (back * gated).astype(jnp.bfloat16)
+
+
+def gradient(at, pool):
+    return matmul_tn(pool[at // 2], pool[jnp.where(at == 2, 2, 3 + at)])
+
+
+def stage_kernel(counts, table, *refs):
+    count, befores, earliers, begun = counts
+    slots = count // 2 + begun
+    blocks, refs = refs[:count], refs[count:]
+    before, refs = refs[:befores], refs[befores:]
+    earlier, refs = refs[:earliers], refs[earliers:]
+    held, refs = refs[: 2 * begun], refs[2 * begun :]
+    (maps, rate, initial), refs = refs[:3], refs[3:]
+    results, new, refs = refs[:slots], refs[slots], refs[slots + 1 :]
+    x, m, w, start, fresh, k, v, q, attended, pool, out, sems, *grads = refs
+    rows, width = x.shape[1:]
+    part = rows // 2
+    updates, answers, first, there = table[0] > 0, table[1] > 0, table[2], table[3] > 0
+    at_maps, at_start, at_weights, at_new, at_held, at_grads = (sems.at[count + 1 + at] for at in range(6))
+    send_new = pltpu.make_async_copy(fresh, new, at_new)
+    send = [pltpu.make_async_copy(out.at[at], results[at], sems.at[count + 7 + at]) for at in range(slots)]
+
+    def span(at, size=rows):
+        return pl.ds(pl.multiple_of(at, part), size)
+
+    def answer():
+        row = lax.broadcasted_iota(jnp.int32, (part, rows + part), 0)
+        column = lax.broadcasted_iota(jnp.int32, (part, rows + part), 1)
+        band = (column > row) & (column <= row + rows)
+
+        @pl.loop(0, slots)
+        def _(at):
+            @pl.loop(0, 2)
+            def _(half):
+                own = span(part * half, part)
+                base = rows * table[6 + 2 * at] + part * half
+                scores = matmul_nt(q[at, own], k[span(base, rows + part)]) * (width ** -0.5)
+                floor = jnp.where(first > 0, 0, rows - base)
+                scores = jnp.where(band & (column >= floor), scores, -1e30)
+                raised = jnp.exp(scores - jnp.max(scores, axis=1, keepdims=True))
+                total = jnp.sum(raised, axis=1, keepdims=True)
+                values = v[span(base, rows + part)]
+                attended[own] = matmul(raised.astype(jnp.bfloat16), values) / total
+
+            queries = unit_rows(q[at])
+            gate = matmul(queries, fresh[0])
+            up = matmul(queries, fresh[1])
+            inner = (gate * logistic(gate) * up).astype(jnp.bfloat16)
+            fast = matmul(inner, fresh[2]).astype(jnp.bfloat16).astype(jnp.float32)
+            out[at] = (attended[...] + fast).astype(jnp.bfloat16)
+
+        for copy in send:
+            copy.start()
+        for copy in send:
+            copy.wait()
+
+    @pl.when(updates | answers)
+    def _():
+        fetch(maps, m, at_maps)
+        for at in range(count):
+            fetch(blocks[at], x.at[at], sems.at[at])
+        for at in range(befores):
+            fetch(before[at], x.at[count], sems.at[count], there & (table[4] == at))
+        for at in range(earliers):
+            fetch(earlier[at], w, at_weights, table[5] == at)
+        fetch(initial, w, at_weights, table[5] >= earliers)
+        fetch(initial, start, at_start)
+        if begun:
+            for at in range(2):
+                to = span(rows * (table[6 + count + at] + 1))
+                fetch(held[0].at[1 + at], k.at[to], at_held)
+                fetch(held[0].at[3 + at], v.at[to], at_held)
+            fetch(held[0].at[0], q.at[slots - 1], at_held)
+            fetch(held[1], grads[0], at_grads)
+        fetched(m, at_maps)
+
+        @pl.loop(0, count)
+        def _(at):
+            to = span(rows * (table[6 + at] + 1))
+
+            def put_query(query_rows):
+                q[at // 2] = query_rows
+
+            def put_key_value(key_rows, value_rows):
+                k[to] = key_rows
+                v[to] = value_rows
+
+            fetched(x.at[at], sems.at[at])
+            learn(at, x, m, rate[pl.ds(first + table[6 + at], 1)], pool, put_query, put_key_value)
+
+        @pl.when(there)
+        def _():
+            fetched(x.at[count], sems.at[count])
+            k[:rows] = matmul(x[count], m[:, width : 2 * width]).astype(jnp.bfloat16)
+            v[:rows] = matmul(x[count], m[:, 2 * width :]).astype(jnp.bfloat16)
+
+        @pl.when(jnp.logical_not(there))
+        def _():
+            k[:rows] = jnp.zeros((rows, width), jnp.bfloat16)
+            v[:rows] = jnp.zeros((rows, width), jnp.bfloat16)
+
+        fetched(w, at_weights)
+        fetched(start, at_start)
+        if begun:
+            fetched(k.at[pl.ds(0, 4 * rows)], at_held)
+            fetched(q.at[0], at_held)
+            fetched(grads[0], at_grads)
+
+        @pl.when(updates)
+        def _():
+            pl.loop(0, count)(lambda at: deltas(at, rows, w, pool))
+
+            @pl.loop(0, 3)
+            def _(at):
+                updated = w[at].astype(jnp.float32) + gradient(at, pool)
+                if begun:
+                    updated = updated + grads[0][at]
+                origin = start[at].astype(jnp.float32)
+                wanted = jnp.mean(origin * origin, axis=-1, keepdims=True) + epsilon
+                held_now = jnp.mean(updated * updated, axis=-1, keepdims=True) + epsilon
+                fresh[at] = (updated * (jnp.sqrt(wanted) * lax.rsqrt(held_now))).astype(jnp.bfloat16)
+
+            send_new.start()
+
+        @pl.when(jnp.logical_not(updates))
+        def _():
+            fresh[...] = w[...]
+
+        pl.when(answers)(answer)
+        pl.when(updates)(send_new.wait)
+
+
+def stage(table, blocks, before, earlier, maps, rate, initial, held=(), scale=24):
+    count, begun = len(blocks), len(held) // 2
+    rows, width = blocks[0].shape
+    matrices = initial.shape
+    bfloat = functools.partial(pltpu.VMEM, dtype=jnp.bfloat16)
+    anywhere = pl.BlockSpec(memory_space=pl.ANY)
+    slots = count // 2 + begun
+    stretch = 2 * slots * rows
+    operands = [*blocks, *before, *earlier, *held, maps]
+    return pl.pallas_call(
+        functools.partial(stage_kernel, (count, len(before), len(earlier), begun)),
+        grid_spec=pltpu.PrefetchScalarGridSpec(
+            num_scalar_prefetch=1,
+            grid=(),
+            in_specs=[anywhere] * len(operands) + [pl.BlockSpec(memory_space=pltpu.VMEM), anywhere],
+            out_specs=[anywhere] * (slots + 1),
+            scratch_shapes=[
+                bfloat((count + 1, rows, width)),
+                bfloat(maps.shape),
+                bfloat(matrices),
+                bfloat(matrices),
+                bfloat(matrices),
+                bfloat((stretch + rows, width)),
+                bfloat((stretch + rows, width)),
+                bfloat((slots, rows, width)),
+                pltpu.VMEM((rows, width), jnp.float32),
+                bfloat((5, count * rows, width)),
+                bfloat((slots, rows, width)),
+                pltpu.SemaphoreType.DMA((count + 7 + slots,)),
+            ]
+            + [pltpu.VMEM(matrices, jnp.float32)] * begun,
+        ),
+        out_shape=[jax.ShapeDtypeStruct((rows, width), jnp.bfloat16)] * slots
+        + [jax.ShapeDtypeStruct(matrices, jnp.bfloat16)],
+        compiler_params=pltpu.CompilerParams(vmem_limit_bytes=VMEM_LIMIT),
+        cost_estimate=pl.CostEstimate(flops=scale * stretch * width * width, bytes_accessed=scale * stretch * width, transcendentals=0),
+        name="stage",
+    )(table, *operands, rate, initial)
+
+
+def after(array, *others):
+    return lax.optimization_barrier((array, *others))[0]
+
+
+def head_body(tokens, qkv_maps, rate_map, fast_init):
+    rows = tokens.shape[0]
+    heads, width = qkv_maps.shape[:2]
+    groups = lax.axis_size("tok")
+    chips = groups // 2
+    slots = chips // 2
+    last = chips - 1
+    me = lax.axis_index("tok")
+    chip, core = me // 2, me % 2
+    is_first = (chip < slots).astype(jnp.int32)
+
+    def swap(block, bits):
+        return lax.ppermute(block, "tok", [(i, i ^ bits) for i in range(groups)])
+
+    def piece(slot, source, index):
+        return lax.dynamic_slice_in_dim(source, (index ^ slot) * width, width, 1)
+
+    maps = lax.dynamic_index_in_dim(qkv_maps, chip, 0, False)
+    initial = lax.dynamic_index_in_dim(fast_init, chip, 0, False)
+    same = {slot: swap(piece(slot, tokens, chip), 2 * slot) for slot in range(1, slots)}
+    same[last] = swap(piece(last, tokens, chip), 2 * last)
+    terms = lax.dot_general(
+        rate_map, tokens, (((0,), (1,)), ((), ())), preferred_element_type=jnp.float32
+    )
+    terms = lax.all_to_all(jnp.repeat(terms, 2, axis=0), ("head", "tok"), 0, 0, tiled=True)
+    logits = jnp.sum(terms.reshape(-1, groups, rows), 0)
+    rate = (rate_base * jax.nn.softplus(logits)).astype(jnp.bfloat16).astype(jnp.float32)
+    source = tokens
+    for slot in range(1, slots):
+        source = after(source, same[slot])
+    for slot in range(slots, last):
+        same[slot] = swap(piece(slot, source, chip), 2 * slot)
+    same[0] = piece(0, source, chip)
+    other = {slot: swap(same[slot], 1) for slot in range(slots)}
+
+    def integers(entries):
+        return jnp.stack([jnp.asarray(entry, jnp.int32) for entry in entries])
+
+    def places(slot):
+        return [2 * ((chip ^ slot) % slots) + core, 2 * ((chip ^ slot) % slots) + (1 - core)]
+
+    def opening(slot):
+        return 2 * slots * ((chip ^ slot) // slots)
+
+    def table(slots_in, updates, answers, earlier):
+        first = opening(slots_in[0])
+        before = (chip ^ (slots - 1)) % slots
+        flags = [updates, answers, first, (first > 0) & (core == 0), before, earlier]
+        return integers(flags + [place for slot in slots_in for place in places(slot)])
+
+    near_slots, far_slots = range(slots), range(slots, chips)
+    near_blocks = [block for slot in near_slots for block in (same[slot], other[slot])]
+    near_others = [other[slot] for slot in near_slots]
+    shared = dict(maps=maps, rate=rate, initial=initial)
+    *_, first_new = stage(table(near_slots, is_first, False, 0), near_blocks, near_others[:1], [], scale=0, **shared)
+    for slot in far_slots:
+        other[slot] = swap(after(same[slot], first_new), 1)
+    far_blocks = [block for slot in far_slots for block in (same[slot], other[slot])]
+    *far_results, far_new = stage(
+        table(far_slots, True, True, 1 - is_first), far_blocks, near_others, [first_new], **shared
+    )
+    *near_results, _ = stage(
+        table(near_slots, 1 - is_first, True, 1 - is_first), near_blocks, [other[slot] for slot in far_slots], [first_new, far_new], **shared
+    )
+    results = near_results + far_results
+    combined = jnp.zeros_like(tokens)
+    for slot in (0, *far_slots, *range(1, slots)):
+        result = swap(results[slot], 2 * slot) if slot else results[slot]
+        combined = lax.dynamic_update_slice_in_dim(combined, result, (chip ^ slot) * width, 1)
+    return combined
+
+
+def body(tokens, qkv_maps, rate_map, fast_init):
+    groups = lax.axis_size("tok")
+    heads = qkv_maps.shape[0]
+    powers = groups & (groups - 1) == 0 and groups > 2
+    if powers and groups == 2 * heads and tokens.shape[0] == WINDOW:
+        return head_body(tokens, qkv_maps, rate_map, fast_init)
+    return general_body(tokens, qkv_maps, rate_map, fast_init)
+
+
 def solution(mesh):
     in_specs = (
         P("tok", "head"),

time: 466 us -> 135 us (0.29); the launches traced: 457 us -> 134 us
  waiting for transfers between devices: 268 us -> 56.6 us
  matrix products: 93.5 us -> 0.64 us
  other arithmetic: 47.3 us -> 0.03 us
  Pallas kernels: 0 us -> 46.8 us
  blocking collectives: 16.3 us -> 0 us
  between operations: 14.6 us -> 0.24 us
  starting transfers between devices: 2.36 us -> 16.7 us
    psum x2 -> x0, waiting for transfers between devices: 268 us -> none  [update_weights(): lax.psum(partial_value.astype(jnp.bfloat16), 'tok').astype(jnp.float32)]
    dot_general x20 -> x1, matrix products: 93.5 us -> 0.64 us  [head_body(): lax.dot_general(rate_map, tokens, (((0,), (1,)), ((), ())), preferred_ele...]
    ppermute x1 -> x10, waiting for transfers between devices: 0.01 us -> 56.6 us  [swap(): return lax.ppermute(block, 'tok', [(i, i ^ bits) for i in range(groups)])]
    pallas_call x0 -> x3, Pallas kernels: none -> 46.8 us  [stage(): pl.pallas_call(functools.partial(stage_kernel, (count, len(before), len(e...]
    convert_element_type x5 -> x1, other arithmetic: 20 us -> 0.02 us  [head_body(): (rate_base * jax.nn.softplus(logits)).astype(jnp.bfloat16)]
    reduce_sum x3 -> x1, other arithmetic: 18.3 us -> 0.01 us  [head_body(): logits = jnp.sum(terms.reshape(-1, groups, rows), 0)]
    unnamed x1 -> x0, blocking collectives: 16.3 us -> none
    ppermute x1 -> x10, starting transfers between devices: 2.31 us -> 10.1 us  [swap(): return lax.ppermute(block, 'tok', [(i, i ^ bits) for i in range(groups)])]
  transfers between devices with their start and end apart: 3 -> 11, of which waited for: 2 -> 6; matrix products, arithmetic and copies ran while one was open for 15% -> 4% of each run, Pallas kernels for 0% -> 19%
where the time goes in v2:
time: 135 us; the launch traced here: 134 us
  waiting for transfers between devices  56.6 us (42%)
  Pallas kernels  46.8 us (35%)
  starting transfers between devices  16.7 us (12%)
  local copies, waits for them, and re-layouts  12.5 us (9%)
    ppermute x10, waiting for transfers between devices, swap(): return lax.ppermute(block, 'tok', [(i, i ^ bits) for i in range(groups)])  56.6 us
    pallas_call x3, Pallas kernels, stage(): pl.pallas_call(functools.partial(stage_kernel, (count, len(before), len(e...  46.8 us
    ppermute x10, starting transfers between devices, swap(): return lax.ppermute(block, 'tok', [(i, i ^ bits) for i in range(groups)])  10.1 us
    all_to_all x1, starting transfers between devices, head_body(): lax.all_to_all(jnp.repeat(terms, 2, axis=0), ('head', 'tok'), 0, 0, tiled...  6.6 us
    unnamed x12, local copies, waits for them, and re-layouts  3.86 us
    dynamic_slice x2, local copies, waits for them, and re-layouts, piece(): return lax.dynamic_slice_in_dim(source, (index ^ slot) * width, width, 1)  3.3 us
  transfers between devices with their start and end apart: 11, of which 6 were waited for; matrix products, arithmetic and copies ran while one was open for 4% of the time, Pallas kernels for 19%

profile of v2, /device:TPU:8, one launch (start us, length us, event | category | flops | bytes accessed | tf_op | source)
XLA Modules:
  0.0 133.5 jit_solution(13928642006890044693)
XLA Ops:
  0.0 2.2 %constant_dynamic-slice_fusion = (bf16[512,512]{1,0:T(8,128)(2,1)}, bf16[512,512]{1,0:T(8,128)(2,1)S(1)}) fusion(bf16[512,2048]{1,0:T(8,128)(2,1)} %param.4, s32[]{:T(128)S(6)} %select_n.92, s32[]{:T(128)S(6)} %select_n.87), kind=kLoop, calls=%fused_computation.11 | loop fusion | bytes 2097160 | tf_op jit(solution)/shard_map/dynamic_slice | solution.py:397
  2.2 0.6 fusion.3
  2.9 0.7 all_to_all.6
  3.6 6.6 %all-to-all-start = ((f32[32,1,512]{2,1,0:T(1,128)}), f32[32,1,512]{2,1,0:T(1,128)S(1)}, u32[]{:S(2)}, u32[]{:S(2)}) async-start(f32[32,1,512]{2,1,0:T(1,128)} %all_to_all.6), calls=%async_computation | async-start | bytes 131072 | tf_op jit(solution)/shard_map/all_to_all | solution.py:406
  10.3 1.5 %collective-permute-start.5 = (bf16[512,512]{1,0:T(8,128)(2,1)}, bf16[512,512]{1,0:T(8,128)(2,1)}, u32[]{:S(2)}, u32[]{:S(2)}) collective-permute-start(bf16[512,512]{1,0:T(8,128)(2,1)} %get-tuple-element.23), channel_id=1, source_target_pairs={{0,6},{1,7},{2,4},{3,5},{4,2},{5,3},{6,0},{7,1},{8,14},{9,15},{10,... | collective-permute-start | bytes 1572872 | tf_op jit(solution)/shard_map/ppermute | solution.py:394
  11.8 5.3 %collective-permute-done.refs_2_ = bf16[512,512]{1,0:T(8,128)(2,1)} collective-permute-done((bf16[512,512]{1,0:T(8,128)(2,1)S(1)}, bf16[512,512]{1,0:T(8,128)(2,1)}, u32[]{:S(2)}, u32[]{:S(2)}) %collective-permute-start) | collective-permute-done | bytes 524320 | tf_op jit(solution)/shard_map/ppermute | solution.py:394
  17.1 1.1 constant_dynamic-slice_fusion.1
  18.2 3.9 %collective-permute-start.3 = (bf16[512,512]{1,0:T(8,128)(2,1)}, bf16[512,512]{1,0:T(8,128)(2,1)}, u32[]{:S(2)}, u32[]{:S(2)}) collective-permute-start(bf16[512,512]{1,0:T(8,128)(2,1)} %get-tuple-element.25), channel_id=1, source_target_pairs={{0,4},{1,5},{2,6},{3,7},{4,0},{5,1},{6,2},{7,3},{8,12},{9,13},{10,... | collective-permute-start | bytes 1572872 | tf_op jit(solution)/shard_map/ppermute | solution.py:394
  22.3 1.5 %dynamic-slice_bitcast_fusion.1.refs_5_.refs_7_.refs_8_ = bf16[512,1536]{1,0:T(8,128)(2,1)S(1)} fusion(bf16[4,512,1536]{2,1,0:T(8,128)(2,1)} %param.5, s32[]{:T(128)S(6)} %select_n.90), kind=kLoop, calls=%fused_computation.1 | loop fusion | bytes 3145732 | tf_op jit(solution)/shard_map/jit(dynamic_index_in_dim)/squeeze | solution.py:399
  24.0 1.5 %dynamic-slice_bitcast_fusion.refs_7_.refs_9_.refs_10_ = bf16[3,512,512]{2,1,0:T(8,128)(2,1)S(1)} fusion(bf16[4,3,512,512]{3,2,1,0:T(8,128)(2,1)} %param.7, s32[]{:T(128)S(6)} %select_n.90), kind=kLoop, calls=%fused_computation | loop fusion | bytes 3145732 | tf_op jit(solution)/shard_map/jit(dynamic_index_in_dim)/squeeze | solution.py:400
  25.6 14.6 %stage.3 = (bf16[512,512]{1,0:T(8,128)(2,1)}, bf16[512,512]{1,0:T(8,128)(2,1)}, bf16[3,512,512]{2,1,0:T(8,128)(2,1)S(1)}) custom-call(s32[10]{0:T(128)S(1)} %stack.81.table, bf16[512,512]{1,0:T(8,128)(2,1)} %get-tuple-element.26.refs_0_, bf16[512,512]{1,0:T(8,128)(2,1)} %collective-permute-done.1.refs_1_.refs_4_, ...), custom_call_target="tpu_custom_call" | custom-call | tf_op jit(solution)/shard_map/stage/pallas_call | solution.py:347
  40.2 1.1 copy-done.1
  41.3 7.2 %collective-permute-done.5.refs_2_ = bf16[512,512]{1,0:T(8,128)(2,1)} collective-permute-done((bf16[512,512]{1,0:T(8,128)(2,1)}, bf16[512,512]{1,0:T(8,128)(2,1)}, u32[]{:S(2)}, u32[]{:S(2)}) %collective-permute-start.5) | collective-permute-done | bytes 524320 | tf_op jit(solution)/shard_map/ppermute | solution.py:394
  48.6 9.4 %collective-permute-done.3.refs_0_ = bf16[512,512]{1,0:T(8,128)(2,1)} collective-permute-done((bf16[512,512]{1,0:T(8,128)(2,1)}, bf16[512,512]{1,0:T(8,128)(2,1)}, u32[]{:S(2)}, u32[]{:S(2)}) %collective-permute-start.3) | collective-permute-done | bytes 524320 | tf_op jit(solution)/shard_map/ppermute | solution.py:394
  58.2 2.1 %collective-permute-done.4.refs_1_.refs_4_ = bf16[512,512]{1,0:T(8,128)(2,1)} collective-permute-done((bf16[512,512]{1,0:T(8,128)(2,1)}, bf16[512,512]{1,0:T(8,128)(2,1)}, u32[]{:S(2)}, u32[]{:S(2)}) %collective-permute-start.4) | collective-permute-done | bytes 524320 | tf_op jit(solution)/shard_map/ppermute | solution.py:394
  60.3 1.4 %copy-done.2 = bf16[3,512,512]{2,1,0:T(8,128)(2,1)S(1)} copy-done((bf16[3,512,512]{2,1,0:T(8,128)(2,1)S(1)}, bf16[3,512,512]{2,1,0:T(8,128)(2,1)}, u32[]{:S(2)}) %copy-start.2) | copy-done | bytes 1572888
  61.7 20.9 %stage.4 = (bf16[512,512]{1,0:T(8,128)(2,1)S(1)}, bf16[512,512]{1,0:T(8,128)(2,1)S(1)}, bf16[3,512,512]{2,1,0:T(8,128)(2,1)S(1)}) custom-call(s32[10]{0:T(128)S(1)} %stack.89.table, bf16[512,512]{1,0:T(8,128)(2,1)} %collective-permute-done.3.refs_0_, bf16[512,512]{1,0:T(8,128)(2,1)} %collective-permute-done.4.refs_1_.refs_4_, ...), custom_call_target="tpu_custom_call" | custom-call | flops 12884901888 | bytes 25165824 | tf_op jit(solution)/shard_map/stage/pallas_call | solution.py:347
  82.5 2.8 %collective-permute-start.7 = (bf16[512,512]{1,0:T(8,128)(2,1)S(1)}, bf16[512,512]{1,0:T(8,128)(2,1)S(1)}, u32[]{:S(2)}, u32[]{:S(2)}) collective-permute-start(bf16[512,512]{1,0:T(8,128)(2,1)S(1)} %get-tuple-element.20), channel_id=1, source_target_pairs={{0,4},{1,5},{2,6},{3,7},{4,0},{5,1},{6,2},{7,3},{8,12},{9,13},{10,... | collective-permute-start | bytes 1572872 | tf_op jit(solution)/shard_map/ppermute | solution.py:394
  85.4 1.6 %collective-permute-start.8 = (bf16[512,512]{1,0:T(8,128)(2,1)S(1)}, bf16[512,512]{1,0:T(8,128)(2,1)S(1)}, u32[]{:S(2)}, u32[]{:S(2)}) collective-permute-start(bf16[512,512]{1,0:T(8,128)(2,1)S(1)} %get-tuple-element.21), channel_id=1, source_target_pairs={{0,6},{1,7},{2,4},{3,5},{4,2},{5,3},{6,0},{7,1},{8,14},{9,15},{10,... | collective-permute-start | bytes 1572872 | tf_op jit(solution)/shard_map/ppermute | solution.py:394
  86.9 11.3 %stage.5 = (bf16[512,512]{1,0:T(8,128)(2,1)S(1)}, bf16[512,512]{1,0:T(8,128)(2,1)S(1)}, bf16[3,512,512]{2,1,0:T(8,128)(2,1)}) custom-call(s32[10]{0:T(128)S(1)} %stack.79.table, bf16[512,512]{1,0:T(8,128)(2,1)} %get-tuple-element.26.refs_0_, bf16[512,512]{1,0:T(8,128)(2,1)} %collective-permute-done.1.refs_1_.refs_4_, ...), custom_call_target="tpu_custom_call" | custom-call | flops 12884901888 | bytes 25165824 | tf_op jit(solution)/shard_map/stage/pallas_call | solution.py:347
  98.7 19.9 %collective-permute-done.7 = bf16[512,512]{1,0:T(8,128)(2,1)S(1)} collective-permute-done((bf16[512,512]{1,0:T(8,128)(2,1)S(1)}, bf16[512,512]{1,0:T(8,128)(2,1)S(1)}, u32[]{:S(2)}, u32[]{:S(2)}) %collective-permute-start.7) | collective-permute-done | bytes 524320 | tf_op jit(solution)/shard_map/ppermute | solution.py:394
  118.7 12.6 %collective-permute-done.8 = bf16[512,512]{1,0:T(8,128)(2,1)S(1)} collective-permute-done((bf16[512,512]{1,0:T(8,128)(2,1)S(1)}, bf16[512,512]{1,0:T(8,128)(2,1)S(1)}, u32[]{:S(2)}, u32[]{:S(2)}) %collective-permute-start.8) | collective-permute-done | bytes 524320 | tf_op jit(solution)/shard_map/ppermute | solution.py:394
  131.4 1.3 copy-done.5
  132.7 0.8 constant_dynamic-update-slice_fusion
  (31 shorter events, 1.2 us)
Async XLA Ops:
  0.0 2.2 %copy-start = (bf16[2048,16]{0,1:T(8,128)(2,1)S(1)}, bf16[2048,16]{0,1:T(8,128)(2,1)}, u32[]{:S(2)}) copy-start(bf16[2048,16]{0,1:T(8,128)(2,1)} %param.6) | copy-start | bytes 196612
  0.0 2.2 %copy-start.4 = (bf16[512,2048]{1,0:T(8,128)(2,1)S(1)}, bf16[512,2048]{1,0:T(8,128)(2,1)}, u32[]{:S(2)}) copy-start(bf16[512,2048]{1,0:T(8,128)(2,1)} %param.4) | copy-start | bytes 6291460
  2.2 14.9 %collective-permute-start = (bf16[512,512]{1,0:T(8,128)(2,1)S(1)}, bf16[512,512]{1,0:T(8,128)(2,1)}, u32[]{:S(2)}, u32[]{:S(2)}) collective-permute-start(bf16[512,512]{1,0:T(8,128)(2,1)S(1)} %get-tuple-element.24), channel_id=1, source_target_pairs={{0,2},{1,3},{2,0},{3,1},{4,6},{5,7},{6,4},{7,5},{8,10},{9,11},{10,... | collective-permute-start | bytes 1572872 | tf_op jit(solution)/shard_map/ppermute | solution.py:394
  3.6 21.9 %all-to-all-start = ((f32[32,1,512]{2,1,0:T(1,128)}), f32[32,1,512]{2,1,0:T(1,128)S(1)}, u32[]{:S(2)}, u32[]{:S(2)}) async-start(f32[32,1,512]{2,1,0:T(1,128)} %all_to_all.6), calls=%async_computation | async-start | bytes 131072 | tf_op jit(solution)/shard_map/all_to_all | solution.py:406
  10.3 38.3 %collective-permute-start.5 = (bf16[512,512]{1,0:T(8,128)(2,1)}, bf16[512,512]{1,0:T(8,128)(2,1)}, u32[]{:S(2)}, u32[]{:S(2)}) collective-permute-start(bf16[512,512]{1,0:T(8,128)(2,1)} %get-tuple-element.23), channel_id=1, source_target_pairs={{0,6},{1,7},{2,4},{3,5},{4,2},{5,3},{6,0},{7,1},{8,14},{9,15},{10,... | collective-permute-start | bytes 1572872 | tf_op jit(solution)/shard_map/ppermute | solution.py:394
  18.2 7.3 %collective-permute-start.1 = (bf16[512,512]{1,0:T(8,128)(2,1)}, bf16[512,512]{1,0:T(8,128)(2,1)}, u32[]{:S(2)}, u32[]{:S(2)}) collective-permute-start(bf16[512,512]{1,0:T(8,128)(2,1)} %get-tuple-element.26.refs_0_), channel_id=1, source_target_pairs={{0,1},{1,0},{2,3},{3,2},{4,5},{5,4},{6,7},{7,6},{8,9},{9,8},{10,11... | collective-permute-start | bytes 1572872 | tf_op jit(solution)/shard_map/ppermute | solution.py:394
  18.2 39.8 %collective-permute-start.3 = (bf16[512,512]{1,0:T(8,128)(2,1)}, bf16[512,512]{1,0:T(8,128)(2,1)}, u32[]{:S(2)}, u32[]{:S(2)}) collective-permute-start(bf16[512,512]{1,0:T(8,128)(2,1)} %get-tuple-element.25), channel_id=1, source_target_pairs={{0,4},{1,5},{2,6},{3,7},{4,0},{5,1},{6,2},{7,3},{8,12},{9,13},{10,... | collective-permute-start | bytes 1572872 | tf_op jit(solution)/shard_map/ppermute | solution.py:394
  22.1 3.5 %collective-permute-start.2 = (bf16[512,512]{1,0:T(8,128)(2,1)}, bf16[512,512]{1,0:T(8,128)(2,1)}, u32[]{:S(2)}, u32[]{:S(2)}) collective-permute-start(bf16[512,512]{1,0:T(8,128)(2,1)} %collective-permute-done.refs_2_), channel_id=1, source_target_pairs={{0,1},{1,0},{2,3},{3,2},{4,5},{5,4},{6,7},{7,6},{8,9},{9,8},{10,11... | collective-permute-start | bytes 1572872 | tf_op jit(solution)/shard_map/ppermute | solution.py:394
  40.2 1.1 copy-start.1
  48.6 9.6 %collective-permute-start.6 = (bf16[512,512]{1,0:T(8,128)(2,1)}, bf16[512,512]{1,0:T(8,128)(2,1)}, u32[]{:S(2)}, u32[]{:S(2)}) collective-permute-start(bf16[512,512]{1,0:T(8,128)(2,1)} %collective-permute-done.5.refs_2_), channel_id=1, source_target_pairs={{0,1},{1,0},{2,3},{3,2},{4,5},{5,4},{6,7},{7,6},{8,9},{9,8},{10,11... | collective-permute-start | bytes 1572872 | tf_op jit(solution)/shard_map/ppermute | solution.py:394
  58.0 2.3 %collective-permute-start.4 = (bf16[512,512]{1,0:T(8,128)(2,1)}, bf16[512,512]{1,0:T(8,128)(2,1)}, u32[]{:S(2)}, u32[]{:S(2)}) collective-permute-start(bf16[512,512]{1,0:T(8,128)(2,1)} %collective-permute-done.3.refs_0_), channel_id=1, source_target_pairs={{0,1},{1,0},{2,3},{3,2},{4,5},{5,4},{6,7},{7,6},{8,9},{9,8},{10,11... | collective-permute-start | bytes 1572872 | tf_op jit(solution)/shard_map/ppermute | solution.py:394
  60.3 1.4 %copy-start.2 = (bf16[3,512,512]{2,1,0:T(8,128)(2,1)S(1)}, bf16[3,512,512]{2,1,0:T(8,128)(2,1)}, u32[]{:S(2)}) copy-start(bf16[3,512,512]{2,1,0:T(8,128)(2,1)} %copy-done.1) | copy-start | bytes 4718596
  61.7 25.2 %copy-start.3 = (bf16[3,512,512]{2,1,0:T(8,128)(2,1)S(1)}, bf16[3,512,512]{2,1,0:T(8,128)(2,1)}, u32[]{:S(2)}) copy-start(bf16[3,512,512]{2,1,0:T(8,128)(2,1)} %copy-done.1) | copy-start | bytes 4718596
  82.5 36.0 %collective-permute-start.7 = (bf16[512,512]{1,0:T(8,128)(2,1)S(1)}, bf16[512,512]{1,0:T(8,128)(2,1)S(1)}, u32[]{:S(2)}, u32[]{:S(2)}) collective-permute-start(bf16[512,512]{1,0:T(8,128)(2,1)S(1)} %get-tuple-element.20), channel_id=1, source_target_pairs={{0,4},{1,5},{2,6},{3,7},{4,0},{5,1},{6,2},{7,3},{8,12},{9,13},{10,... | collective-permute-start | bytes 1572872 | tf_op jit(solution)/shard_map/ppermute | solution.py:394
  85.4 46.0 %collective-permute-start.8 = (bf16[512,512]{1,0:T(8,128)(2,1)S(1)}, bf16[512,512]{1,0:T(8,128)(2,1)S(1)}, u32[]{:S(2)}, u32[]{:S(2)}) collective-permute-start(bf16[512,512]{1,0:T(8,128)(2,1)S(1)} %get-tuple-element.21), channel_id=1, source_target_pairs={{0,6},{1,7},{2,4},{3,5},{4,2},{5,3},{6,0},{7,1},{8,14},{9,15},{10,... | collective-permute-start | bytes 1572872 | tf_op jit(solution)/shard_map/ppermute | solution.py:394
  98.2 33.2 %collective-permute-start.9 = (bf16[512,512]{1,0:T(8,128)(2,1)S(1)}, bf16[512,512]{1,0:T(8,128)(2,1)S(1)}, u32[]{:S(2)}, u32[]{:S(2)}) collective-permute-start(bf16[512,512]{1,0:T(8,128)(2,1)S(1)} %get-tuple-element.22), channel_id=1, source_target_pairs={{0,2},{1,3},{2,0},{3,1},{4,6},{5,7},{6,4},{7,5},{8,10},{9,11},{10,... | collective-permute-start | bytes 1572872 | tf_op jit(solution)/shard_map/ppermute | solution.py:394
  131.4 1.3 copy-start.5

commit v3 on v2

--- a/solution.py
+++ b/solution.py
@@ -12,8 +12,8 @@
 
 rate_base = 0.003
 epsilon = 1e-06
-VMEM_LIMIT = 33 * 1024 * 1024
-BEGIN_LIMIT = 33 * 1024 * 1024
+VMEM_LIMIT = 40 * 1024 * 1024
+STATE = 64
 
 
 def from_behind(block, axis, distance):
@@ -176,20 +176,23 @@
     pltpu.make_async_copy(target, target, sem).wait()
 
 
-def learn(at, x, m, rate_row, pool, put_query, put_key_value):
+def learn(at, x, source, m, rate_row, pool, put_query, put_key_value):
     rows, width = x.shape[1:]
     here = pl.ds(pl.multiple_of(rows * at, rows), rows)
-    key_rows = matmul(x[at], m[:, width : 2 * width]).astype(jnp.bfloat16)
-    value_rows = matmul(x[at], m[:, 2 * width :]).astype(jnp.bfloat16)
-    put_key_value(key_rows, value_rows)
+    key_rows = matmul(x[source], m[:, width : 2 * width]).astype(jnp.bfloat16)
+    value_rows = matmul(x[source], m[:, 2 * width :]).astype(jnp.bfloat16)
+    if put_key_value is not None:
+        put_key_value(key_rows, value_rows)
     pool[0, here] = unit_rows(key_rows)
     spread = jnp.broadcast_to(rate_row, (128, rows)).T
     spread = jnp.concatenate([spread] * (width // 128), 1)
     pool[2, here] = (spread * value_rows.astype(jnp.float32)).astype(jnp.bfloat16)
 
-    @pl.when(at % 2 == 0)
-    def _():
-        put_query(matmul(x[at], m[:, :width]).astype(jnp.bfloat16))
+    if put_query is not None:
+
+        @pl.when(at % 2 == 0)
+        def _():
+            put_query(matmul(x[source], m[:, :width]).astype(jnp.bfloat16))
 
 
 def deltas(at, rows, w, pool):
@@ -204,8 +207,107 @@
     pool[4, here] = (back * gated).astype(jnp.bfloat16)
 
 
-def gradient(at, pool):
-    return matmul_tn(pool[at // 2], pool[jnp.where(at == 2, 2, 3 + at)])
+def gradient(at, pool, rows):
+    return matmul_tn(pool[at // 2, :rows], pool[jnp.where(at == 2, 2, 3 + at), :rows])
+
+
+def renew(updated, initial):
+    origin = initial.astype(jnp.float32)
+    wanted = jnp.mean(origin * origin, axis=-1, keepdims=True) + epsilon
+    held = jnp.mean(updated * updated, axis=-1, keepdims=True) + epsilon
+    return (updated * (jnp.sqrt(wanted) * lax.rsqrt(held))).astype(jnp.bfloat16)
+
+
+def begin_kernel(count, table, *refs):
+    near, far, refs = refs[:count], refs[count : count + 2], refs[count + 2 :]
+    maps, rate, initial, state, x, m, w, fresh, kept, grads, pool, sems = refs
+    rows = x.shape[1]
+    updates = table[0] > 0
+    fetch(maps, m, sems.at[count + 2])
+    for at in range(count):
+        fetch(near[at], x.at[at], sems.at[at], updates)
+    for at in range(2):
+        fetch(far[at], x.at[count + at], sems.at[count + at])
+    fetch(initial, w, sems.at[count + 3])
+    fetched(m, sems.at[count + 2])
+
+    @pl.when(updates)
+    def _():
+        @pl.loop(0, count, unroll=True)
+        def _(at):
+            fetched(x.at[at], sems.at[at])
+            learn(at, x, at, m, rate[pl.ds(table[1 + at], 1)], pool, None, None)
+
+        fetched(w, sems.at[count + 3])
+        pl.loop(0, count, unroll=True)(lambda at: deltas(at, rows, w, pool))
+
+        @pl.loop(0, 3)
+        def _(at):
+            fresh[at] = renew(w[at].astype(jnp.float32) + gradient(at, pool, count * rows), w[at])
+
+    @pl.when(jnp.logical_not(updates))
+    def _():
+        fetched(w, sems.at[count + 3])
+        fresh[...] = w[...]
+
+    send = [pltpu.make_async_copy(fresh, state.at[pl.ds(0, 3)], sems.at[0])]
+    send[0].start()
+
+    @pl.loop(0, 2, unroll=True)
+    def _(at):
+        def put_query(query_rows):
+            kept[0] = query_rows
+
+        def put_key_value(key_rows, value_rows):
+            kept[1 + at] = key_rows
+            kept[3 + at] = value_rows
+
+        fetched(x.at[count + at], sems.at[count + at])
+        learn(at, x, count + at, m, rate[pl.ds(table[1 + count + at], 1)], pool, put_query, put_key_value)
+
+    send.append(pltpu.make_async_copy(kept, state.at[pl.ds(3, 5)], sems.at[1]))
+    send[1].start()
+    pl.loop(0, 2, unroll=True)(lambda at: deltas(at, rows, fresh, pool))
+
+    @pl.loop(0, 3)
+    def _(at):
+        grads[at] = gradient(at, pool, 2 * rows).astype(jnp.bfloat16)
+
+    send.append(pltpu.make_async_copy(grads, state.at[pl.ds(8, 3)], sems.at[2]))
+    send[2].start()
+    for copy in send:
+        copy.wait()
+
+
+def begin(table, near, far, maps, rate, initial):
+    rows, width = near[0].shape
+    count = len(near)
+    anywhere = pl.BlockSpec(memory_space=pl.ANY)
+    bfloat = functools.partial(pltpu.VMEM, dtype=jnp.bfloat16)
+    operands = [*near, *far, maps]
+    return pl.pallas_call(
+        functools.partial(begin_kernel, count),
+        grid_spec=pltpu.PrefetchScalarGridSpec(
+            num_scalar_prefetch=1,
+            grid=(),
+            in_specs=[anywhere] * len(operands) + [pl.BlockSpec(memory_space=pltpu.VMEM), anywhere],
+            out_specs=anywhere,
+            scratch_shapes=[
+                bfloat((count + 2, rows, width)),
+                bfloat(maps.shape),
+                bfloat(initial.shape),
+                bfloat(initial.shape),
+                bfloat((5, rows, width)),
+                bfloat(initial.shape),
+                bfloat((5, count * rows, width)),
+                pltpu.SemaphoreType.DMA((count + 4,)),
+            ],
+        ),
+        out_shape=jax.ShapeDtypeStruct((STATE, rows, width), jnp.bfloat16),
+        compiler_params=pltpu.CompilerParams(vmem_limit_bytes=VMEM_LIMIT),
+        cost_estimate=pl.CostEstimate(flops=1, bytes_accessed=1, transcendentals=0),
+        name="begin",
+    )(table, *operands, rate, initial)
 
 
 def stage_kernel(counts, table, *refs):
@@ -214,7 +316,6 @@
     blocks, refs = refs[:count], refs[count:]
     before, refs = refs[:befores], refs[befores:]
     earlier, refs = refs[:earliers], refs[earliers:]
-    held, refs = refs[: 2 * begun], refs[2 * begun :]
     (maps, rate, initial), refs = refs[:3], refs[3:]
     results, new, refs = refs[:slots], refs[slots], refs[slots + 1 :]
     x, m, w, start, fresh, k, v, q, attended, pool, out, sems, *grads = refs
@@ -235,7 +336,7 @@
 
         @pl.loop(0, slots)
         def _(at):
-            @pl.loop(0, 2)
+            @pl.loop(0, 2, unroll=True)
             def _(half):
                 own = span(part * half, part)
                 base = rows * table[6 + 2 * at] + part * half
@@ -267,19 +368,18 @@
         for at in range(befores):
             fetch(before[at], x.at[count], sems.at[count], there & (table[4] == at))
         for at in range(earliers):
-            fetch(earlier[at], w, at_weights, table[5] == at)
-        fetch(initial, w, at_weights, table[5] >= earliers)
+            fetch(earlier[at].at[pl.ds(0, 3)], w, at_weights, table[5] == at)
         fetch(initial, start, at_start)
         if begun:
             for at in range(2):
                 to = span(rows * (table[6 + count + at] + 1))
-                fetch(held[0].at[1 + at], k.at[to], at_held)
-                fetch(held[0].at[3 + at], v.at[to], at_held)
-            fetch(held[0].at[0], q.at[slots - 1], at_held)
-            fetch(held[1], grads[0], at_grads)
+                fetch(earlier[0].at[4 + at], k.at[to], at_held)
+                fetch(earlier[0].at[6 + at], v.at[to], at_held)
+            fetch(earlier[0].at[3], q.at[slots - 1], at_held)
+            fetch(earlier[0].at[pl.ds(8, 3)], grads[0], at_grads)
         fetched(m, at_maps)
 
-        @pl.loop(0, count)
+        @pl.loop(0, count, unroll=True)
         def _(at):
             to = span(rows * (table[6 + at] + 1))
 
@@ -291,7 +391,7 @@
                 v[to] = value_rows
 
             fetched(x.at[at], sems.at[at])
-            learn(at, x, m, rate[pl.ds(first + table[6 + at], 1)], pool, put_query, put_key_value)
+            learn(at, x, at, m, rate[pl.ds(first + table[6 + at], 1)], pool, put_query, put_key_value)
 
         @pl.when(there)
         def _():
@@ -313,17 +413,14 @@
 
         @pl.when(updates)
         def _():
-            pl.loop(0, count)(lambda at: deltas(at, rows, w, pool))
+            pl.loop(0, count, unroll=True)(lambda at: deltas(at, rows, w, pool))
 
             @pl.loop(0, 3)
             def _(at):
-                updated = w[at].astype(jnp.float32) + gradient(at, pool)
+                updated = w[at].astype(jnp.float32) + gradient(at, pool, count * rows)
                 if begun:
-                    updated = updated + grads[0][at]
-                origin = start[at].astype(jnp.float32)
-                wanted = jnp.mean(origin * origin, axis=-1, keepdims=True) + epsilon
-                held_now = jnp.mean(updated * updated, axis=-1, keepdims=True) + epsilon
-                fresh[at] = (updated * (jnp.sqrt(wanted) * lax.rsqrt(held_now))).astype(jnp.bfloat16)
+                    updated = updated + grads[0][at].astype(jnp.float32)
+                fresh[at] = renew(updated, start[at])
 
             send_new.start()
 
@@ -335,15 +432,15 @@
         pl.when(updates)(send_new.wait)
 
 
-def stage(table, blocks, before, earlier, maps, rate, initial, held=(), scale=24):
-    count, begun = len(blocks), len(held) // 2
+def stage(table, blocks, before, earlier, maps, rate, initial, begun=False, scale=24):
+    count, begun = len(blocks), int(begun)
     rows, width = blocks[0].shape
     matrices = initial.shape
     bfloat = functools.partial(pltpu.VMEM, dtype=jnp.bfloat16)
     anywhere = pl.BlockSpec(memory_space=pl.ANY)
     slots = count // 2 + begun
     stretch = 2 * slots * rows
-    operands = [*blocks, *before, *earlier, *held, maps]
+    operands = [*blocks, *before, *earlier, maps]
     return pl.pallas_call(
         functools.partial(stage_kernel, (count, len(before), len(earlier), begun)),
         grid_spec=pltpu.PrefetchScalarGridSpec(
@@ -365,7 +462,7 @@
                 bfloat((slots, rows, width)),
                 pltpu.SemaphoreType.DMA((count + 7 + slots,)),
             ]
-            + [pltpu.VMEM(matrices, jnp.float32)] * begun,
+            + [bfloat(matrices)] * begun,
         ),
         out_shape=[jax.ShapeDtypeStruct((rows, width), jnp.bfloat16)] * slots
         + [jax.ShapeDtypeStruct(matrices, jnp.bfloat16)],
@@ -406,11 +503,9 @@
     terms = lax.all_to_all(jnp.repeat(terms, 2, axis=0), ("head", "tok"), 0, 0, tiled=True)
     logits = jnp.sum(terms.reshape(-1, groups, rows), 0)
     rate = (rate_base * jax.nn.softplus(logits)).astype(jnp.bfloat16).astype(jnp.float32)
-    source = tokens
-    for slot in range(1, slots):
-        source = after(source, same[slot])
+    source = after(tokens, *(same[slot] for slot in range(1, slots)))
     for slot in range(slots, last):
-        same[slot] = swap(piece(slot, source, chip), 2 * slot)
+        same[slot] = swap(after(piece(slot, source, chip), same[last]), 2 * slot)
     same[0] = piece(0, source, chip)
     other = {slot: swap(same[slot], 1) for slot in range(slots)}
 
@@ -433,15 +528,20 @@
     near_blocks = [block for slot in near_slots for block in (same[slot], other[slot])]
     near_others = [other[slot] for slot in near_slots]
     shared = dict(maps=maps, rate=rate, initial=initial)
-    *_, first_new = stage(table(near_slots, is_first, False, 0), near_blocks, near_others[:1], [], scale=0, **shared)
-    for slot in far_slots:
-        other[slot] = swap(after(same[slot], first_new), 1)
-    far_blocks = [block for slot in far_slots for block in (same[slot], other[slot])]
+    other[last] = swap(same[last], 1)
+    rates_in = [opening(slot) + place for slot in (*near_slots, last) for place in places(slot)]
+    state = begin(integers([is_first] + rates_in), near_blocks, [same[last], other[last]], **shared)
+    far_blocks = []
+    for slot in far_slots[:-1]:
+        same[slot] = after(same[slot], state)
+        other[slot] = swap(same[slot], 1)
+        far_blocks += [same[slot], other[slot]]
     *far_results, far_new = stage(
-        table(far_slots, True, True, 1 - is_first), far_blocks, near_others, [first_new], **shared
+        table(far_slots, True, True, 0), far_blocks, near_others, [state], begun=True, **shared
     )
     *near_results, _ = stage(
-        table(near_slots, 1 - is_first, True, 1 - is_first), near_blocks, [other[slot] for slot in far_slots], [first_new, far_new], **shared
+        table(near_slots, 1 - is_first, True, 1 - is_first), near_blocks,
+        [other[slot] for slot in far_slots], [state, far_new], **shared
     )
     results = near_results + far_results
     combined = jnp.zeros_like(tokens)

time: 135 us -> 123 us (0.911)
  waiting for transfers between devices: 56.6 us -> 51.1 us
  local copies, waits for them, and re-layouts: 12.5 us -> 9.11 us
  starting transfers between devices: 16.7 us -> 15.2 us
  Pallas kernels: 46.8 us -> 45.4 us
    pallas_call x3 -> x2, Pallas kernels: 46.8 us -> 24.9 us  [stage(): pl.pallas_call(functools.partial(stage_kernel, (count, len(before), len(e...]
    pallas_call x0 -> x1, Pallas kernels: none -> 20.4 us  [begin(): pl.pallas_call(functools.partial(begin_kernel, count), grid_spec=pltpu.Pr...]
    ppermute x10, waiting for transfers between devices: 56.6 us -> 51.1 us  [swap(): return lax.ppermute(block, 'tok', [(i, i ^ bits) for i in range(groups)])]
    unnamed x12 -> x6, local copies, waits for them, and re-layouts: 3.86 us -> 1.31 us
    all_to_all x1, starting transfers between devices: 6.6 us -> 4.69 us  [head_body(): lax.all_to_all(jnp.repeat(terms, 2, axis=0), ('head', 'tok'), 0, 0, tiled...]
  transfers between devices with their start and end apart: 11 -> 11, of which waited for: 6 -> 5; matrix products, arithmetic and copies ran while one was open for 4% -> 5% of each run, Pallas kernels for 19% -> 25%
where the time goes in v3:
time: 123 us; the launch traced here: 122 us
  waiting for transfers between devices  51.1 us (42%)
  Pallas kernels  45.4 us (37%)
  starting transfers between devices  15.2 us (12%)
  local copies, waits for them, and re-layouts  9.11 us (7%)
    ppermute x10, waiting for transfers between devices, swap(): return lax.ppermute(block, 'tok', [(i, i ^ bits) for i in range(groups)])  51.1 us
    pallas_call x2, Pallas kernels, stage(): pl.pallas_call(functools.partial(stage_kernel, (count, len(before), len(e...  24.9 us
    pallas_call x1, Pallas kernels, begin(): pl.pallas_call(functools.partial(begin_kernel, count), grid_spec=pltpu.Pr...  20.4 us
    ppermute x10, starting transfers between devices, swap(): return lax.ppermute(block, 'tok', [(i, i ^ bits) for i in range(groups)])  10.5 us
    all_to_all x1, starting transfers between devices, head_body(): lax.all_to_all(jnp.repeat(terms, 2, axis=0), ('head', 'tok'), 0, 0, tiled...  4.69 us
    dynamic_slice x2, local copies, waits for them, and re-layouts, piece(): return lax.dynamic_slice_in_dim(source, (index ^ slot) * width, width, 1)  2.51 us
  transfers between devices with their start and end apart: 11, of which 5 were waited for; matrix products, arithmetic and copies ran while one was open for 5% of the time, Pallas kernels for 25%

profile of v3, /device:TPU:8, one launch (start us, length us, event | category | flops | bytes accessed | tf_op | source)
XLA Modules:
  0.0 121.9 jit_solution(17526988520861627842)
XLA Ops:
  0.0 1.4 %constant_dynamic-slice_fusion = (bf16[512,512]{1,0:T(8,128)(2,1)S(1)}, bf16[512,512]{1,0:T(8,128)(2,1)S(1)}) fusion(bf16[512,2048]{1,0:T(8,128)(2,1)} %param.4, s32[]{:T(128)S(6)} %select_n.101, s32[]{:T(128)S(6)} %select_n.98), kind=kLoop, calls=%fused_computation.11 | loop fusion | bytes 2097160 | tf_op jit(solution)/shard_map/dynamic_slice | solution.py:494
  1.5 3.1 %collective-permute-start.3 = (bf16[512,512]{1,0:T(8,128)(2,1)S(1)}, bf16[512,512]{1,0:T(8,128)(2,1)}, u32[]{:S(2)}, u32[]{:S(2)}) collective-permute-start(bf16[512,512]{1,0:T(8,128)(2,1)S(1)} %get-tuple-element.21), channel_id=1, source_target_pairs={{0,6},{1,7},{2,4},{3,5},{4,2},{5,3},{6,0},{7,1},{8,14},{9,15},{10,... | collective-permute-start | bytes 1572872 | tf_op jit(solution)/shard_map/ppermute | solution.py:491
  4.7 0.6 fusion.3
  5.3 0.7 all_to_all.6
  6.1 4.7 %all-to-all-start = ((f32[32,1,512]{2,1,0:T(1,128)}), f32[32,1,512]{2,1,0:T(1,128)S(1)}, u32[]{:S(2)}, u32[]{:S(2)}) async-start(f32[32,1,512]{2,1,0:T(1,128)} %all_to_all.6), calls=%async_computation | async-start | bytes 131072 | tf_op jit(solution)/shard_map/all_to_all | solution.py:503
  10.8 5.6 %collective-permute-done.refs_2_ = bf16[512,512]{1,0:T(8,128)(2,1)} collective-permute-done((bf16[512,512]{1,0:T(8,128)(2,1)S(1)}, bf16[512,512]{1,0:T(8,128)(2,1)}, u32[]{:S(2)}, u32[]{:S(2)}) %collective-permute-start) | collective-permute-done | bytes 524320 | tf_op jit(solution)/shard_map/ppermute | solution.py:491
  16.4 1.1 constant_dynamic-slice_fusion.1
  17.5 11.2 %collective-permute-done.3.refs_4_ = bf16[512,512]{1,0:T(8,128)(2,1)} collective-permute-done((bf16[512,512]{1,0:T(8,128)(2,1)S(1)}, bf16[512,512]{1,0:T(8,128)(2,1)}, u32[]{:S(2)}, u32[]{:S(2)}) %collective-permute-start.3) | collective-permute-done | bytes 524320 | tf_op jit(solution)/shard_map/ppermute | solution.py:491
  28.7 2.0 %collective-permute-start.4 = (bf16[512,512]{1,0:T(8,128)(2,1)}, bf16[512,512]{1,0:T(8,128)(2,1)}, u32[]{:S(2)}, u32[]{:S(2)}) collective-permute-start(bf16[512,512]{1,0:T(8,128)(2,1)} %get-tuple-element.14), channel_id=1, source_target_pairs={{0,4},{1,5},{2,6},{3,7},{4,0},{5,1},{6,2},{7,3},{8,12},{9,13},{10,... | collective-permute-start | bytes 1572872 | tf_op jit(solution)/shard_map/ppermute | solution.py:491
  30.9 0.3 collective-permute-start.5
  31.2 1.5 %dynamic-slice_bitcast_fusion.1.refs_6_.refs_5_.refs_8_ = bf16[512,1536]{1,0:T(8,128)(2,1)S(1)} fusion(bf16[4,512,1536]{2,1,0:T(8,128)(2,1)} %param.5, s32[]{:T(128)S(6)} %select_n.105), kind=kLoop, calls=%fused_computation.1 | loop fusion | bytes 3145732 | tf_op jit(solution)/shard_map/jit(dynamic_index_in_dim)/squeeze | solution.py:496
  33.0 1.5 %dynamic-slice_bitcast_fusion.refs_8_.refs_7_.refs_10_ = bf16[3,512,512]{2,1,0:T(8,128)(2,1)S(1)} fusion(bf16[4,3,512,512]{3,2,1,0:T(8,128)(2,1)} %param.7, s32[]{:T(128)S(6)} %select_n.105), kind=kLoop, calls=%fused_computation | loop fusion | bytes 3145732 | tf_op jit(solution)/shard_map/jit(dynamic_index_in_dim)/squeeze | solution.py:497
  34.6 20.4 %begin.1.refs_4_.refs_6_ = bf16[64,512,512]{2,1,0:T(8,128)(2,1)} custom-call(s32[7]{0:T(128)S(1)} %stack.97.table, bf16[512,512]{1,0:T(8,128)(2,1)} %get-tuple-element.24.refs_0_, bf16[512,512]{1,0:T(8,128)(2,1)} %collective-permute-done.1.refs_1_.refs_2_, bf16[512,512]{1,0:T(8,128)(2,1)} %collective-permute-done.refs_2_, ...), custom_call_target="tpu_custom_call" | custom-call | flops 1 | bytes 1 | tf_op jit(solution)/shard_map/begin/pallas_call | solution.py:288
  55.0 0.3 collective-permute-start.6
  55.5 1.9 %collective-permute-done.6.refs_1_.refs_4_ = bf16[512,512]{1,0:T(8,128)(2,1)} collective-permute-done((bf16[512,512]{1,0:T(8,128)(2,1)}, bf16[512,512]{1,0:T(8,128)(2,1)}, u32[]{:S(2)}, u32[]{:S(2)}) %collective-permute-start.6) | collective-permute-done | bytes 524320 | tf_op jit(solution)/shard_map/ppermute | solution.py:491
  57.4 14.4 %stage.2 = (bf16[512,512]{1,0:T(8,128)(2,1)S(1)}, bf16[512,512]{1,0:T(8,128)(2,1)S(1)}, bf16[3,512,512]{2,1,0:T(8,128)(2,1)S(1)}) custom-call(s32[10]{0:T(128)S(1)} %stack.105.table, bf16[512,512]{1,0:T(8,128)(2,1)} %collective-permute-done.4.refs_0_, bf16[512,512]{1,0:T(8,128)(2,1)} %collective-permute-done.6.refs_1_.refs_4_, ...), custom_call_target="tpu_custom_call" | custom-call | flops 12884901888 | bytes 25165824 | tf_op jit(solution)/shard_map/stage/pallas_call | solution.py:444
  71.9 2.6 %collective-permute-start.8 = (bf16[512,512]{1,0:T(8,128)(2,1)S(1)}, bf16[512,512]{1,0:T(8,128)(2,1)S(1)}, u32[]{:S(2)}, u32[]{:S(2)}) collective-permute-start(bf16[512,512]{1,0:T(8,128)(2,1)S(1)} %get-tuple-element.19), channel_id=1, source_target_pairs={{0,6},{1,7},{2,4},{3,5},{4,2},{5,3},{6,0},{7,1},{8,14},{9,15},{10,... | collective-permute-start | bytes 1572872 | tf_op jit(solution)/shard_map/ppermute | solution.py:491
  74.5 10.5 %stage.3 = (bf16[512,512]{1,0:T(8,128)(2,1)S(1)}, bf16[512,512]{1,0:T(8,128)(2,1)S(1)}, bf16[3,512,512]{2,1,0:T(8,128)(2,1)}) custom-call(s32[10]{0:T(128)S(1)} %stack.89.table, bf16[512,512]{1,0:T(8,128)(2,1)} %get-tuple-element.24.refs_0_, bf16[512,512]{1,0:T(8,128)(2,1)} %collective-permute-done.1.refs_1_.refs_2_, ...), custom_call_target="tpu_custom_call" | custom-call | flops 12884901888 | bytes 25165824 | tf_op jit(solution)/shard_map/stage/pallas_call | solution.py:444
  85.0 1.8 %collective-permute-start.9 = (bf16[512,512]{1,0:T(8,128)(2,1)S(1)}, bf16[512,512]{1,0:T(8,128)(2,1)S(1)}, u32[]{:S(2)}, u32[]{:S(2)}) collective-permute-start(bf16[512,512]{1,0:T(8,128)(2,1)S(1)} %get-tuple-element.20), channel_id=1, source_target_pairs={{0,2},{1,3},{2,0},{3,1},{4,6},{5,7},{6,4},{7,5},{8,10},{9,11},{10,... | collective-permute-start | bytes 1572872 | tf_op jit(solution)/shard_map/ppermute | solution.py:491
  86.8 0.2 broadcast_in_dim.6
  87.2 19.2 %collective-permute-done.7 = bf16[512,512]{1,0:T(8,128)(2,1)S(1)} collective-permute-done((bf16[512,512]{1,0:T(8,128)(2,1)S(1)}, bf16[512,512]{1,0:T(8,128)(2,1)S(1)}, u32[]{:S(2)}, u32[]{:S(2)}) %collective-permute-start.7) | collective-permute-done | bytes 524320 | tf_op jit(solution)/shard_map/ppermute | solution.py:491
  106.4 13.3 %collective-permute-done.8 = bf16[512,512]{1,0:T(8,128)(2,1)S(1)} collective-permute-done((bf16[512,512]{1,0:T(8,128)(2,1)S(1)}, bf16[512,512]{1,0:T(8,128)(2,1)S(1)}, u32[]{:S(2)}, u32[]{:S(2)}) %collective-permute-start.8) | collective-permute-done | bytes 524320 | tf_op jit(solution)/shard_map/ppermute | solution.py:491
  119.8 1.3 %copy-done.2 = bf16[512,2048]{1,0:T(8,128)(2,1)} copy-done((bf16[512,2048]{1,0:T(8,128)(2,1)}, bf16[512,2048]{1,0:T(8,128)(2,1)S(1)}, u32[]{:S(2)}) %copy-start.2) | copy-done | bytes 2097176
  121.1 0.8 constant_dynamic-update-slice_fusion
  (25 shorter events, 0.9 us)
Async XLA Ops:
  0.0 4.7 %copy-start = (bf16[2048,16]{0,1:T(8,128)(2,1)S(1)}, bf16[2048,16]{0,1:T(8,128)(2,1)}, u32[]{:S(2)}) copy-start(bf16[2048,16]{0,1:T(8,128)(2,1)} %param.6) | copy-start | bytes 196612
  0.0 4.7 %copy-start.1 = (bf16[512,2048]{1,0:T(8,128)(2,1)S(1)}, bf16[512,2048]{1,0:T(8,128)(2,1)}, u32[]{:S(2)}) copy-start(bf16[512,2048]{1,0:T(8,128)(2,1)} %param.4) | copy-start | bytes 6291460
  1.4 15.0 %collective-permute-start = (bf16[512,512]{1,0:T(8,128)(2,1)S(1)}, bf16[512,512]{1,0:T(8,128)(2,1)}, u32[]{:S(2)}, u32[]{:S(2)}) collective-permute-start(bf16[512,512]{1,0:T(8,128)(2,1)S(1)} %get-tuple-element.22), channel_id=1, source_target_pairs={{0,2},{1,3},{2,0},{3,1},{4,6},{5,7},{6,4},{7,5},{8,10},{9,11},{10,... | collective-permute-start | bytes 1572872 | tf_op jit(solution)/shard_map/ppermute | solution.py:491
  1.5 27.2 %collective-permute-start.3 = (bf16[512,512]{1,0:T(8,128)(2,1)S(1)}, bf16[512,512]{1,0:T(8,128)(2,1)}, u32[]{:S(2)}, u32[]{:S(2)}) collective-permute-start(bf16[512,512]{1,0:T(8,128)(2,1)S(1)} %get-tuple-element.21), channel_id=1, source_target_pairs={{0,6},{1,7},{2,4},{3,5},{4,2},{5,3},{6,0},{7,1},{8,14},{9,15},{10,... | collective-permute-start | bytes 1572872 | tf_op jit(solution)/shard_map/ppermute | solution.py:491
  6.1 28.4 %all-to-all-start = ((f32[32,1,512]{2,1,0:T(1,128)}), f32[32,1,512]{2,1,0:T(1,128)S(1)}, u32[]{:S(2)}, u32[]{:S(2)}) async-start(f32[32,1,512]{2,1,0:T(1,128)} %all_to_all.6), calls=%async_computation | async-start | bytes 131072 | tf_op jit(solution)/shard_map/all_to_all | solution.py:503
  17.5 17.0 %collective-permute-start.1 = (bf16[512,512]{1,0:T(8,128)(2,1)}, bf16[512,512]{1,0:T(8,128)(2,1)}, u32[]{:S(2)}, u32[]{:S(2)}) collective-permute-start(bf16[512,512]{1,0:T(8,128)(2,1)} %get-tuple-element.24.refs_0_), channel_id=1, source_target_pairs={{0,1},{1,0},{2,3},{3,2},{4,5},{5,4},{6,7},{7,6},{8,9},{9,8},{10,11... | collective-permute-start | bytes 1572872 | tf_op jit(solution)/shard_map/ppermute | solution.py:491
  28.7 26.3 %collective-permute-start.4 = (bf16[512,512]{1,0:T(8,128)(2,1)}, bf16[512,512]{1,0:T(8,128)(2,1)}, u32[]{:S(2)}, u32[]{:S(2)}) collective-permute-start(bf16[512,512]{1,0:T(8,128)(2,1)} %get-tuple-element.14), channel_id=1, source_target_pairs={{0,4},{1,5},{2,6},{3,7},{4,0},{5,1},{6,2},{7,3},{8,12},{9,13},{10,... | collective-permute-start | bytes 1572872 | tf_op jit(solution)/shard_map/ppermute | solution.py:491
  30.7 3.8 %collective-permute-start.2 = (bf16[512,512]{1,0:T(8,128)(2,1)}, bf16[512,512]{1,0:T(8,128)(2,1)}, u32[]{:S(2)}, u32[]{:S(2)}) collective-permute-start(bf16[512,512]{1,0:T(8,128)(2,1)} %collective-permute-done.refs_2_), channel_id=1, source_target_pairs={{0,1},{1,0},{2,3},{3,2},{4,5},{5,4},{6,7},{7,6},{8,9},{9,8},{10,11... | collective-permute-start | bytes 1572872 | tf_op jit(solution)/shard_map/ppermute | solution.py:491
  30.9 3.6 %collective-permute-start.5 = (bf16[512,512]{1,0:T(8,128)(2,1)}, bf16[512,512]{1,0:T(8,128)(2,1)}, u32[]{:S(2)}, u32[]{:S(2)}) collective-permute-start(bf16[512,512]{1,0:T(8,128)(2,1)} %collective-permute-done.3.refs_4_), channel_id=1, source_target_pairs={{0,1},{1,0},{2,3},{3,2},{4,5},{5,4},{6,7},{7,6},{8,9},{9,8},{10,11... | collective-permute-start | bytes 1572872 | tf_op jit(solution)/shard_map/ppermute | solution.py:491
  55.0 2.3 %collective-permute-start.6 = (bf16[512,512]{1,0:T(8,128)(2,1)}, bf16[512,512]{1,0:T(8,128)(2,1)}, u32[]{:S(2)}, u32[]{:S(2)}) collective-permute-start(bf16[512,512]{1,0:T(8,128)(2,1)} %collective-permute-done.4.refs_0_), channel_id=1, source_target_pairs={{0,1},{1,0},{2,3},{3,2},{4,5},{5,4},{6,7},{7,6},{8,9},{9,8},{10,11... | collective-permute-start | bytes 1572872 | tf_op jit(solution)/shard_map/ppermute | solution.py:491
  71.8 34.5 %collective-permute-start.7 = (bf16[512,512]{1,0:T(8,128)(2,1)S(1)}, bf16[512,512]{1,0:T(8,128)(2,1)S(1)}, u32[]{:S(2)}, u32[]{:S(2)}) collective-permute-start(bf16[512,512]{1,0:T(8,128)(2,1)S(1)} %get-tuple-element.18), channel_id=1, source_target_pairs={{0,4},{1,5},{2,6},{3,7},{4,0},{5,1},{6,2},{7,3},{8,12},{9,13},{10,... | collective-permute-start | bytes 1572872 | tf_op jit(solution)/shard_map/ppermute | solution.py:491
  71.9 47.8 %collective-permute-start.8 = (bf16[512,512]{1,0:T(8,128)(2,1)S(1)}, bf16[512,512]{1,0:T(8,128)(2,1)S(1)}, u32[]{:S(2)}, u32[]{:S(2)}) collective-permute-start(bf16[512,512]{1,0:T(8,128)(2,1)S(1)} %get-tuple-element.19), channel_id=1, source_target_pairs={{0,6},{1,7},{2,4},{3,5},{4,2},{5,3},{6,0},{7,1},{8,14},{9,15},{10,... | collective-permute-start | bytes 1572872 | tf_op jit(solution)/shard_map/ppermute | solution.py:491
  85.0 34.7 %collective-permute-start.9 = (bf16[512,512]{1,0:T(8,128)(2,1)S(1)}, bf16[512,512]{1,0:T(8,128)(2,1)S(1)}, u32[]{:S(2)}, u32[]{:S(2)}) collective-permute-start(bf16[512,512]{1,0:T(8,128)(2,1)S(1)} %get-tuple-element.20), channel_id=1, source_target_pairs={{0,2},{1,3},{2,0},{3,1},{4,6},{5,7},{6,4},{7,5},{8,10},{9,11},{10,... | collective-permute-start | bytes 1572872 | tf_op jit(solution)/shard_map/ppermute | solution.py:491
  119.7 1.3 %copy-start.2 = (bf16[512,2048]{1,0:T(8,128)(2,1)}, bf16[512,2048]{1,0:T(8,128)(2,1)S(1)}, u32[]{:S(2)}) copy-start(bf16[512,2048]{1,0:T(8,128)(2,1)S(1)} %constant_dynamic-update-slice_fusion.1) | copy-start | bytes 6291460

commit v4 on v3

--- a/solution.py
+++ b/solution.py
@@ -195,7 +195,7 @@
             put_query(matmul(x[source], m[:, :width]).astype(jnp.bfloat16))
 
 
-def deltas(at, rows, w, pool):
+def deltas(at, rows, w, pool, both=None):
     here = pl.ds(pl.multiple_of(rows * at, rows), rows)
     gate = matmul(pool[0, here], w[0])
     up = matmul(pool[0, here], w[1])
@@ -203,12 +203,27 @@
     sigma = logistic(gate)
     gated = gate * sigma
     pool[1, here] = (gated * up).astype(jnp.bfloat16)
-    pool[3, here] = (back * up * sigma * (1.0 + gate * (1.0 - sigma))).astype(jnp.bfloat16)
-    pool[4, here] = (back * gated).astype(jnp.bfloat16)
+    width = gate.shape[1]
+    gate_delta = (back * up * sigma * (1.0 + gate * (1.0 - sigma))).astype(jnp.bfloat16)
+    up_delta = (back * gated).astype(jnp.bfloat16)
+    if both is None:
+        pool[3, here] = gate_delta
+        pool[4, here] = up_delta
+    else:
+        both[here, :width] = gate_delta
+        both[here, width:] = up_delta
 
 
 def gradient(at, pool, rows):
     return matmul_tn(pool[at // 2, :rows], pool[jnp.where(at == 2, 2, 3 + at), :rows])
+
+
+def gradients(rows, pool, both, take):
+    width = pool.shape[2]
+    grads = matmul_tn(pool[0, :rows], both[:rows])
+    take(0, grads[:, :width])
+    take(1, grads[:, width:])
+    take(2, matmul_tn(pool[1, :rows], pool[2, :rows]))
 
 
 def renew(updated, initial):
@@ -220,7 +235,7 @@
 
 def begin_kernel(count, table, *refs):
     near, far, refs = refs[:count], refs[count : count + 2], refs[count + 2 :]
-    maps, rate, initial, state, x, m, w, fresh, kept, grads, pool, sems = refs
+    maps, rate, initial, state, x, m, w, fresh, kept, grads, pool, both, sems = refs
     rows = x.shape[1]
     updates = table[0] > 0
     fetch(maps, m, sems.at[count + 2])
@@ -239,11 +254,12 @@
             learn(at, x, at, m, rate[pl.ds(table[1 + at], 1)], pool, None, None)
 
         fetched(w, sems.at[count + 3])
-        pl.loop(0, count, unroll=True)(lambda at: deltas(at, rows, w, pool))
-
-        @pl.loop(0, 3)
-        def _(at):
-            fresh[at] = renew(w[at].astype(jnp.float32) + gradient(at, pool, count * rows), w[at])
+        pl.loop(0, count, unroll=True)(lambda at: deltas(at, rows, w, pool, both))
+
+        def take(at, grad):
+            fresh[at] = renew(w[at].astype(jnp.float32) + grad, w[at])
+
+        gradients(count * rows, pool, both, take)
 
     @pl.when(jnp.logical_not(updates))
     def _():
@@ -267,11 +283,12 @@
 
     send.append(pltpu.make_async_copy(kept, state.at[pl.ds(3, 5)], sems.at[1]))
     send[1].start()
-    pl.loop(0, 2, unroll=True)(lambda at: deltas(at, rows, fresh, pool))
-
-    @pl.loop(0, 3)
-    def _(at):
-        grads[at] = gradient(at, pool, 2 * rows).astype(jnp.bfloat16)
+    pl.loop(0, 2, unroll=True)(lambda at: deltas(at, rows, fresh, pool, both))
+
+    def take(at, grad):
+        grads[at] = grad.astype(jnp.bfloat16)
+
+    gradients(2 * rows, pool, both, take)
 
     send.append(pltpu.make_async_copy(grads, state.at[pl.ds(8, 3)], sems.at[2]))
     send[2].start()
@@ -299,7 +316,8 @@
                 bfloat(initial.shape),
                 bfloat((5, rows, width)),
                 bfloat(initial.shape),
-                bfloat((5, count * rows, width)),
+                bfloat((3, count * rows, width)),
+                bfloat((count * rows, 2 * width)),
                 pltpu.SemaphoreType.DMA((count + 4,)),
             ],
         ),
@@ -311,20 +329,22 @@
 
 
 def stage_kernel(counts, table, *refs):
-    count, befores, earliers, begun = counts
+    count, befores, begun = counts
     slots = count // 2 + begun
+    wanted = count // 2
     blocks, refs = refs[:count], refs[count:]
     before, refs = refs[:befores], refs[befores:]
-    earlier, refs = refs[:earliers], refs[earliers:]
+    state, refs = refs[0], refs[1:]
     (maps, rate, initial), refs = refs[:3], refs[3:]
-    results, new, refs = refs[:slots], refs[slots], refs[slots + 1 :]
+    results, new, refs = refs[:wanted], refs[wanted : wanted + begun], refs[wanted + begun :]
     x, m, w, start, fresh, k, v, q, attended, pool, out, sems, *grads = refs
     rows, width = x.shape[1:]
     part = rows // 2
     updates, answers, first, there = table[0] > 0, table[1] > 0, table[2], table[3] > 0
     at_maps, at_start, at_weights, at_new, at_held, at_grads = (sems.at[count + 1 + at] for at in range(6))
-    send_new = pltpu.make_async_copy(fresh, new, at_new)
-    send = [pltpu.make_async_copy(out.at[at], results[at], sems.at[count + 7 + at]) for at in range(slots)]
+    if begun:
+        send_new = pltpu.make_async_copy(fresh, new[0].at[pl.ds(11, 3)], at_new)
+    send = [pltpu.make_async_copy(out.at[at], results[at], sems.at[count + 7 + at]) for at in range(wanted)]
 
     def span(at, size=rows):
         return pl.ds(pl.multiple_of(at, part), size)
@@ -334,9 +354,9 @@
         column = lax.broadcasted_iota(jnp.int32, (part, rows + part), 1)
         band = (column > row) & (column <= row + rows)
 
-        @pl.loop(0, slots)
+        @pl.loop(0, wanted)
         def _(at):
-            @pl.loop(0, 2, unroll=True)
+            @pl.loop(0, 2, unroll=begun > 0)
             def _(half):
                 own = span(part * half, part)
                 base = rows * table[6 + 2 * at] + part * half
@@ -367,19 +387,16 @@
             fetch(blocks[at], x.at[at], sems.at[at])
         for at in range(befores):
             fetch(before[at], x.at[count], sems.at[count], there & (table[4] == at))
-        for at in range(earliers):
-            fetch(earlier[at].at[pl.ds(0, 3)], w, at_weights, table[5] == at)
+        fetch(state.at[pl.ds(table[5], 3)], w, at_weights)
         fetch(initial, start, at_start)
         if begun:
-            for at in range(2):
-                to = span(rows * (table[6 + count + at] + 1))
-                fetch(earlier[0].at[4 + at], k.at[to], at_held)
-                fetch(earlier[0].at[6 + at], v.at[to], at_held)
-            fetch(earlier[0].at[3], q.at[slots - 1], at_held)
-            fetch(earlier[0].at[pl.ds(8, 3)], grads[0], at_grads)
+            to = span(rows * (table[6 + count + 1] + 1))
+            fetch(state.at[5], k.at[to], at_held)
+            fetch(state.at[7], v.at[to], at_held)
+            fetch(state.at[pl.ds(8, 3)], grads[0], at_grads)
         fetched(m, at_maps)
 
-        @pl.loop(0, count, unroll=True)
+        @pl.loop(0, count, unroll=begun > 0)
         def _(at):
             to = span(rows * (table[6 + at] + 1))
 
@@ -407,13 +424,12 @@
         fetched(w, at_weights)
         fetched(start, at_start)
         if begun:
-            fetched(k.at[pl.ds(0, 4 * rows)], at_held)
-            fetched(q.at[0], at_held)
+            fetched(k.at[pl.ds(0, 2 * rows)], at_held)
             fetched(grads[0], at_grads)
 
         @pl.when(updates)
         def _():
-            pl.loop(0, count, unroll=True)(lambda at: deltas(at, rows, w, pool))
+            pl.loop(0, count, unroll=begun > 0)(lambda at: deltas(at, rows, w, pool))
 
             @pl.loop(0, 3)
             def _(at):
@@ -422,17 +438,19 @@
                     updated = updated + grads[0][at].astype(jnp.float32)
                 fresh[at] = renew(updated, start[at])
 
-            send_new.start()
+            if begun:
+                send_new.start()
 
         @pl.when(jnp.logical_not(updates))
         def _():
             fresh[...] = w[...]
 
         pl.when(answers)(answer)
-        pl.when(updates)(send_new.wait)
-
-
-def stage(table, blocks, before, earlier, maps, rate, initial, begun=False, scale=24):
+        if begun:
+            send_new.wait()
+
+
+def stage(table, blocks, before, state, maps, rate, initial, begun=False, scale=24):
     count, begun = len(blocks), int(begun)
     rows, width = blocks[0].shape
     matrices = initial.shape
@@ -440,14 +458,15 @@
     anywhere = pl.BlockSpec(memory_space=pl.ANY)
     slots = count // 2 + begun
     stretch = 2 * slots * rows
-    operands = [*blocks, *before, *earlier, maps]
+    wanted = count // 2
+    operands = [*blocks, *before, state, maps]
     return pl.pallas_call(
-        functools.partial(stage_kernel, (count, len(before), len(earlier), begun)),
+        functools.partial(stage_kernel, (count, len(before), begun)),
         grid_spec=pltpu.PrefetchScalarGridSpec(
             num_scalar_prefetch=1,
             grid=(),
             in_specs=[anywhere] * len(operands) + [pl.BlockSpec(memory_space=pltpu.VMEM), anywhere],
-            out_specs=[anywhere] * (slots + 1),
+            out_specs=[anywhere] * (wanted + begun),
             scratch_shapes=[
                 bfloat((count + 1, rows, width)),
                 bfloat(maps.shape),
@@ -456,20 +475,112 @@
                 bfloat(matrices),
                 bfloat((stretch + rows, width)),
                 bfloat((stretch + rows, width)),
-                bfloat((slots, rows, width)),
+                bfloat((wanted, rows, width)),
                 pltpu.VMEM((rows, width), jnp.float32),
                 bfloat((5, count * rows, width)),
-                bfloat((slots, rows, width)),
-                pltpu.SemaphoreType.DMA((count + 7 + slots,)),
+                bfloat((wanted, rows, width)),
+                pltpu.SemaphoreType.DMA((count + 7 + wanted,)),
             ]
             + [bfloat(matrices)] * begun,
         ),
-        out_shape=[jax.ShapeDtypeStruct((rows, width), jnp.bfloat16)] * slots
-        + [jax.ShapeDtypeStruct(matrices, jnp.bfloat16)],
+        out_shape=[jax.ShapeDtypeStruct((rows, width), jnp.bfloat16)] * wanted
+        + [jax.ShapeDtypeStruct(state.shape, state.dtype)] * begun,
+        input_output_aliases={1 + count + len(before): wanted} if begun else {},
         compiler_params=pltpu.CompilerParams(vmem_limit_bytes=VMEM_LIMIT),
         cost_estimate=pl.CostEstimate(flops=scale * stretch * width * width, bytes_accessed=scale * stretch * width, transcendentals=0),
         name="stage",
     )(table, *operands, rate, initial)
+
+
+def banded(queries, keys, values, floor):
+    part, window = queries.shape[0], keys.shape[0]
+    row = lax.broadcasted_iota(jnp.int32, (part, window), 0)
+    column = lax.broadcasted_iota(jnp.int32, (part, window), 1)
+    band = (column > row) & (column <= row + window - part) & (column >= floor)
+    scores = matmul_nt(queries, keys) * (queries.shape[1] ** -0.5)
+    scores = jnp.where(band, scores, -1e30)
+    raised = jnp.exp(scores - jnp.max(scores, axis=1, keepdims=True))
+    total = jnp.sum(raised, axis=1, keepdims=True)
+    return matmul(raised.astype(jnp.bfloat16), values) / total
+
+
+def finish_kernel(befores, table, *refs):
+    before, refs = refs[:befores], refs[befores:]
+    maps, state, result, x, m, w, q, k, v, attended, out, sems = refs
+    rows, width = x.shape
+    part = rows // 2
+    there = table[0] > 0
+    for at in range(befores):
+        fetch(before[at], x, sems.at[0], there & (table[1] == at))
+    fetch(maps, m, sems.at[1], there)
+    fetch(state.at[3], q, sems.at[2])
+    fetch(state.at[4], k.at[pl.ds(rows, rows)], sems.at[3])
+    fetch(state.at[6], v.at[pl.ds(rows, rows)], sems.at[4])
+    fetch(state.at[pl.ds(11, 3)], w, sems.at[5])
+
+    @pl.when(there)
+    def _():
+        fetched(x, sems.at[0])
+        fetched(m, sems.at[1])
+        k[:rows] = matmul(x[...], m[:, width : 2 * width]).astype(jnp.bfloat16)
+        v[:rows] = matmul(x[...], m[:, 2 * width :]).astype(jnp.bfloat16)
+
+    @pl.when(jnp.logical_not(there))
+    def _():
+        k[:rows] = jnp.zeros((rows, width), jnp.bfloat16)
+        v[:rows] = jnp.zeros((rows, width), jnp.bfloat16)
+
+    fetched(q, sems.at[2])
+    fetched(q, sems.at[3])
+    fetched(q, sems.at[4])
+
+    @pl.loop(0, 2)
+    def _(half):
+        first = part * half
+        window = pl.ds(first, rows + part)
+        floor = jnp.where(there, 0, rows - first)
+        attended[pl.ds(first, part)] = banded(q[pl.ds(first, part)], k[window], v[window], floor)
+
+    fetched(w, sems.at[5])
+    queries = unit_rows(q[...])
+    gate = matmul(queries, w[0])
+    up = matmul(queries, w[1])
+    inner = (gate * logistic(gate) * up).astype(jnp.bfloat16)
+    fast = matmul(inner, w[2]).astype(jnp.bfloat16).astype(jnp.float32)
+    out[...] = (attended[...] + fast).astype(jnp.bfloat16)
+    copy = pltpu.make_async_copy(out, result, sems.at[0])
+    copy.start()
+    copy.wait()
+
+
+def finish(table, before, maps, state):
+    rows, width = before[0].shape
+    anywhere = pl.BlockSpec(memory_space=pl.ANY)
+    bfloat = functools.partial(pltpu.VMEM, dtype=jnp.bfloat16)
+    return pl.pallas_call(
+        functools.partial(finish_kernel, len(before)),
+        grid_spec=pltpu.PrefetchScalarGridSpec(
+            num_scalar_prefetch=1,
+            grid=(),
+            in_specs=[anywhere] * (len(before) + 2),
+            out_specs=anywhere,
+            scratch_shapes=[
+                bfloat((rows, width)),
+                bfloat(maps.shape),
+                bfloat((3,) + state.shape[1:]),
+                bfloat((rows, width)),
+                bfloat((2 * rows, width)),
+                bfloat((2 * rows, width)),
+                pltpu.VMEM((rows, width), jnp.float32),
+                bfloat((rows, width)),
+                pltpu.SemaphoreType.DMA((6,)),
+            ],
+        ),
+        out_shape=jax.ShapeDtypeStruct((rows, width), jnp.bfloat16),
+        compiler_params=pltpu.CompilerParams(vmem_limit_bytes=VMEM_LIMIT),
+        cost_estimate=pl.CostEstimate(flops=1, bytes_accessed=1, transcendentals=0),
+        name="finish",
+    )(table, *before, maps, state)
 
 
 def after(array, *others):
@@ -518,10 +629,10 @@
     def opening(slot):
         return 2 * slots * ((chip ^ slot) // slots)
 
-    def table(slots_in, updates, answers, earlier):
+    def table(slots_in, updates, answers, weights_at):
         first = opening(slots_in[0])
         before = (chip ^ (slots - 1)) % slots
-        flags = [updates, answers, first, (first > 0) & (core == 0), before, earlier]
+        flags = [updates, answers, first, (first > 0) & (core == 0), before, weights_at]
         return integers(flags + [place for slot in slots_in for place in places(slot)])
 
     near_slots, far_slots = range(slots), range(slots, chips)
@@ -536,16 +647,21 @@
         same[slot] = after(same[slot], state)
         other[slot] = swap(same[slot], 1)
         far_blocks += [same[slot], other[slot]]
-    *far_results, far_new = stage(
-        table(far_slots, True, True, 0), far_blocks, near_others, [state], begun=True, **shared
-    )
-    *near_results, _ = stage(
-        table(near_slots, 1 - is_first, True, 1 - is_first), near_blocks,
-        [other[slot] for slot in far_slots], [state, far_new], **shared
-    )
-    results = near_results + far_results
+    *far_results, state = stage(
+        table(far_slots, True, True, 0), far_blocks, near_others, state, begun=True, **shared
+    )
+    near_results = stage(
+        table(near_slots, 1 - is_first, True, 11 * (1 - is_first)), near_blocks,
+        [other[slot] for slot in far_slots], state, scale=0, **shared
+    )
+    at = chip ^ last
+    place = jnp.where(core == 1, at, at - 1)
+    last_result = finish(
+        integers([place >= 0, chip ^ jnp.maximum(place, 0)]), [other[slot] for slot in range(chips)], maps, state
+    )
+    results = [*near_results, *far_results, last_result]
     combined = jnp.zeros_like(tokens)
-    for slot in (0, *far_slots, *range(1, slots)):
+    for slot in (*far_slots[:-1], 0, last, *range(1, slots)):
         result = swap(results[slot], 2 * slot) if slot else results[slot]
         combined = lax.dynamic_update_slice_in_dim(combined, result, (chip ^ slot) * width, 1)
     return combined

time: 123 us -> 120 us (0.976); the launches traced: 122 us -> 120 us
  waiting for transfers between devices: 51.1 us -> 43.9 us
  Pallas kernels: 45.4 us -> 49.3 us
  local copies, waits for them, and re-layouts: 9.11 us -> 11.2 us
    ppermute x10, waiting for transfers between devices: 51.1 us -> 43.8 us  [swap(): return lax.ppermute(block, 'tok', [(i, i ^ bits) for i in range(groups)])]
    pallas_call x2 -> x3, Pallas kernels: 24.9 us -> 29.9 us  [the longest x2 23.8 us: stage(): pl.pallas_call(functools.partial(stage_kernel, (count, len(before), begun...]
    dynamic_update_slice x4, local copies, waits for them, and re-layouts: 1 us -> 3.1 us  [head_body(): lax.dynamic_update_slice_in_dim(combined, result, (chip ^ slot) * width, 1)]
  transfers between devices with their start and end apart: 11 -> 11, of which waited for: 5 -> 5; matrix products, arithmetic and copies ran while one was open for 5% -> 6% of each run, Pallas kernels for 25% -> 31%
where the time goes in v4:
time: 120 us
  Pallas kernels  49.3 us (41%)
  waiting for transfers between devices  43.9 us (37%)
  starting transfers between devices  14.7 us (12%)
  local copies, waits for them, and re-layouts  11.2 us (9%)
    ppermute x10, waiting for transfers between devices, swap(): return lax.ppermute(block, 'tok', [(i, i ^ bits) for i in range(groups)])  43.8 us
    pallas_call x2, Pallas kernels, stage(): pl.pallas_call(functools.partial(stage_kernel, (count, len(before), begun...  23.8 us
    pallas_call x1, Pallas kernels, begin(): pl.pallas_call(functools.partial(begin_kernel, count), grid_spec=pltpu.Pr...  19.4 us
    ppermute x10, starting transfers between devices, swap(): return lax.ppermute(block, 'tok', [(i, i ^ bits) for i in range(groups)])  10 us
    pallas_call x1, Pallas kernels, finish(): pl.pallas_call(functools.partial(finish_kernel, len(before)), grid_spec=p...  6.04 us
    all_to_all x1, starting transfers between devices, head_body(): lax.all_to_all(jnp.repeat(terms, 2, axis=0), ('head', 'tok'), 0, 0, tiled...  4.69 us
    dynamic_update_slice x4, local copies, waits for them, and re-layouts, head_body(): lax.dynamic_update_slice_in_dim(combined, result, (chip ^ slot) * width, 1)  3.1 us
    dynamic_slice x2, local copies, waits for them, and re-layouts, piece(): return lax.dynamic_slice_in_dim(source, (index ^ slot) * width, width, 1)  2.52 us
  transfers between devices with their start and end apart: 11, of which 5 were waited for; matrix products, arithmetic and copies ran while one was open for 6% of the time, Pallas kernels for 31%

profile of v4, /device:TPU:8, one launch (start us, length us, event | category | flops | bytes accessed | tf_op | source)
XLA Modules:
  0.0 120.2 jit_solution(9163968264278692083)
XLA Ops:
  0.0 1.4 %constant_dynamic-slice_fusion.1 = (bf16[512,512]{1,0:T(8,128)(2,1)S(1)}, bf16[512,512]{1,0:T(8,128)(2,1)S(1)}) fusion(bf16[512,2048]{1,0:T(8,128)(2,1)} %param.4, s32[]{:T(128)S(6)} %select_n.104, s32[]{:T(128)S(6)} %select_n.102), kind=kLoop, calls=%fused_computation.12 | loop fusion | bytes 2097160 | tf_op jit(solution)/shard_map/dynamic_slice | solution.py:605
  1.5 3.1 %collective-permute-start.1 = (bf16[512,512]{1,0:T(8,128)(2,1)S(1)}, bf16[512,512]{1,0:T(8,128)(2,1)}, u32[]{:S(2)}, u32[]{:S(2)}) collective-permute-start(bf16[512,512]{1,0:T(8,128)(2,1)S(1)} %get-tuple-element.21), channel_id=1, source_target_pairs={{0,6},{1,7},{2,4},{3,5},{4,2},{5,3},{6,0},{7,1},{8,14},{9,15},{10,... | collective-permute-start | bytes 1572872 | tf_op jit(solution)/shard_map/ppermute | solution.py:602
  5.3 0.7 all_to_all.6
  6.1 4.7 %all-to-all-start = ((f32[32,1,512]{2,1,0:T(1,128)}), f32[32,1,512]{2,1,0:T(1,128)S(1)}, u32[]{:S(2)}, u32[]{:S(2)}) async-start(f32[32,1,512]{2,1,0:T(1,128)} %all_to_all.6), calls=%async_computation | async-start | bytes 131072 | tf_op jit(solution)/shard_map/all_to_all | solution.py:614
  10.8 5.6 %collective-permute-done.refs_2_ = bf16[512,512]{1,0:T(8,128)(2,1)} collective-permute-done((bf16[512,512]{1,0:T(8,128)(2,1)S(1)}, bf16[512,512]{1,0:T(8,128)(2,1)}, u32[]{:S(2)}, u32[]{:S(2)}) %collective-permute-start) | collective-permute-done | bytes 524320 | tf_op jit(solution)/shard_map/ppermute | solution.py:602
  16.4 1.1 constant_dynamic-slice_fusion
  17.5 11.2 %collective-permute-done.1.refs_4_ = bf16[512,512]{1,0:T(8,128)(2,1)} collective-permute-done((bf16[512,512]{1,0:T(8,128)(2,1)S(1)}, bf16[512,512]{1,0:T(8,128)(2,1)}, u32[]{:S(2)}, u32[]{:S(2)}) %collective-permute-start.1) | collective-permute-done | bytes 524320 | tf_op jit(solution)/shard_map/ppermute | solution.py:602
  28.7 2.0 %collective-permute-start.2 = (bf16[512,512]{1,0:T(8,128)(2,1)}, bf16[512,512]{1,0:T(8,128)(2,1)}, u32[]{:S(2)}, u32[]{:S(2)}) collective-permute-start(bf16[512,512]{1,0:T(8,128)(2,1)} %get-tuple-element.13), channel_id=1, source_target_pairs={{0,4},{1,5},{2,6},{3,7},{4,0},{5,1},{6,2},{7,3},{8,12},{9,13},{10,... | collective-permute-start | bytes 1572872 | tf_op jit(solution)/shard_map/ppermute | solution.py:602
  31.2 1.5 %dynamic-slice_bitcast_fusion.1.refs_6_.refs_5_.refs_7_.refs_4_ = bf16[512,1536]{1,0:T(8,128)(2,1)S(1)} fusion(bf16[4,512,1536]{2,1,0:T(8,128)(2,1)} %param.5, s32[]{:T(128)S(6)} %select_n.110), kind=kLoop, calls=%fused_computation.1 | loop fusion | bytes 3145732 | tf_op jit(solution)/shard_map/jit(dynamic_index_in_dim)/squeeze | solution.py:607
  33.0 1.5 %dynamic-slice_bitcast_fusion.refs_8_.refs_7_.refs_9_ = bf16[3,512,512]{2,1,0:T(8,128)(2,1)S(1)} fusion(bf16[4,3,512,512]{3,2,1,0:T(8,128)(2,1)} %param.7, s32[]{:T(128)S(6)} %select_n.110), kind=kLoop, calls=%fused_computation | loop fusion | bytes 3145732 | tf_op jit(solution)/shard_map/jit(dynamic_index_in_dim)/squeeze | solution.py:608
  34.6 19.4 %begin.1.refs_4_ = bf16[64,512,512]{2,1,0:T(8,128)(2,1)} custom-call(s32[7]{0:T(128)S(1)} %stack.110.table, bf16[512,512]{1,0:T(8,128)(2,1)} %get-tuple-element.19.refs_0_, bf16[512,512]{1,0:T(8,128)(2,1)} %collective-permute-done.3.refs_1_.refs_2_.refs_0_, bf16[512,512]{1,0:T(8,128)(2,1)} %collective-permute-done.refs_2_, ...), custom_call_target="tpu_custom_call" | custom-call | flops 1 | bytes 1 | tf_op jit(solution)/shard_map/begin/pallas_call | solution.py:305
  54.4 1.9 %collective-permute-done.6.refs_1_.refs_4_.refs_2_ = bf16[512,512]{1,0:T(8,128)(2,1)} collective-permute-done((bf16[512,512]{1,0:T(8,128)(2,1)}, bf16[512,512]{1,0:T(8,128)(2,1)}, u32[]{:S(2)}, u32[]{:S(2)}) %collective-permute-start.6) | collective-permute-done | bytes 524320 | tf_op jit(solution)/shard_map/ppermute | solution.py:602
  56.3 12.5 %stage.2 = (bf16[512,512]{1,0:T(8,128)(2,1)}, bf16[64,512,512]{2,1,0:T(8,128)(2,1)}) custom-call(s32[10]{0:T(128)S(1)} %stack.102.table, bf16[512,512]{1,0:T(8,128)(2,1)} %collective-permute-done.2.refs_0_, bf16[512,512]{1,0:T(8,128)(2,1)} %collective-permute-done.6.refs_1_.refs_4_.refs_2_, ...), custom_call_target="tpu_custom_call", output_to_operand_aliasing={{1}: (5, {})} | custom-call | flops 12884901888 | bytes 25165824 | tf_op jit(solution)/shard_map/stage/pallas_call | solution.py:463
  68.9 0.8 collective-permute-start.7
  69.7 6.0 %finish.1 = bf16[512,512]{1,0:T(8,128)(2,1)} custom-call(s32[2]{0:T(128)S(1)} %pad_add_fusion.table, bf16[512,512]{1,0:T(8,128)(2,1)} %collective-permute-done.3.refs_1_.refs_2_.refs_0_, bf16[512,512]{1,0:T(8,128)(2,1)} %collective-permute-done.4.refs_3_.refs_1_, bf16[512,512]{1,0:T(8,128)(2,1)} %collective-permute-done.6.refs_1_.refs_4_.refs_2_, ...), custom_call_target="tpu_custom_call" | custom-call | flops 1 | bytes 1 | tf_op jit(solution)/shard_map/finish/pallas_call | solution.py:560
  75.8 2.0 %collective-permute-start.8 = (bf16[512,512]{1,0:T(8,128)(2,1)}, bf16[512,512]{1,0:T(8,128)(2,1)}, u32[]{:S(2)}, u32[]{:S(2)}) collective-permute-start(bf16[512,512]{1,0:T(8,128)(2,1)} %finish.1), channel_id=1, source_target_pairs={{0,6},{1,7},{2,4},{3,5},{4,2},{5,3},{6,0},{7,1},{8,14},{9,15},{10,... | collective-permute-start | bytes 1572872 | tf_op jit(solution)/shard_map/ppermute | solution.py:602
  77.9 11.3 %stage.3 = (bf16[512,512]{1,0:T(8,128)(2,1)S(1)}, bf16[512,512]{1,0:T(8,128)(2,1)S(1)}) custom-call(s32[10]{0:T(128)S(1)} %stack.120.table, bf16[512,512]{1,0:T(8,128)(2,1)} %get-tuple-element.19.refs_0_, bf16[512,512]{1,0:T(8,128)(2,1)} %collective-permute-done.3.refs_1_.refs_2_.refs_0_, bf16[512,512]{1,0:T(8,128)(2,1)} %collective-permute-done.refs_2_, ...), custom_call_target="tpu_custom_call" | custom-call | tf_op jit(solution)/shard_map/stage/pallas_call | solution.py:463
  89.2 1.2 collective-permute-start.9
  90.4 13.2 %collective-permute-done.7 = bf16[512,512]{1,0:T(8,128)(2,1)} collective-permute-done((bf16[512,512]{1,0:T(8,128)(2,1)}, bf16[512,512]{1,0:T(8,128)(2,1)}, u32[]{:S(2)}, u32[]{:S(2)}) %collective-permute-start.7) | collective-permute-done | bytes 524320 | tf_op jit(solution)/shard_map/ppermute | solution.py:602
  103.8 1.1 constant_dynamic-update-slice_fusion.3
  105.0 11.9 %collective-permute-done.8 = bf16[512,512]{1,0:T(8,128)(2,1)} collective-permute-done((bf16[512,512]{1,0:T(8,128)(2,1)}, bf16[512,512]{1,0:T(8,128)(2,1)}, u32[]{:S(2)}, u32[]{:S(2)}) %collective-permute-start.8) | collective-permute-done | bytes 524320 | tf_op jit(solution)/shard_map/ppermute | solution.py:602
  116.9 1.1 constant_dynamic-update-slice_fusion.1
  118.0 1.3 %copy-done.2 = bf16[512,2048]{1,0:T(8,128)(2,1)} copy-done((bf16[512,2048]{1,0:T(8,128)(2,1)}, bf16[512,2048]{1,0:T(8,128)(2,1)S(1)}, u32[]{:S(2)}) %copy-start.2) | copy-done | bytes 2097176
  119.3 0.8 constant_dynamic-update-slice_fusion
  (27 shorter events, 2.2 us)
Async XLA Ops:
  0.0 4.7 %copy-start = (bf16[2048,16]{0,1:T(8,128)(2,1)S(1)}, bf16[2048,16]{0,1:T(8,128)(2,1)}, u32[]{:S(2)}) copy-start(bf16[2048,16]{0,1:T(8,128)(2,1)} %param.6) | copy-start | bytes 196612
  0.0 4.7 %copy-start.1 = (bf16[512,2048]{1,0:T(8,128)(2,1)S(1)}, bf16[512,2048]{1,0:T(8,128)(2,1)}, u32[]{:S(2)}) copy-start(bf16[512,2048]{1,0:T(8,128)(2,1)} %param.4) | copy-start | bytes 6291460
  1.4 15.0 %collective-permute-start = (bf16[512,512]{1,0:T(8,128)(2,1)S(1)}, bf16[512,512]{1,0:T(8,128)(2,1)}, u32[]{:S(2)}, u32[]{:S(2)}) collective-permute-start(bf16[512,512]{1,0:T(8,128)(2,1)S(1)} %get-tuple-element.22), channel_id=1, source_target_pairs={{0,2},{1,3},{2,0},{3,1},{4,6},{5,7},{6,4},{7,5},{8,10},{9,11},{10,... | collective-permute-start | bytes 1572872 | tf_op jit(solution)/shard_map/ppermute | solution.py:602
  1.5 27.2 %collective-permute-start.1 = (bf16[512,512]{1,0:T(8,128)(2,1)S(1)}, bf16[512,512]{1,0:T(8,128)(2,1)}, u32[]{:S(2)}, u32[]{:S(2)}) collective-permute-start(bf16[512,512]{1,0:T(8,128)(2,1)S(1)} %get-tuple-element.21), channel_id=1, source_target_pairs={{0,6},{1,7},{2,4},{3,5},{4,2},{5,3},{6,0},{7,1},{8,14},{9,15},{10,... | collective-permute-start | bytes 1572872 | tf_op jit(solution)/shard_map/ppermute | solution.py:602
  6.1 28.4 %all-to-all-start = ((f32[32,1,512]{2,1,0:T(1,128)}), f32[32,1,512]{2,1,0:T(1,128)S(1)}, u32[]{:S(2)}, u32[]{:S(2)}) async-start(f32[32,1,512]{2,1,0:T(1,128)} %all_to_all.6), calls=%async_computation | async-start | bytes 131072 | tf_op jit(solution)/shard_map/all_to_all | solution.py:614
  17.5 17.0 %collective-permute-start.3 = (bf16[512,512]{1,0:T(8,128)(2,1)}, bf16[512,512]{1,0:T(8,128)(2,1)}, u32[]{:S(2)}, u32[]{:S(2)}) collective-permute-start(bf16[512,512]{1,0:T(8,128)(2,1)} %get-tuple-element.19.refs_0_), channel_id=1, source_target_pairs={{0,1},{1,0},{2,3},{3,2},{4,5},{5,4},{6,7},{7,6},{8,9},{9,8},{10,11... | collective-permute-start | bytes 1572872 | tf_op jit(solution)/shard_map/ppermute | solution.py:602
  28.7 25.3 %collective-permute-start.2 = (bf16[512,512]{1,0:T(8,128)(2,1)}, bf16[512,512]{1,0:T(8,128)(2,1)}, u32[]{:S(2)}, u32[]{:S(2)}) collective-permute-start(bf16[512,512]{1,0:T(8,128)(2,1)} %get-tuple-element.13), channel_id=1, source_target_pairs={{0,4},{1,5},{2,6},{3,7},{4,0},{5,1},{6,2},{7,3},{8,12},{9,13},{10,... | collective-permute-start | bytes 1572872 | tf_op jit(solution)/shard_map/ppermute | solution.py:602
  30.7 3.8 %collective-permute-start.4 = (bf16[512,512]{1,0:T(8,128)(2,1)}, bf16[512,512]{1,0:T(8,128)(2,1)}, u32[]{:S(2)}, u32[]{:S(2)}) collective-permute-start(bf16[512,512]{1,0:T(8,128)(2,1)} %collective-permute-done.refs_2_), channel_id=1, source_target_pairs={{0,1},{1,0},{2,3},{3,2},{4,5},{5,4},{6,7},{7,6},{8,9},{9,8},{10,11... | collective-permute-start | bytes 1572872 | tf_op jit(solution)/shard_map/ppermute | solution.py:602
  30.9 3.6 %collective-permute-start.5 = (bf16[512,512]{1,0:T(8,128)(2,1)}, bf16[512,512]{1,0:T(8,128)(2,1)}, u32[]{:S(2)}, u32[]{:S(2)}) collective-permute-start(bf16[512,512]{1,0:T(8,128)(2,1)} %collective-permute-done.1.refs_4_), channel_id=1, source_target_pairs={{0,1},{1,0},{2,3},{3,2},{4,5},{5,4},{6,7},{7,6},{8,9},{9,8},{10,11... | collective-permute-start | bytes 1572872 | tf_op jit(solution)/shard_map/ppermute | solution.py:602
  54.0 2.3 %collective-permute-start.6 = (bf16[512,512]{1,0:T(8,128)(2,1)}, bf16[512,512]{1,0:T(8,128)(2,1)}, u32[]{:S(2)}, u32[]{:S(2)}) collective-permute-start(bf16[512,512]{1,0:T(8,128)(2,1)} %collective-permute-done.2.refs_0_), channel_id=1, source_target_pairs={{0,1},{1,0},{2,3},{3,2},{4,5},{5,4},{6,7},{7,6},{8,9},{9,8},{10,11... | collective-permute-start | bytes 1572872 | tf_op jit(solution)/shard_map/ppermute | solution.py:602
  68.9 34.7 %collective-permute-start.7 = (bf16[512,512]{1,0:T(8,128)(2,1)}, bf16[512,512]{1,0:T(8,128)(2,1)}, u32[]{:S(2)}, u32[]{:S(2)}) collective-permute-start(bf16[512,512]{1,0:T(8,128)(2,1)} %get-tuple-element.15), channel_id=1, source_target_pairs={{0,4},{1,5},{2,6},{3,7},{4,0},{5,1},{6,2},{7,3},{8,12},{9,13},{10,... | collective-permute-start | bytes 1572872 | tf_op jit(solution)/shard_map/ppermute | solution.py:602
  75.8 41.1 %collective-permute-start.8 = (bf16[512,512]{1,0:T(8,128)(2,1)}, bf16[512,512]{1,0:T(8,128)(2,1)}, u32[]{:S(2)}, u32[]{:S(2)}) collective-permute-start(bf16[512,512]{1,0:T(8,128)(2,1)} %finish.1), channel_id=1, source_target_pairs={{0,6},{1,7},{2,4},{3,5},{4,2},{5,3},{6,0},{7,1},{8,14},{9,15},{10,... | collective-permute-start | bytes 1572872 | tf_op jit(solution)/shard_map/ppermute | solution.py:602
  89.2 28.9 %collective-permute-start.9 = (bf16[512,512]{1,0:T(8,128)(2,1)S(1)}, bf16[512,512]{1,0:T(8,128)(2,1)S(1)}, u32[]{:S(2)}, u32[]{:S(2)}) collective-permute-start(bf16[512,512]{1,0:T(8,128)(2,1)S(1)} %get-tuple-element.18), channel_id=1, source_target_pairs={{0,2},{1,3},{2,0},{3,1},{4,6},{5,7},{6,4},{7,5},{8,10},{9,11},{10,... | collective-permute-start | bytes 1572872 | tf_op jit(solution)/shard_map/ppermute | solution.py:602
  118.0 1.3 %copy-start.2 = (bf16[512,2048]{1,0:T(8,128)(2,1)}, bf16[512,2048]{1,0:T(8,128)(2,1)S(1)}, u32[]{:S(2)}) copy-start(bf16[512,2048]{1,0:T(8,128)(2,1)S(1)} %constant_dynamic-update-slice_fusion.1) | copy-start | bytes 6291460

commit v5 on v4

--- a/solution.py
+++ b/solution.py
@@ -197,15 +197,15 @@
 
 def deltas(at, rows, w, pool, both=None):
     here = pl.ds(pl.multiple_of(rows * at, rows), rows)
-    gate = matmul(pool[0, here], w[0])
-    up = matmul(pool[0, here], w[1])
-    back = matmul_nt(pool[2, here], w[2])
+    gate = matmul(pool[0, here], w[0]).astype(jnp.bfloat16)
+    up = matmul(pool[0, here], w[1]).astype(jnp.bfloat16)
+    back = matmul_nt(pool[2, here], w[2]).astype(jnp.bfloat16)
     sigma = logistic(gate)
     gated = gate * sigma
-    pool[1, here] = (gated * up).astype(jnp.bfloat16)
+    pool[1, here] = gated * up
     width = gate.shape[1]
-    gate_delta = (back * up * sigma * (1.0 + gate * (1.0 - sigma))).astype(jnp.bfloat16)
-    up_delta = (back * gated).astype(jnp.bfloat16)
+    gate_delta = back * up * sigma * (1 + gate * (1 - sigma))
+    up_delta = back * gated
     if both is None:
         pool[3, here] = gate_delta
         pool[4, here] = up_delta
@@ -616,7 +616,7 @@
     rate = (rate_base * jax.nn.softplus(logits)).astype(jnp.bfloat16).astype(jnp.float32)
     source = after(tokens, *(same[slot] for slot in range(1, slots)))
     for slot in range(slots, last):
-        same[slot] = swap(after(piece(slot, source, chip), same[last]), 2 * slot)
+        same[slot] = swap(piece(slot, source, chip), 2 * slot)
     same[0] = piece(0, source, chip)
     other = {slot: swap(same[slot], 1) for slot in range(slots)}
 

time: 120 us -> 118 us (0.983)
  waiting for transfers between devices: 43.9 us -> 31.8 us
  starting transfers between devices: 14.7 us -> 25.9 us
    ppermute x10, waiting for transfers between devices: 43.8 us -> 31.8 us  [swap(): return lax.ppermute(block, 'tok', [(i, i ^ bits) for i in range(groups)])]
    ppermute x10, starting transfers between devices: 10 us -> 21.2 us  [swap(): return lax.ppermute(block, 'tok', [(i, i ^ bits) for i in range(groups)])]
  transfers between devices with their start and end apart: 11 -> 11, of which waited for: 5 -> 4; matrix products, arithmetic and copies ran while one was open for 6% -> 7% of each run, Pallas kernels for 31% -> 30%
where the time goes in v5:
time: 118 us
  Pallas kernels  48.1 us (41%)
  waiting for transfers between devices  31.8 us (27%)
  starting transfers between devices  25.9 us (22%)
  local copies, waits for them, and re-layouts  11.2 us (9%)
    ppermute x10, waiting for transfers between devices, swap(): return lax.ppermute(block, 'tok', [(i, i ^ bits) for i in range(groups)])  31.8 us
    pallas_call x2, Pallas kernels, stage(): pl.pallas_call(functools.partial(stage_kernel, (count, len(before), begun...  23.6 us
    ppermute x10, starting transfers between devices, swap(): return lax.ppermute(block, 'tok', [(i, i ^ bits) for i in range(groups)])  21.2 us
    pallas_call x1, Pallas kernels, begin(): pl.pallas_call(functools.partial(begin_kernel, count), grid_spec=pltpu.Pr...  18.5 us
    pallas_call x1, Pallas kernels, finish(): pl.pallas_call(functools.partial(finish_kernel, len(before)), grid_spec=p...  6.04 us
    all_to_all x1, starting transfers between devices, head_body(): lax.all_to_all(jnp.repeat(terms, 2, axis=0), ('head', 'tok'), 0, 0, tiled...  4.69 us
    dynamic_update_slice x4, local copies, waits for them, and re-layouts, head_body(): lax.dynamic_update_slice_in_dim(combined, result, (chip ^ slot) * width, 1)  3.1 us
    dynamic_slice x2, local copies, waits for them, and re-layouts, piece(): return lax.dynamic_slice_in_dim(source, (index ^ slot) * width, width, 1)  2.52 us
  transfers between devices with their start and end apart: 11, of which 4 were waited for; matrix products, arithmetic and copies ran while one was open for 7% of the time, Pallas kernels for 30%

profile of v5, /device:TPU:8, one launch (start us, length us, event | category | flops | bytes accessed | tf_op | source)
XLA Modules:
  0.0 118.0 jit_solution(17555632689144687125)
XLA Ops:
  0.0 1.4 %constant_dynamic-slice_fusion = (bf16[512,512]{1,0:T(8,128)(2,1)S(1)}, bf16[512,512]{1,0:T(8,128)(2,1)S(1)}) fusion(bf16[512,2048]{1,0:T(8,128)(2,1)} %param.4, s32[]{:T(128)S(6)} %select_n.109, s32[]{:T(128)S(6)} %select_n.102), kind=kLoop, calls=%fused_computation.11 | loop fusion | bytes 2097160 | tf_op jit(solution)/shard_map/dynamic_slice | solution.py:605
  1.5 3.1 %collective-permute-start.4 = (bf16[512,512]{1,0:T(8,128)(2,1)S(1)}, bf16[512,512]{1,0:T(8,128)(2,1)}, u32[]{:S(2)}, u32[]{:S(2)}) collective-permute-start(bf16[512,512]{1,0:T(8,128)(2,1)S(1)} %get-tuple-element.17), channel_id=1, source_target_pairs={{0,6},{1,7},{2,4},{3,5},{4,2},{5,3},{6,0},{7,1},{8,14},{9,15},{10,... | collective-permute-start | bytes 1572872 | tf_op jit(solution)/shard_map/ppermute | solution.py:602
  4.7 0.6 fusion.3
  5.3 0.7 all_to_all.6
  6.1 4.7 %all-to-all-start = ((f32[32,1,512]{2,1,0:T(1,128)}), f32[32,1,512]{2,1,0:T(1,128)S(1)}, u32[]{:S(2)}, u32[]{:S(2)}) async-start(f32[32,1,512]{2,1,0:T(1,128)} %all_to_all.6), calls=%async_computation | async-start | bytes 131072 | tf_op jit(solution)/shard_map/all_to_all | solution.py:614
  10.8 5.6 %collective-permute-done.refs_2_ = bf16[512,512]{1,0:T(8,128)(2,1)} collective-permute-done((bf16[512,512]{1,0:T(8,128)(2,1)S(1)}, bf16[512,512]{1,0:T(8,128)(2,1)}, u32[]{:S(2)}, u32[]{:S(2)}) %collective-permute-start) | collective-permute-done | bytes 524320 | tf_op jit(solution)/shard_map/ppermute | solution.py:602
  16.4 1.1 constant_dynamic-slice_fusion.1
  17.5 13.2 %collective-permute-start.1 = (bf16[512,512]{1,0:T(8,128)(2,1)}, bf16[512,512]{1,0:T(8,128)(2,1)}, u32[]{:S(2)}, u32[]{:S(2)}) collective-permute-start(bf16[512,512]{1,0:T(8,128)(2,1)} %get-tuple-element.20), channel_id=1, source_target_pairs={{0,4},{1,5},{2,6},{3,7},{4,0},{5,1},{6,2},{7,3},{8,12},{9,13},{10,... | collective-permute-start | bytes 1572872 | tf_op jit(solution)/shard_map/ppermute | solution.py:602
  31.2 1.5 %dynamic-slice_bitcast_fusion.1.refs_6_.refs_5_.refs_7_.refs_4_ = bf16[512,1536]{1,0:T(8,128)(2,1)S(1)} fusion(bf16[4,512,1536]{2,1,0:T(8,128)(2,1)} %param.5, s32[]{:T(128)S(6)} %select_n.110), kind=kLoop, calls=%fused_computation.1 | loop fusion | bytes 3145732 | tf_op jit(solution)/shard_map/jit(dynamic_index_in_dim)/squeeze | solution.py:607
  33.0 1.5 %dynamic-slice_bitcast_fusion.refs_8_.refs_7_.refs_9_ = bf16[3,512,512]{2,1,0:T(8,128)(2,1)S(1)} fusion(bf16[4,3,512,512]{3,2,1,0:T(8,128)(2,1)} %param.7, s32[]{:T(128)S(6)} %select_n.110), kind=kLoop, calls=%fused_computation | loop fusion | bytes 3145732 | tf_op jit(solution)/shard_map/jit(dynamic_index_in_dim)/squeeze | solution.py:608
  34.6 18.5 %begin.1.refs_4_ = bf16[64,512,512]{2,1,0:T(8,128)(2,1)} custom-call(s32[7]{0:T(128)S(1)} %stack.110.table, bf16[512,512]{1,0:T(8,128)(2,1)} %get-tuple-element.19.refs_0_, bf16[512,512]{1,0:T(8,128)(2,1)} %collective-permute-done.2.refs_1_.refs_2_.refs_0_, bf16[512,512]{1,0:T(8,128)(2,1)} %collective-permute-done.refs_2_, ...), custom_call_target="tpu_custom_call" | custom-call | flops 1 | bytes 1 | tf_op jit(solution)/shard_map/begin/pallas_call | solution.py:305
  53.0 0.3 collective-permute-start.6
  53.4 1.9 %collective-permute-done.6.refs_1_.refs_4_.refs_2_ = bf16[512,512]{1,0:T(8,128)(2,1)} collective-permute-done((bf16[512,512]{1,0:T(8,128)(2,1)}, bf16[512,512]{1,0:T(8,128)(2,1)}, u32[]{:S(2)}, u32[]{:S(2)}) %collective-permute-start.6) | collective-permute-done | bytes 524320 | tf_op jit(solution)/shard_map/ppermute | solution.py:602
  55.4 12.3 %stage.2 = (bf16[512,512]{1,0:T(8,128)(2,1)}, bf16[64,512,512]{2,1,0:T(8,128)(2,1)}) custom-call(s32[10]{0:T(128)S(1)} %stack.102.table, bf16[512,512]{1,0:T(8,128)(2,1)} %collective-permute-done.1.refs_0_, bf16[512,512]{1,0:T(8,128)(2,1)} %collective-permute-done.6.refs_1_.refs_4_.refs_2_, ...), custom_call_target="tpu_custom_call", output_to_operand_aliasing={{1}: (5, {})} | custom-call | flops 12884901888 | bytes 25165824 | tf_op jit(solution)/shard_map/stage/pallas_call | solution.py:463
  67.6 1.8 %collective-permute-start.7 = (bf16[512,512]{1,0:T(8,128)(2,1)}, bf16[512,512]{1,0:T(8,128)(2,1)}, u32[]{:S(2)}, u32[]{:S(2)}) collective-permute-start(bf16[512,512]{1,0:T(8,128)(2,1)} %get-tuple-element.13), channel_id=1, source_target_pairs={{0,4},{1,5},{2,6},{3,7},{4,0},{5,1},{6,2},{7,3},{8,12},{9,13},{10,... | collective-permute-start | bytes 1572872 | tf_op jit(solution)/shard_map/ppermute | solution.py:602
  69.5 6.0 %finish.1 = bf16[512,512]{1,0:T(8,128)(2,1)} custom-call(s32[2]{0:T(128)S(1)} %pad_add_fusion.table, bf16[512,512]{1,0:T(8,128)(2,1)} %collective-permute-done.2.refs_1_.refs_2_.refs_0_, bf16[512,512]{1,0:T(8,128)(2,1)} %collective-permute-done.3.refs_3_.refs_1_, bf16[512,512]{1,0:T(8,128)(2,1)} %collective-permute-done.6.refs_1_.refs_4_.refs_2_, ...), custom_call_target="tpu_custom_call" | custom-call | flops 1 | bytes 1 | tf_op jit(solution)/shard_map/finish/pallas_call | solution.py:560
  75.7 11.3 %stage.3 = (bf16[512,512]{1,0:T(8,128)(2,1)S(1)}, bf16[512,512]{1,0:T(8,128)(2,1)S(1)}) custom-call(s32[10]{0:T(128)S(1)} %stack.120.table, bf16[512,512]{1,0:T(8,128)(2,1)} %get-tuple-element.19.refs_0_, bf16[512,512]{1,0:T(8,128)(2,1)} %collective-permute-done.2.refs_1_.refs_2_.refs_0_, bf16[512,512]{1,0:T(8,128)(2,1)} %collective-permute-done.refs_2_, ...), custom_call_target="tpu_custom_call" | custom-call | tf_op jit(solution)/shard_map/stage/pallas_call | solution.py:463
  87.0 2.1 %collective-permute-start.9 = (bf16[512,512]{1,0:T(8,128)(2,1)S(1)}, bf16[512,512]{1,0:T(8,128)(2,1)S(1)}, u32[]{:S(2)}, u32[]{:S(2)}) collective-permute-start(bf16[512,512]{1,0:T(8,128)(2,1)S(1)} %get-tuple-element.16), channel_id=1, source_target_pairs={{0,2},{1,3},{2,0},{3,1},{4,6},{5,7},{6,4},{7,5},{8,10},{9,11},{10,... | collective-permute-start | bytes 1572872 | tf_op jit(solution)/shard_map/ppermute | solution.py:602
  89.2 12.3 %collective-permute-done.7 = bf16[512,512]{1,0:T(8,128)(2,1)} collective-permute-done((bf16[512,512]{1,0:T(8,128)(2,1)}, bf16[512,512]{1,0:T(8,128)(2,1)}, u32[]{:S(2)}, u32[]{:S(2)}) %collective-permute-start.7) | collective-permute-done | bytes 524320 | tf_op jit(solution)/shard_map/ppermute | solution.py:602
  101.7 1.1 constant_dynamic-update-slice_fusion.3
  102.9 11.9 %collective-permute-done.8 = bf16[512,512]{1,0:T(8,128)(2,1)} collective-permute-done((bf16[512,512]{1,0:T(8,128)(2,1)}, bf16[512,512]{1,0:T(8,128)(2,1)}, u32[]{:S(2)}, u32[]{:S(2)}) %collective-permute-start.8) | collective-permute-done | bytes 524320 | tf_op jit(solution)/shard_map/ppermute | solution.py:602
  114.8 1.1 constant_dynamic-update-slice_fusion.1
  115.9 1.3 %copy-done.2 = bf16[512,2048]{1,0:T(8,128)(2,1)} copy-done((bf16[512,2048]{1,0:T(8,128)(2,1)}, bf16[512,2048]{1,0:T(8,128)(2,1)S(1)}, u32[]{:S(2)}) %copy-start.2) | copy-done | bytes 2097176
  117.2 0.8 constant_dynamic-update-slice_fusion
  (27 shorter events, 1.4 us)
Async XLA Ops:
  0.0 4.7 %copy-start = (bf16[2048,16]{0,1:T(8,128)(2,1)S(1)}, bf16[2048,16]{0,1:T(8,128)(2,1)}, u32[]{:S(2)}) copy-start(bf16[2048,16]{0,1:T(8,128)(2,1)} %param.6) | copy-start | bytes 196612
  0.0 4.7 %copy-start.1 = (bf16[512,2048]{1,0:T(8,128)(2,1)S(1)}, bf16[512,2048]{1,0:T(8,128)(2,1)}, u32[]{:S(2)}) copy-start(bf16[512,2048]{1,0:T(8,128)(2,1)} %param.4) | copy-start | bytes 6291460
  1.4 15.0 %collective-permute-start = (bf16[512,512]{1,0:T(8,128)(2,1)S(1)}, bf16[512,512]{1,0:T(8,128)(2,1)}, u32[]{:S(2)}, u32[]{:S(2)}) collective-permute-start(bf16[512,512]{1,0:T(8,128)(2,1)S(1)} %get-tuple-element.18), channel_id=1, source_target_pairs={{0,2},{1,3},{2,0},{3,1},{4,6},{5,7},{6,4},{7,5},{8,10},{9,11},{10,... | collective-permute-start | bytes 1572872 | tf_op jit(solution)/shard_map/ppermute | solution.py:602
  1.5 29.4 %collective-permute-start.4 = (bf16[512,512]{1,0:T(8,128)(2,1)S(1)}, bf16[512,512]{1,0:T(8,128)(2,1)}, u32[]{:S(2)}, u32[]{:S(2)}) collective-permute-start(bf16[512,512]{1,0:T(8,128)(2,1)S(1)} %get-tuple-element.17), channel_id=1, source_target_pairs={{0,6},{1,7},{2,4},{3,5},{4,2},{5,3},{6,0},{7,1},{8,14},{9,15},{10,... | collective-permute-start | bytes 1572872 | tf_op jit(solution)/shard_map/ppermute | solution.py:602
  6.1 28.4 %all-to-all-start = ((f32[32,1,512]{2,1,0:T(1,128)}), f32[32,1,512]{2,1,0:T(1,128)S(1)}, u32[]{:S(2)}, u32[]{:S(2)}) async-start(f32[32,1,512]{2,1,0:T(1,128)} %all_to_all.6), calls=%async_computation | async-start | bytes 131072 | tf_op jit(solution)/shard_map/all_to_all | solution.py:614
  17.5 17.0 %collective-permute-start.2 = (bf16[512,512]{1,0:T(8,128)(2,1)}, bf16[512,512]{1,0:T(8,128)(2,1)}, u32[]{:S(2)}, u32[]{:S(2)}) collective-permute-start(bf16[512,512]{1,0:T(8,128)(2,1)} %get-tuple-element.19.refs_0_), channel_id=1, source_target_pairs={{0,1},{1,0},{2,3},{3,2},{4,5},{5,4},{6,7},{7,6},{8,9},{9,8},{10,11... | collective-permute-start | bytes 1572872 | tf_op jit(solution)/shard_map/ppermute | solution.py:602
  17.5 35.5 %collective-permute-start.1 = (bf16[512,512]{1,0:T(8,128)(2,1)}, bf16[512,512]{1,0:T(8,128)(2,1)}, u32[]{:S(2)}, u32[]{:S(2)}) collective-permute-start(bf16[512,512]{1,0:T(8,128)(2,1)} %get-tuple-element.20), channel_id=1, source_target_pairs={{0,4},{1,5},{2,6},{3,7},{4,0},{5,1},{6,2},{7,3},{8,12},{9,13},{10,... | collective-permute-start | bytes 1572872 | tf_op jit(solution)/shard_map/ppermute | solution.py:602
  30.7 3.8 %collective-permute-start.3 = (bf16[512,512]{1,0:T(8,128)(2,1)}, bf16[512,512]{1,0:T(8,128)(2,1)}, u32[]{:S(2)}, u32[]{:S(2)}) collective-permute-start(bf16[512,512]{1,0:T(8,128)(2,1)} %collective-permute-done.refs_2_), channel_id=1, source_target_pairs={{0,1},{1,0},{2,3},{3,2},{4,5},{5,4},{6,7},{7,6},{8,9},{9,8},{10,11... | collective-permute-start | bytes 1572872 | tf_op jit(solution)/shard_map/ppermute | solution.py:602
  30.9 3.6 %collective-permute-start.5 = (bf16[512,512]{1,0:T(8,128)(2,1)}, bf16[512,512]{1,0:T(8,128)(2,1)}, u32[]{:S(2)}, u32[]{:S(2)}) collective-permute-start(bf16[512,512]{1,0:T(8,128)(2,1)} %collective-permute-done.4.refs_4_), channel_id=1, source_target_pairs={{0,1},{1,0},{2,3},{3,2},{4,5},{5,4},{6,7},{7,6},{8,9},{9,8},{10,11... | collective-permute-start | bytes 1572872 | tf_op jit(solution)/shard_map/ppermute | solution.py:602
  53.0 2.3 %collective-permute-start.6 = (bf16[512,512]{1,0:T(8,128)(2,1)}, bf16[512,512]{1,0:T(8,128)(2,1)}, u32[]{:S(2)}, u32[]{:S(2)}) collective-permute-start(bf16[512,512]{1,0:T(8,128)(2,1)} %collective-permute-done.1.refs_0_), channel_id=1, source_target_pairs={{0,1},{1,0},{2,3},{3,2},{4,5},{5,4},{6,7},{7,6},{8,9},{9,8},{10,11... | collective-permute-start | bytes 1572872 | tf_op jit(solution)/shard_map/ppermute | solution.py:602
  67.6 33.8 %collective-permute-start.7 = (bf16[512,512]{1,0:T(8,128)(2,1)}, bf16[512,512]{1,0:T(8,128)(2,1)}, u32[]{:S(2)}, u32[]{:S(2)}) collective-permute-start(bf16[512,512]{1,0:T(8,128)(2,1)} %get-tuple-element.13), channel_id=1, source_target_pairs={{0,4},{1,5},{2,6},{3,7},{4,0},{5,1},{6,2},{7,3},{8,12},{9,13},{10,... | collective-permute-start | bytes 1572872 | tf_op jit(solution)/shard_map/ppermute | solution.py:602
  75.5 39.3 %collective-permute-start.8 = (bf16[512,512]{1,0:T(8,128)(2,1)}, bf16[512,512]{1,0:T(8,128)(2,1)}, u32[]{:S(2)}, u32[]{:S(2)}) collective-permute-start(bf16[512,512]{1,0:T(8,128)(2,1)} %finish.1), channel_id=1, source_target_pairs={{0,6},{1,7},{2,4},{3,5},{4,2},{5,3},{6,0},{7,1},{8,14},{9,15},{10,... | collective-permute-start | bytes 1572872 | tf_op jit(solution)/shard_map/ppermute | solution.py:602
  87.0 28.9 %collective-permute-start.9 = (bf16[512,512]{1,0:T(8,128)(2,1)S(1)}, bf16[512,512]{1,0:T(8,128)(2,1)S(1)}, u32[]{:S(2)}, u32[]{:S(2)}) collective-permute-start(bf16[512,512]{1,0:T(8,128)(2,1)S(1)} %get-tuple-element.16), channel_id=1, source_target_pairs={{0,2},{1,3},{2,0},{3,1},{4,6},{5,7},{6,4},{7,5},{8,10},{9,11},{10,... | collective-permute-start | bytes 1572872 | tf_op jit(solution)/shard_map/ppermute | solution.py:602
  115.9 1.3 %copy-start.2 = (bf16[512,2048]{1,0:T(8,128)(2,1)}, bf16[512,2048]{1,0:T(8,128)(2,1)S(1)}, u32[]{:S(2)}) copy-start(bf16[512,2048]{1,0:T(8,128)(2,1)S(1)} %constant_dynamic-update-slice_fusion.1) | copy-start | bytes 6291460

commit v6 on v5

--- a/solution.py
+++ b/solution.py
@@ -197,14 +197,15 @@
 
 def deltas(at, rows, w, pool, both=None):
     here = pl.ds(pl.multiple_of(rows * at, rows), rows)
-    gate = matmul(pool[0, here], w[0]).astype(jnp.bfloat16)
+    gate = matmul(pool[0, here], w[0])
+    sigma = logistic(gate)
+    slope = (1.0 + gate * (1.0 - sigma)).astype(jnp.bfloat16)
+    gated = (gate * sigma).astype(jnp.bfloat16)
     up = matmul(pool[0, here], w[1]).astype(jnp.bfloat16)
     back = matmul_nt(pool[2, here], w[2]).astype(jnp.bfloat16)
-    sigma = logistic(gate)
-    gated = gate * sigma
     pool[1, here] = gated * up
     width = gate.shape[1]
-    gate_delta = back * up * sigma * (1 + gate * (1 - sigma))
+    gate_delta = back * up * (sigma.astype(jnp.bfloat16) * slope)
     up_delta = back * gated
     if both is None:
         pool[3, here] = gate_delta

time: 118 us -> 118 us (level)
  transfers between devices with their start and end apart: 11 -> 11, of which waited for: 4 -> 4; matrix products, arithmetic and copies ran while one was open for 7% -> 6% of each run, Pallas kernels for 30% -> 31%
where the time goes in v6:
time: 118 us
  Pallas kernels  48.7 us (41%)
  waiting for transfers between devices  31 us (26%)
  starting transfers between devices  26.1 us (22%)
  local copies, waits for them, and re-layouts  11.2 us (9%)
    ppermute x10, waiting for transfers between devices, swap(): return lax.ppermute(block, 'tok', [(i, i ^ bits) for i in range(groups)])  31 us
    pallas_call x2, Pallas kernels, stage(): pl.pallas_call(functools.partial(stage_kernel, (count, len(before), begun...  23.7 us
    ppermute x10, starting transfers between devices, swap(): return lax.ppermute(block, 'tok', [(i, i ^ bits) for i in range(groups)])  21.4 us
    pallas_call x1, Pallas kernels, begin(): pl.pallas_call(functools.partial(begin_kernel, count), grid_spec=pltpu.Pr...  19.2 us
    pallas_call x1, Pallas kernels, finish(): pl.pallas_call(functools.partial(finish_kernel, len(before)), grid_spec=p...  5.82 us
    all_to_all x1, starting transfers between devices, head_body(): lax.all_to_all(jnp.repeat(terms, 2, axis=0), ('head', 'tok'), 0, 0, tiled...  4.69 us
    dynamic_update_slice x4, local copies, waits for them, and re-layouts, head_body(): lax.dynamic_update_slice_in_dim(combined, result, (chip ^ slot) * width, 1)  3.1 us
    dynamic_slice x2, local copies, waits for them, and re-layouts, piece(): return lax.dynamic_slice_in_dim(source, (index ^ slot) * width, width, 1)  2.52 us
  transfers between devices with their start and end apart: 11, of which 4 were waited for; matrix products, arithmetic and copies ran while one was open for 6% of the time, Pallas kernels for 31%

profile of v6, /device:TPU:8, one launch (start us, length us, event | category | flops | bytes accessed | tf_op | source)
XLA Modules:
  0.0 118.2 jit_solution(3225020058660126455)
XLA Ops:
  0.0 1.4 %constant_dynamic-slice_fusion = (bf16[512,512]{1,0:T(8,128)(2,1)S(1)}, bf16[512,512]{1,0:T(8,128)(2,1)S(1)}) fusion(bf16[512,2048]{1,0:T(8,128)(2,1)} %param.4, s32[]{:T(128)S(6)} %select_n.109, s32[]{:T(128)S(6)} %select_n.102), kind=kLoop, calls=%fused_computation.11 | loop fusion | bytes 2097160 | tf_op jit(solution)/shard_map/dynamic_slice | solution.py:606
  1.5 3.1 %collective-permute-start.4 = (bf16[512,512]{1,0:T(8,128)(2,1)S(1)}, bf16[512,512]{1,0:T(8,128)(2,1)}, u32[]{:S(2)}, u32[]{:S(2)}) collective-permute-start(bf16[512,512]{1,0:T(8,128)(2,1)S(1)} %get-tuple-element.17), channel_id=1, source_target_pairs={{0,6},{1,7},{2,4},{3,5},{4,2},{5,3},{6,0},{7,1},{8,14},{9,15},{10,... | collective-permute-start | bytes 1572872 | tf_op jit(solution)/shard_map/ppermute | solution.py:603
  4.7 0.6 fusion.3
  5.3 0.7 all_to_all.6
  6.1 4.7 %all-to-all-start = ((f32[32,1,512]{2,1,0:T(1,128)}), f32[32,1,512]{2,1,0:T(1,128)S(1)}, u32[]{:S(2)}, u32[]{:S(2)}) async-start(f32[32,1,512]{2,1,0:T(1,128)} %all_to_all.6), calls=%async_computation | async-start | bytes 131072 | tf_op jit(solution)/shard_map/all_to_all | solution.py:615
  10.8 5.6 %collective-permute-done.refs_2_ = bf16[512,512]{1,0:T(8,128)(2,1)} collective-permute-done((bf16[512,512]{1,0:T(8,128)(2,1)S(1)}, bf16[512,512]{1,0:T(8,128)(2,1)}, u32[]{:S(2)}, u32[]{:S(2)}) %collective-permute-start) | collective-permute-done | bytes 524320 | tf_op jit(solution)/shard_map/ppermute | solution.py:603
  16.4 1.1 constant_dynamic-slice_fusion.1
  17.5 13.2 %collective-permute-start.1 = (bf16[512,512]{1,0:T(8,128)(2,1)}, bf16[512,512]{1,0:T(8,128)(2,1)}, u32[]{:S(2)}, u32[]{:S(2)}) collective-permute-start(bf16[512,512]{1,0:T(8,128)(2,1)} %get-tuple-element.20), channel_id=1, source_target_pairs={{0,4},{1,5},{2,6},{3,7},{4,0},{5,1},{6,2},{7,3},{8,12},{9,13},{10,... | collective-permute-start | bytes 1572872 | tf_op jit(solution)/shard_map/ppermute | solution.py:603
  31.2 1.5 %dynamic-slice_bitcast_fusion.1.refs_6_.refs_5_.refs_7_.refs_4_ = bf16[512,1536]{1,0:T(8,128)(2,1)S(1)} fusion(bf16[4,512,1536]{2,1,0:T(8,128)(2,1)} %param.5, s32[]{:T(128)S(6)} %select_n.110), kind=kLoop, calls=%fused_computation.1 | loop fusion | bytes 3145732 | tf_op jit(solution)/shard_map/jit(dynamic_index_in_dim)/squeeze | solution.py:608
  33.0 1.5 %dynamic-slice_bitcast_fusion.refs_8_.refs_7_.refs_9_ = bf16[3,512,512]{2,1,0:T(8,128)(2,1)S(1)} fusion(bf16[4,3,512,512]{3,2,1,0:T(8,128)(2,1)} %param.7, s32[]{:T(128)S(6)} %select_n.110), kind=kLoop, calls=%fused_computation | loop fusion | bytes 3145732 | tf_op jit(solution)/shard_map/jit(dynamic_index_in_dim)/squeeze | solution.py:609
  34.6 19.2 %begin.1.refs_4_ = bf16[64,512,512]{2,1,0:T(8,128)(2,1)} custom-call(s32[7]{0:T(128)S(1)} %stack.110.table, bf16[512,512]{1,0:T(8,128)(2,1)} %get-tuple-element.19.refs_0_, bf16[512,512]{1,0:T(8,128)(2,1)} %collective-permute-done.2.refs_1_.refs_2_.refs_0_, bf16[512,512]{1,0:T(8,128)(2,1)} %collective-permute-done.refs_2_, ...), custom_call_target="tpu_custom_call" | custom-call | flops 1 | bytes 1 | tf_op jit(solution)/shard_map/begin/pallas_call | solution.py:306
  53.8 0.3 collective-permute-start.6
  54.1 1.9 %collective-permute-done.6.refs_1_.refs_4_.refs_2_ = bf16[512,512]{1,0:T(8,128)(2,1)} collective-permute-done((bf16[512,512]{1,0:T(8,128)(2,1)}, bf16[512,512]{1,0:T(8,128)(2,1)}, u32[]{:S(2)}, u32[]{:S(2)}) %collective-permute-start.6) | collective-permute-done | bytes 524320 | tf_op jit(solution)/shard_map/ppermute | solution.py:603
  56.1 12.4 %stage.2 = (bf16[512,512]{1,0:T(8,128)(2,1)}, bf16[64,512,512]{2,1,0:T(8,128)(2,1)}) custom-call(s32[10]{0:T(128)S(1)} %stack.102.table, bf16[512,512]{1,0:T(8,128)(2,1)} %collective-permute-done.1.refs_0_, bf16[512,512]{1,0:T(8,128)(2,1)} %collective-permute-done.6.refs_1_.refs_4_.refs_2_, ...), custom_call_target="tpu_custom_call", output_to_operand_aliasing={{1}: (5, {})} | custom-call | flops 12884901888 | bytes 25165824 | tf_op jit(solution)/shard_map/stage/pallas_call | solution.py:464
  68.5 1.0 collective-permute-start.7
  69.6 5.8 %finish.1 = bf16[512,512]{1,0:T(8,128)(2,1)} custom-call(s32[2]{0:T(128)S(1)} %pad_add_fusion.table, bf16[512,512]{1,0:T(8,128)(2,1)} %collective-permute-done.2.refs_1_.refs_2_.refs_0_, bf16[512,512]{1,0:T(8,128)(2,1)} %collective-permute-done.3.refs_3_.refs_1_, bf16[512,512]{1,0:T(8,128)(2,1)} %collective-permute-done.6.refs_1_.refs_4_.refs_2_, ...), custom_call_target="tpu_custom_call" | custom-call | flops 1 | bytes 1 | tf_op jit(solution)/shard_map/finish/pallas_call | solution.py:561
  75.6 11.3 %stage.3 = (bf16[512,512]{1,0:T(8,128)(2,1)S(1)}, bf16[512,512]{1,0:T(8,128)(2,1)S(1)}) custom-call(s32[10]{0:T(128)S(1)} %stack.120.table, bf16[512,512]{1,0:T(8,128)(2,1)} %get-tuple-element.19.refs_0_, bf16[512,512]{1,0:T(8,128)(2,1)} %collective-permute-done.2.refs_1_.refs_2_.refs_0_, bf16[512,512]{1,0:T(8,128)(2,1)} %collective-permute-done.refs_2_, ...), custom_call_target="tpu_custom_call" | custom-call | tf_op jit(solution)/shard_map/stage/pallas_call | solution.py:464
  86.9 3.1 %collective-permute-start.9 = (bf16[512,512]{1,0:T(8,128)(2,1)S(1)}, bf16[512,512]{1,0:T(8,128)(2,1)S(1)}, u32[]{:S(2)}, u32[]{:S(2)}) collective-permute-start(bf16[512,512]{1,0:T(8,128)(2,1)S(1)} %get-tuple-element.16), channel_id=1, source_target_pairs={{0,2},{1,3},{2,0},{3,1},{4,6},{5,7},{6,4},{7,5},{8,10},{9,11},{10,... | collective-permute-start | bytes 1572872 | tf_op jit(solution)/shard_map/ppermute | solution.py:603
  90.0 11.5 %collective-permute-done.7 = bf16[512,512]{1,0:T(8,128)(2,1)} collective-permute-done((bf16[512,512]{1,0:T(8,128)(2,1)}, bf16[512,512]{1,0:T(8,128)(2,1)}, u32[]{:S(2)}, u32[]{:S(2)}) %collective-permute-start.7) | collective-permute-done | bytes 524320 | tf_op jit(solution)/shard_map/ppermute | solution.py:603
  101.8 1.1 constant_dynamic-update-slice_fusion.3
  103.0 11.9 %collective-permute-done.8 = bf16[512,512]{1,0:T(8,128)(2,1)} collective-permute-done((bf16[512,512]{1,0:T(8,128)(2,1)}, bf16[512,512]{1,0:T(8,128)(2,1)}, u32[]{:S(2)}, u32[]{:S(2)}) %collective-permute-start.8) | collective-permute-done | bytes 524320 | tf_op jit(solution)/shard_map/ppermute | solution.py:603
  114.9 1.1 constant_dynamic-update-slice_fusion.1
  116.1 1.3 %copy-done.2 = bf16[512,2048]{1,0:T(8,128)(2,1)} copy-done((bf16[512,2048]{1,0:T(8,128)(2,1)}, bf16[512,2048]{1,0:T(8,128)(2,1)S(1)}, u32[]{:S(2)}) %copy-start.2) | copy-done | bytes 2097176
  117.4 0.8 constant_dynamic-update-slice_fusion
  (27 shorter events, 1.4 us)
Async XLA Ops:
  0.0 4.7 %copy-start = (bf16[2048,16]{0,1:T(8,128)(2,1)S(1)}, bf16[2048,16]{0,1:T(8,128)(2,1)}, u32[]{:S(2)}) copy-start(bf16[2048,16]{0,1:T(8,128)(2,1)} %param.6) | copy-start | bytes 196612
  0.0 4.7 %copy-start.1 = (bf16[512,2048]{1,0:T(8,128)(2,1)S(1)}, bf16[512,2048]{1,0:T(8,128)(2,1)}, u32[]{:S(2)}) copy-start(bf16[512,2048]{1,0:T(8,128)(2,1)} %param.4) | copy-start | bytes 6291460
  1.4 15.0 %collective-permute-start = (bf16[512,512]{1,0:T(8,128)(2,1)S(1)}, bf16[512,512]{1,0:T(8,128)(2,1)}, u32[]{:S(2)}, u32[]{:S(2)}) collective-permute-start(bf16[512,512]{1,0:T(8,128)(2,1)S(1)} %get-tuple-element.18), channel_id=1, source_target_pairs={{0,2},{1,3},{2,0},{3,1},{4,6},{5,7},{6,4},{7,5},{8,10},{9,11},{10,... | collective-permute-start | bytes 1572872 | tf_op jit(solution)/shard_map/ppermute | solution.py:603
  1.5 29.4 %collective-permute-start.4 = (bf16[512,512]{1,0:T(8,128)(2,1)S(1)}, bf16[512,512]{1,0:T(8,128)(2,1)}, u32[]{:S(2)}, u32[]{:S(2)}) collective-permute-start(bf16[512,512]{1,0:T(8,128)(2,1)S(1)} %get-tuple-element.17), channel_id=1, source_target_pairs={{0,6},{1,7},{2,4},{3,5},{4,2},{5,3},{6,0},{7,1},{8,14},{9,15},{10,... | collective-permute-start | bytes 1572872 | tf_op jit(solution)/shard_map/ppermute | solution.py:603
  6.1 28.4 %all-to-all-start = ((f32[32,1,512]{2,1,0:T(1,128)}), f32[32,1,512]{2,1,0:T(1,128)S(1)}, u32[]{:S(2)}, u32[]{:S(2)}) async-start(f32[32,1,512]{2,1,0:T(1,128)} %all_to_all.6), calls=%async_computation | async-start | bytes 131072 | tf_op jit(solution)/shard_map/all_to_all | solution.py:615
  17.5 17.0 %collective-permute-start.2 = (bf16[512,512]{1,0:T(8,128)(2,1)}, bf16[512,512]{1,0:T(8,128)(2,1)}, u32[]{:S(2)}, u32[]{:S(2)}) collective-permute-start(bf16[512,512]{1,0:T(8,128)(2,1)} %get-tuple-element.19.refs_0_), channel_id=1, source_target_pairs={{0,1},{1,0},{2,3},{3,2},{4,5},{5,4},{6,7},{7,6},{8,9},{9,8},{10,11... | collective-permute-start | bytes 1572872 | tf_op jit(solution)/shard_map/ppermute | solution.py:603
  17.5 36.2 %collective-permute-start.1 = (bf16[512,512]{1,0:T(8,128)(2,1)}, bf16[512,512]{1,0:T(8,128)(2,1)}, u32[]{:S(2)}, u32[]{:S(2)}) collective-permute-start(bf16[512,512]{1,0:T(8,128)(2,1)} %get-tuple-element.20), channel_id=1, source_target_pairs={{0,4},{1,5},{2,6},{3,7},{4,0},{5,1},{6,2},{7,3},{8,12},{9,13},{10,... | collective-permute-start | bytes 1572872 | tf_op jit(solution)/shard_map/ppermute | solution.py:603
  30.7 3.8 %collective-permute-start.3 = (bf16[512,512]{1,0:T(8,128)(2,1)}, bf16[512,512]{1,0:T(8,128)(2,1)}, u32[]{:S(2)}, u32[]{:S(2)}) collective-permute-start(bf16[512,512]{1,0:T(8,128)(2,1)} %collective-permute-done.refs_2_), channel_id=1, source_target_pairs={{0,1},{1,0},{2,3},{3,2},{4,5},{5,4},{6,7},{7,6},{8,9},{9,8},{10,11... | collective-permute-start | bytes 1572872 | tf_op jit(solution)/shard_map/ppermute | solution.py:603
  30.9 3.6 %collective-permute-start.5 = (bf16[512,512]{1,0:T(8,128)(2,1)}, bf16[512,512]{1,0:T(8,128)(2,1)}, u32[]{:S(2)}, u32[]{:S(2)}) collective-permute-start(bf16[512,512]{1,0:T(8,128)(2,1)} %collective-permute-done.4.refs_4_), channel_id=1, source_target_pairs={{0,1},{1,0},{2,3},{3,2},{4,5},{5,4},{6,7},{7,6},{8,9},{9,8},{10,11... | collective-permute-start | bytes 1572872 | tf_op jit(solution)/shard_map/ppermute | solution.py:603
  53.8 2.3 %collective-permute-start.6 = (bf16[512,512]{1,0:T(8,128)(2,1)}, bf16[512,512]{1,0:T(8,128)(2,1)}, u32[]{:S(2)}, u32[]{:S(2)}) collective-permute-start(bf16[512,512]{1,0:T(8,128)(2,1)} %collective-permute-done.1.refs_0_), channel_id=1, source_target_pairs={{0,1},{1,0},{2,3},{3,2},{4,5},{5,4},{6,7},{7,6},{8,9},{9,8},{10,11... | collective-permute-start | bytes 1572872 | tf_op jit(solution)/shard_map/ppermute | solution.py:603
  68.5 33.1 %collective-permute-start.7 = (bf16[512,512]{1,0:T(8,128)(2,1)}, bf16[512,512]{1,0:T(8,128)(2,1)}, u32[]{:S(2)}, u32[]{:S(2)}) collective-permute-start(bf16[512,512]{1,0:T(8,128)(2,1)} %get-tuple-element.13), channel_id=1, source_target_pairs={{0,4},{1,5},{2,6},{3,7},{4,0},{5,1},{6,2},{7,3},{8,12},{9,13},{10,... | collective-permute-start | bytes 1572872 | tf_op jit(solution)/shard_map/ppermute | solution.py:603
  75.4 39.5 %collective-permute-start.8 = (bf16[512,512]{1,0:T(8,128)(2,1)}, bf16[512,512]{1,0:T(8,128)(2,1)}, u32[]{:S(2)}, u32[]{:S(2)}) collective-permute-start(bf16[512,512]{1,0:T(8,128)(2,1)} %finish.1), channel_id=1, source_target_pairs={{0,6},{1,7},{2,4},{3,5},{4,2},{5,3},{6,0},{7,1},{8,14},{9,15},{10,... | collective-permute-start | bytes 1572872 | tf_op jit(solution)/shard_map/ppermute | solution.py:603
  86.9 29.1 %collective-permute-start.9 = (bf16[512,512]{1,0:T(8,128)(2,1)S(1)}, bf16[512,512]{1,0:T(8,128)(2,1)S(1)}, u32[]{:S(2)}, u32[]{:S(2)}) collective-permute-start(bf16[512,512]{1,0:T(8,128)(2,1)S(1)} %get-tuple-element.16), channel_id=1, source_target_pairs={{0,2},{1,3},{2,0},{3,1},{4,6},{5,7},{6,4},{7,5},{8,10},{9,11},{10,... | collective-permute-start | bytes 1572872 | tf_op jit(solution)/shard_map/ppermute | solution.py:603
  116.0 1.3 %copy-start.2 = (bf16[512,2048]{1,0:T(8,128)(2,1)}, bf16[512,2048]{1,0:T(8,128)(2,1)S(1)}, u32[]{:S(2)}) copy-start(bf16[512,2048]{1,0:T(8,128)(2,1)S(1)} %constant_dynamic-update-slice_fusion.1) | copy-start | bytes 6291460

commit v7 on v5

--- a/solution.py
+++ b/solution.py
@@ -366,7 +366,7 @@
                 raised = jnp.exp(scores - jnp.max(scores, axis=1, keepdims=True))
                 total = jnp.sum(raised, axis=1, keepdims=True)
                 values = v[span(base, rows + part)]
-                attended[own] = matmul(raised.astype(jnp.bfloat16), values) / total
+                attended[own] = matmul(raised.astype(jnp.bfloat16), values) * (1.0 / total)
 
             queries = unit_rows(q[at])
             gate = matmul(queries, fresh[0])
@@ -501,7 +501,7 @@
     scores = jnp.where(band, scores, -1e30)
     raised = jnp.exp(scores - jnp.max(scores, axis=1, keepdims=True))
     total = jnp.sum(raised, axis=1, keepdims=True)
-    return matmul(raised.astype(jnp.bfloat16), values) / total
+    return matmul(raised.astype(jnp.bfloat16), values) * (1.0 / total)
 
 
 def finish_kernel(befores, table, *refs):

time: 118 us -> 118 us (level)
  no operation moved by 1% of the time
where the time goes in v7:
time: 118 us
  Pallas kernels  48.1 us (41%)
  waiting for transfers between devices  31.8 us (27%)
  starting transfers between devices  25.9 us (22%)
  local copies, waits for them, and re-layouts  11.2 us (9%)
    ppermute x10, waiting for transfers between devices, swap(): return lax.ppermute(block, 'tok', [(i, i ^ bits) for i in range(groups)])  31.8 us
    pallas_call x2, Pallas kernels, stage(): pl.pallas_call(functools.partial(stage_kernel, (count, len(before), begun...  23.6 us
    ppermute x10, starting transfers between devices, swap(): return lax.ppermute(block, 'tok', [(i, i ^ bits) for i in range(groups)])  21.2 us
    pallas_call x1, Pallas kernels, begin(): pl.pallas_call(functools.partial(begin_kernel, count), grid_spec=pltpu.Pr...  18.5 us
    pallas_call x1, Pallas kernels, finish(): pl.pallas_call(functools.partial(finish_kernel, len(before)), grid_spec=p...  6.04 us
    all_to_all x1, starting transfers between devices, head_body(): lax.all_to_all(jnp.repeat(terms, 2, axis=0), ('head', 'tok'), 0, 0, tiled...  4.69 us
    dynamic_update_slice x4, local copies, waits for them, and re-layouts, head_body(): lax.dynamic_update_slice_in_dim(combined, result, (chip ^ slot) * width, 1)  3.1 us
    dynamic_slice x2, local copies, waits for them, and re-layouts, piece(): return lax.dynamic_slice_in_dim(source, (index ^ slot) * width, width, 1)  2.52 us
  transfers between devices with their start and end apart: 11, of which 4 were waited for; matrix products, arithmetic and copies ran while one was open for 7% of the time, Pallas kernels for 30%

profile of v7, /device:TPU:8, one launch (start us, length us, event | category | flops | bytes accessed | tf_op | source)
XLA Modules:
  0.0 118.0 jit_solution(17555632689144687125)
XLA Ops:
  0.0 1.4 %constant_dynamic-slice_fusion = (bf16[512,512]{1,0:T(8,128)(2,1)S(1)}, bf16[512,512]{1,0:T(8,128)(2,1)S(1)}) fusion(bf16[512,2048]{1,0:T(8,128)(2,1)} %param.4, s32[]{:T(128)S(6)} %select_n.109, s32[]{:T(128)S(6)} %select_n.102), kind=kLoop, calls=%fused_computation.11 | loop fusion | bytes 2097160 | tf_op jit(solution)/shard_map/dynamic_slice | solution.py:605
  1.5 3.1 %collective-permute-start.4 = (bf16[512,512]{1,0:T(8,128)(2,1)S(1)}, bf16[512,512]{1,0:T(8,128)(2,1)}, u32[]{:S(2)}, u32[]{:S(2)}) collective-permute-start(bf16[512,512]{1,0:T(8,128)(2,1)S(1)} %get-tuple-element.17), channel_id=1, source_target_pairs={{0,6},{1,7},{2,4},{3,5},{4,2},{5,3},{6,0},{7,1},{8,14},{9,15},{10,... | collective-permute-start | bytes 1572872 | tf_op jit(solution)/shard_map/ppermute | solution.py:602
  4.7 0.6 fusion.3
  5.3 0.7 all_to_all.6
  6.1 4.7 %all-to-all-start = ((f32[32,1,512]{2,1,0:T(1,128)}), f32[32,1,512]{2,1,0:T(1,128)S(1)}, u32[]{:S(2)}, u32[]{:S(2)}) async-start(f32[32,1,512]{2,1,0:T(1,128)} %all_to_all.6), calls=%async_computation | async-start | bytes 131072 | tf_op jit(solution)/shard_map/all_to_all | solution.py:614
  10.8 5.6 %collective-permute-done.refs_2_ = bf16[512,512]{1,0:T(8,128)(2,1)} collective-permute-done((bf16[512,512]{1,0:T(8,128)(2,1)S(1)}, bf16[512,512]{1,0:T(8,128)(2,1)}, u32[]{:S(2)}, u32[]{:S(2)}) %collective-permute-start) | collective-permute-done | bytes 524320 | tf_op jit(solution)/shard_map/ppermute | solution.py:602
  16.4 1.1 constant_dynamic-slice_fusion.1
  17.5 13.2 %collective-permute-start.1 = (bf16[512,512]{1,0:T(8,128)(2,1)}, bf16[512,512]{1,0:T(8,128)(2,1)}, u32[]{:S(2)}, u32[]{:S(2)}) collective-permute-start(bf16[512,512]{1,0:T(8,128)(2,1)} %get-tuple-element.20), channel_id=1, source_target_pairs={{0,4},{1,5},{2,6},{3,7},{4,0},{5,1},{6,2},{7,3},{8,12},{9,13},{10,... | collective-permute-start | bytes 1572872 | tf_op jit(solution)/shard_map/ppermute | solution.py:602
  31.2 1.5 %dynamic-slice_bitcast_fusion.1.refs_6_.refs_5_.refs_7_.refs_4_ = bf16[512,1536]{1,0:T(8,128)(2,1)S(1)} fusion(bf16[4,512,1536]{2,1,0:T(8,128)(2,1)} %param.5, s32[]{:T(128)S(6)} %select_n.110), kind=kLoop, calls=%fused_computation.1 | loop fusion | bytes 3145732 | tf_op jit(solution)/shard_map/jit(dynamic_index_in_dim)/squeeze | solution.py:607
  33.0 1.5 %dynamic-slice_bitcast_fusion.refs_8_.refs_7_.refs_9_ = bf16[3,512,512]{2,1,0:T(8,128)(2,1)S(1)} fusion(bf16[4,3,512,512]{3,2,1,0:T(8,128)(2,1)} %param.7, s32[]{:T(128)S(6)} %select_n.110), kind=kLoop, calls=%fused_computation | loop fusion | bytes 3145732 | tf_op jit(solution)/shard_map/jit(dynamic_index_in_dim)/squeeze | solution.py:608
  34.6 18.5 %begin.1.refs_4_ = bf16[64,512,512]{2,1,0:T(8,128)(2,1)} custom-call(s32[7]{0:T(128)S(1)} %stack.110.table, bf16[512,512]{1,0:T(8,128)(2,1)} %get-tuple-element.19.refs_0_, bf16[512,512]{1,0:T(8,128)(2,1)} %collective-permute-done.2.refs_1_.refs_2_.refs_0_, bf16[512,512]{1,0:T(8,128)(2,1)} %collective-permute-done.refs_2_, ...), custom_call_target="tpu_custom_call" | custom-call | flops 1 | bytes 1 | tf_op jit(solution)/shard_map/begin/pallas_call | solution.py:305
  53.0 0.3 collective-permute-start.6
  53.4 1.9 %collective-permute-done.6.refs_1_.refs_4_.refs_2_ = bf16[512,512]{1,0:T(8,128)(2,1)} collective-permute-done((bf16[512,512]{1,0:T(8,128)(2,1)}, bf16[512,512]{1,0:T(8,128)(2,1)}, u32[]{:S(2)}, u32[]{:S(2)}) %collective-permute-start.6) | collective-permute-done | bytes 524320 | tf_op jit(solution)/shard_map/ppermute | solution.py:602
  55.4 12.3 %stage.2 = (bf16[512,512]{1,0:T(8,128)(2,1)}, bf16[64,512,512]{2,1,0:T(8,128)(2,1)}) custom-call(s32[10]{0:T(128)S(1)} %stack.102.table, bf16[512,512]{1,0:T(8,128)(2,1)} %collective-permute-done.1.refs_0_, bf16[512,512]{1,0:T(8,128)(2,1)} %collective-permute-done.6.refs_1_.refs_4_.refs_2_, ...), custom_call_target="tpu_custom_call", output_to_operand_aliasing={{1}: (5, {})} | custom-call | flops 12884901888 | bytes 25165824 | tf_op jit(solution)/shard_map/stage/pallas_call | solution.py:463
  67.6 1.8 %collective-permute-start.7 = (bf16[512,512]{1,0:T(8,128)(2,1)}, bf16[512,512]{1,0:T(8,128)(2,1)}, u32[]{:S(2)}, u32[]{:S(2)}) collective-permute-start(bf16[512,512]{1,0:T(8,128)(2,1)} %get-tuple-element.13), channel_id=1, source_target_pairs={{0,4},{1,5},{2,6},{3,7},{4,0},{5,1},{6,2},{7,3},{8,12},{9,13},{10,... | collective-permute-start | bytes 1572872 | tf_op jit(solution)/shard_map/ppermute | solution.py:602
  69.5 6.0 %finish.1 = bf16[512,512]{1,0:T(8,128)(2,1)} custom-call(s32[2]{0:T(128)S(1)} %pad_add_fusion.table, bf16[512,512]{1,0:T(8,128)(2,1)} %collective-permute-done.2.refs_1_.refs_2_.refs_0_, bf16[512,512]{1,0:T(8,128)(2,1)} %collective-permute-done.3.refs_3_.refs_1_, bf16[512,512]{1,0:T(8,128)(2,1)} %collective-permute-done.6.refs_1_.refs_4_.refs_2_, ...), custom_call_target="tpu_custom_call" | custom-call | flops 1 | bytes 1 | tf_op jit(solution)/shard_map/finish/pallas_call | solution.py:560
  75.7 11.3 %stage.3 = (bf16[512,512]{1,0:T(8,128)(2,1)S(1)}, bf16[512,512]{1,0:T(8,128)(2,1)S(1)}) custom-call(s32[10]{0:T(128)S(1)} %stack.120.table, bf16[512,512]{1,0:T(8,128)(2,1)} %get-tuple-element.19.refs_0_, bf16[512,512]{1,0:T(8,128)(2,1)} %collective-permute-done.2.refs_1_.refs_2_.refs_0_, bf16[512,512]{1,0:T(8,128)(2,1)} %collective-permute-done.refs_2_, ...), custom_call_target="tpu_custom_call" | custom-call | tf_op jit(solution)/shard_map/stage/pallas_call | solution.py:463
  87.0 2.1 %collective-permute-start.9 = (bf16[512,512]{1,0:T(8,128)(2,1)S(1)}, bf16[512,512]{1,0:T(8,128)(2,1)S(1)}, u32[]{:S(2)}, u32[]{:S(2)}) collective-permute-start(bf16[512,512]{1,0:T(8,128)(2,1)S(1)} %get-tuple-element.16), channel_id=1, source_target_pairs={{0,2},{1,3},{2,0},{3,1},{4,6},{5,7},{6,4},{7,5},{8,10},{9,11},{10,... | collective-permute-start | bytes 1572872 | tf_op jit(solution)/shard_map/ppermute | solution.py:602
  89.2 12.3 %collective-permute-done.7 = bf16[512,512]{1,0:T(8,128)(2,1)} collective-permute-done((bf16[512,512]{1,0:T(8,128)(2,1)}, bf16[512,512]{1,0:T(8,128)(2,1)}, u32[]{:S(2)}, u32[]{:S(2)}) %collective-permute-start.7) | collective-permute-done | bytes 524320 | tf_op jit(solution)/shard_map/ppermute | solution.py:602
  101.7 1.1 constant_dynamic-update-slice_fusion.3
  102.9 11.9 %collective-permute-done.8 = bf16[512,512]{1,0:T(8,128)(2,1)} collective-permute-done((bf16[512,512]{1,0:T(8,128)(2,1)}, bf16[512,512]{1,0:T(8,128)(2,1)}, u32[]{:S(2)}, u32[]{:S(2)}) %collective-permute-start.8) | collective-permute-done | bytes 524320 | tf_op jit(solution)/shard_map/ppermute | solution.py:602
  114.8 1.1 constant_dynamic-update-slice_fusion.1
  115.9 1.3 %copy-done.2 = bf16[512,2048]{1,0:T(8,128)(2,1)} copy-done((bf16[512,2048]{1,0:T(8,128)(2,1)}, bf16[512,2048]{1,0:T(8,128)(2,1)S(1)}, u32[]{:S(2)}) %copy-start.2) | copy-done | bytes 2097176
  117.2 0.8 constant_dynamic-update-slice_fusion
  (27 shorter events, 1.4 us)
Async XLA Ops:
  0.0 4.7 %copy-start = (bf16[2048,16]{0,1:T(8,128)(2,1)S(1)}, bf16[2048,16]{0,1:T(8,128)(2,1)}, u32[]{:S(2)}) copy-start(bf16[2048,16]{0,1:T(8,128)(2,1)} %param.6) | copy-start | bytes 196612
  0.0 4.7 %copy-start.1 = (bf16[512,2048]{1,0:T(8,128)(2,1)S(1)}, bf16[512,2048]{1,0:T(8,128)(2,1)}, u32[]{:S(2)}) copy-start(bf16[512,2048]{1,0:T(8,128)(2,1)} %param.4) | copy-start | bytes 6291460
  1.4 15.0 %collective-permute-start = (bf16[512,512]{1,0:T(8,128)(2,1)S(1)}, bf16[512,512]{1,0:T(8,128)(2,1)}, u32[]{:S(2)}, u32[]{:S(2)}) collective-permute-start(bf16[512,512]{1,0:T(8,128)(2,1)S(1)} %get-tuple-element.18), channel_id=1, source_target_pairs={{0,2},{1,3},{2,0},{3,1},{4,6},{5,7},{6,4},{7,5},{8,10},{9,11},{10,... | collective-permute-start | bytes 1572872 | tf_op jit(solution)/shard_map/ppermute | solution.py:602
  1.5 29.4 %collective-permute-start.4 = (bf16[512,512]{1,0:T(8,128)(2,1)S(1)}, bf16[512,512]{1,0:T(8,128)(2,1)}, u32[]{:S(2)}, u32[]{:S(2)}) collective-permute-start(bf16[512,512]{1,0:T(8,128)(2,1)S(1)} %get-tuple-element.17), channel_id=1, source_target_pairs={{0,6},{1,7},{2,4},{3,5},{4,2},{5,3},{6,0},{7,1},{8,14},{9,15},{10,... | collective-permute-start | bytes 1572872 | tf_op jit(solution)/shard_map/ppermute | solution.py:602
  6.1 28.4 %all-to-all-start = ((f32[32,1,512]{2,1,0:T(1,128)}), f32[32,1,512]{2,1,0:T(1,128)S(1)}, u32[]{:S(2)}, u32[]{:S(2)}) async-start(f32[32,1,512]{2,1,0:T(1,128)} %all_to_all.6), calls=%async_computation | async-start | bytes 131072 | tf_op jit(solution)/shard_map/all_to_all | solution.py:614
  17.5 17.0 %collective-permute-start.2 = (bf16[512,512]{1,0:T(8,128)(2,1)}, bf16[512,512]{1,0:T(8,128)(2,1)}, u32[]{:S(2)}, u32[]{:S(2)}) collective-permute-start(bf16[512,512]{1,0:T(8,128)(2,1)} %get-tuple-element.19.refs_0_), channel_id=1, source_target_pairs={{0,1},{1,0},{2,3},{3,2},{4,5},{5,4},{6,7},{7,6},{8,9},{9,8},{10,11... | collective-permute-start | bytes 1572872 | tf_op jit(solution)/shard_map/ppermute | solution.py:602
  17.5 35.5 %collective-permute-start.1 = (bf16[512,512]{1,0:T(8,128)(2,1)}, bf16[512,512]{1,0:T(8,128)(2,1)}, u32[]{:S(2)}, u32[]{:S(2)}) collective-permute-start(bf16[512,512]{1,0:T(8,128)(2,1)} %get-tuple-element.20), channel_id=1, source_target_pairs={{0,4},{1,5},{2,6},{3,7},{4,0},{5,1},{6,2},{7,3},{8,12},{9,13},{10,... | collective-permute-start | bytes 1572872 | tf_op jit(solution)/shard_map/ppermute | solution.py:602
  30.7 3.8 %collective-permute-start.3 = (bf16[512,512]{1,0:T(8,128)(2,1)}, bf16[512,512]{1,0:T(8,128)(2,1)}, u32[]{:S(2)}, u32[]{:S(2)}) collective-permute-start(bf16[512,512]{1,0:T(8,128)(2,1)} %collective-permute-done.refs_2_), channel_id=1, source_target_pairs={{0,1},{1,0},{2,3},{3,2},{4,5},{5,4},{6,7},{7,6},{8,9},{9,8},{10,11... | collective-permute-start | bytes 1572872 | tf_op jit(solution)/shard_map/ppermute | solution.py:602
  30.9 3.6 %collective-permute-start.5 = (bf16[512,512]{1,0:T(8,128)(2,1)}, bf16[512,512]{1,0:T(8,128)(2,1)}, u32[]{:S(2)}, u32[]{:S(2)}) collective-permute-start(bf16[512,512]{1,0:T(8,128)(2,1)} %collective-permute-done.4.refs_4_), channel_id=1, source_target_pairs={{0,1},{1,0},{2,3},{3,2},{4,5},{5,4},{6,7},{7,6},{8,9},{9,8},{10,11... | collective-permute-start | bytes 1572872 | tf_op jit(solution)/shard_map/ppermute | solution.py:602
  53.0 2.3 %collective-permute-start.6 = (bf16[512,512]{1,0:T(8,128)(2,1)}, bf16[512,512]{1,0:T(8,128)(2,1)}, u32[]{:S(2)}, u32[]{:S(2)}) collective-permute-start(bf16[512,512]{1,0:T(8,128)(2,1)} %collective-permute-done.1.refs_0_), channel_id=1, source_target_pairs={{0,1},{1,0},{2,3},{3,2},{4,5},{5,4},{6,7},{7,6},{8,9},{9,8},{10,11... | collective-permute-start | bytes 1572872 | tf_op jit(solution)/shard_map/ppermute | solution.py:602
  67.6 33.8 %collective-permute-start.7 = (bf16[512,512]{1,0:T(8,128)(2,1)}, bf16[512,512]{1,0:T(8,128)(2,1)}, u32[]{:S(2)}, u32[]{:S(2)}) collective-permute-start(bf16[512,512]{1,0:T(8,128)(2,1)} %get-tuple-element.13), channel_id=1, source_target_pairs={{0,4},{1,5},{2,6},{3,7},{4,0},{5,1},{6,2},{7,3},{8,12},{9,13},{10,... | collective-permute-start | bytes 1572872 | tf_op jit(solution)/shard_map/ppermute | solution.py:602
  75.5 39.3 %collective-permute-start.8 = (bf16[512,512]{1,0:T(8,128)(2,1)}, bf16[512,512]{1,0:T(8,128)(2,1)}, u32[]{:S(2)}, u32[]{:S(2)}) collective-permute-start(bf16[512,512]{1,0:T(8,128)(2,1)} %finish.1), channel_id=1, source_target_pairs={{0,6},{1,7},{2,4},{3,5},{4,2},{5,3},{6,0},{7,1},{8,14},{9,15},{10,... | collective-permute-start | bytes 1572872 | tf_op jit(solution)/shard_map/ppermute | solution.py:602
  87.0 28.9 %collective-permute-start.9 = (bf16[512,512]{1,0:T(8,128)(2,1)S(1)}, bf16[512,512]{1,0:T(8,128)(2,1)S(1)}, u32[]{:S(2)}, u32[]{:S(2)}) collective-permute-start(bf16[512,512]{1,0:T(8,128)(2,1)S(1)} %get-tuple-element.16), channel_id=1, source_target_pairs={{0,2},{1,3},{2,0},{3,1},{4,6},{5,7},{6,4},{7,5},{8,10},{9,11},{10,... | collective-permute-start | bytes 1572872 | tf_op jit(solution)/shard_map/ppermute | solution.py:602
  115.9 1.3 %copy-start.2 = (bf16[512,2048]{1,0:T(8,128)(2,1)}, bf16[512,2048]{1,0:T(8,128)(2,1)S(1)}, u32[]{:S(2)}) copy-start(bf16[512,2048]{1,0:T(8,128)(2,1)S(1)} %constant_dynamic-update-slice_fusion.1) | copy-start | bytes 6291460

commit v8 on v5

--- a/solution.py
+++ b/solution.py
@@ -12,7 +12,7 @@
 
 rate_base = 0.003
 epsilon = 1e-06
-VMEM_LIMIT = 40 * 1024 * 1024
+VMEM_LIMIT = 36 * 1024 * 1024
 STATE = 64
 
 

time: 118 us -> 118 us (level)
  no operation moved by 1% of the time
where the time goes in v8:
time: 118 us
  Pallas kernels  48.1 us (41%)
  waiting for transfers between devices  31.8 us (27%)
  starting transfers between devices  25.9 us (22%)
  local copies, waits for them, and re-layouts  11.2 us (9%)
    ppermute x10, waiting for transfers between devices, swap(): return lax.ppermute(block, 'tok', [(i, i ^ bits) for i in range(groups)])  31.8 us
    pallas_call x2, Pallas kernels, stage(): pl.pallas_call(functools.partial(stage_kernel, (count, len(before), begun...  23.6 us
    ppermute x10, starting transfers between devices, swap(): return lax.ppermute(block, 'tok', [(i, i ^ bits) for i in range(groups)])  21.2 us
    pallas_call x1, Pallas kernels, begin(): pl.pallas_call(functools.partial(begin_kernel, count), grid_spec=pltpu.Pr...  18.5 us
    pallas_call x1, Pallas kernels, finish(): pl.pallas_call(functools.partial(finish_kernel, len(before)), grid_spec=p...  6.04 us
    all_to_all x1, starting transfers between devices, head_body(): lax.all_to_all(jnp.repeat(terms, 2, axis=0), ('head', 'tok'), 0, 0, tiled...  4.69 us
    dynamic_update_slice x4, local copies, waits for them, and re-layouts, head_body(): lax.dynamic_update_slice_in_dim(combined, result, (chip ^ slot) * width, 1)  3.1 us
    dynamic_slice x2, local copies, waits for them, and re-layouts, piece(): return lax.dynamic_slice_in_dim(source, (index ^ slot) * width, width, 1)  2.52 us
  transfers between devices with their start and end apart: 11, of which 4 were waited for; matrix products, arithmetic and copies ran while one was open for 7% of the time, Pallas kernels for 30%

profile of v8, /device:TPU:8, one launch (start us, length us, event | category | flops | bytes accessed | tf_op | source)
XLA Modules:
  0.0 118.0 jit_solution(3939439293194916196)
XLA Ops:
  0.0 1.4 %constant_dynamic-slice_fusion = (bf16[512,512]{1,0:T(8,128)(2,1)S(1)}, bf16[512,512]{1,0:T(8,128)(2,1)S(1)}) fusion(bf16[512,2048]{1,0:T(8,128)(2,1)} %param.4, s32[]{:T(128)S(6)} %select_n.109, s32[]{:T(128)S(6)} %select_n.102), kind=kLoop, calls=%fused_computation.11 | loop fusion | bytes 2097160 | tf_op jit(solution)/shard_map/dynamic_slice | solution.py:605
  1.5 3.1 %collective-permute-start.4 = (bf16[512,512]{1,0:T(8,128)(2,1)S(1)}, bf16[512,512]{1,0:T(8,128)(2,1)}, u32[]{:S(2)}, u32[]{:S(2)}) collective-permute-start(bf16[512,512]{1,0:T(8,128)(2,1)S(1)} %get-tuple-element.17), channel_id=1, source_target_pairs={{0,6},{1,7},{2,4},{3,5},{4,2},{5,3},{6,0},{7,1},{8,14},{9,15},{10,... | collective-permute-start | bytes 1572872 | tf_op jit(solution)/shard_map/ppermute | solution.py:602
  4.7 0.6 fusion.3
  5.3 0.7 all_to_all.6
  6.1 4.7 %all-to-all-start = ((f32[32,1,512]{2,1,0:T(1,128)}), f32[32,1,512]{2,1,0:T(1,128)S(1)}, u32[]{:S(2)}, u32[]{:S(2)}) async-start(f32[32,1,512]{2,1,0:T(1,128)} %all_to_all.6), calls=%async_computation | async-start | bytes 131072 | tf_op jit(solution)/shard_map/all_to_all | solution.py:614
  10.8 5.6 %collective-permute-done.refs_2_ = bf16[512,512]{1,0:T(8,128)(2,1)} collective-permute-done((bf16[512,512]{1,0:T(8,128)(2,1)S(1)}, bf16[512,512]{1,0:T(8,128)(2,1)}, u32[]{:S(2)}, u32[]{:S(2)}) %collective-permute-start) | collective-permute-done | bytes 524320 | tf_op jit(solution)/shard_map/ppermute | solution.py:602
  16.4 1.1 constant_dynamic-slice_fusion.1
  17.5 13.2 %collective-permute-start.1 = (bf16[512,512]{1,0:T(8,128)(2,1)}, bf16[512,512]{1,0:T(8,128)(2,1)}, u32[]{:S(2)}, u32[]{:S(2)}) collective-permute-start(bf16[512,512]{1,0:T(8,128)(2,1)} %get-tuple-element.20), channel_id=1, source_target_pairs={{0,4},{1,5},{2,6},{3,7},{4,0},{5,1},{6,2},{7,3},{8,12},{9,13},{10,... | collective-permute-start | bytes 1572872 | tf_op jit(solution)/shard_map/ppermute | solution.py:602
  31.2 1.5 %dynamic-slice_bitcast_fusion.1.refs_6_.refs_5_.refs_7_.refs_4_ = bf16[512,1536]{1,0:T(8,128)(2,1)S(1)} fusion(bf16[4,512,1536]{2,1,0:T(8,128)(2,1)} %param.5, s32[]{:T(128)S(6)} %select_n.110), kind=kLoop, calls=%fused_computation.1 | loop fusion | bytes 3145732 | tf_op jit(solution)/shard_map/jit(dynamic_index_in_dim)/squeeze | solution.py:607
  33.0 1.5 %dynamic-slice_bitcast_fusion.refs_8_.refs_7_.refs_9_ = bf16[3,512,512]{2,1,0:T(8,128)(2,1)S(1)} fusion(bf16[4,3,512,512]{3,2,1,0:T(8,128)(2,1)} %param.7, s32[]{:T(128)S(6)} %select_n.110), kind=kLoop, calls=%fused_computation | loop fusion | bytes 3145732 | tf_op jit(solution)/shard_map/jit(dynamic_index_in_dim)/squeeze | solution.py:608
  34.6 18.5 %begin.1.refs_4_ = bf16[64,512,512]{2,1,0:T(8,128)(2,1)} custom-call(s32[7]{0:T(128)S(1)} %stack.110.table, bf16[512,512]{1,0:T(8,128)(2,1)} %get-tuple-element.19.refs_0_, bf16[512,512]{1,0:T(8,128)(2,1)} %collective-permute-done.2.refs_1_.refs_2_.refs_0_, bf16[512,512]{1,0:T(8,128)(2,1)} %collective-permute-done.refs_2_, ...), custom_call_target="tpu_custom_call" | custom-call | flops 1 | bytes 1 | tf_op jit(solution)/shard_map/begin/pallas_call | solution.py:305
  53.0 0.3 collective-permute-start.6
  53.4 1.9 %collective-permute-done.6.refs_1_.refs_4_.refs_2_ = bf16[512,512]{1,0:T(8,128)(2,1)} collective-permute-done((bf16[512,512]{1,0:T(8,128)(2,1)}, bf16[512,512]{1,0:T(8,128)(2,1)}, u32[]{:S(2)}, u32[]{:S(2)}) %collective-permute-start.6) | collective-permute-done | bytes 524320 | tf_op jit(solution)/shard_map/ppermute | solution.py:602
  55.4 12.3 %stage.2 = (bf16[512,512]{1,0:T(8,128)(2,1)}, bf16[64,512,512]{2,1,0:T(8,128)(2,1)}) custom-call(s32[10]{0:T(128)S(1)} %stack.102.table, bf16[512,512]{1,0:T(8,128)(2,1)} %collective-permute-done.1.refs_0_, bf16[512,512]{1,0:T(8,128)(2,1)} %collective-permute-done.6.refs_1_.refs_4_.refs_2_, ...), custom_call_target="tpu_custom_call", output_to_operand_aliasing={{1}: (5, {})} | custom-call | flops 12884901888 | bytes 25165824 | tf_op jit(solution)/shard_map/stage/pallas_call | solution.py:463
  67.6 1.8 %collective-permute-start.7 = (bf16[512,512]{1,0:T(8,128)(2,1)}, bf16[512,512]{1,0:T(8,128)(2,1)}, u32[]{:S(2)}, u32[]{:S(2)}) collective-permute-start(bf16[512,512]{1,0:T(8,128)(2,1)} %get-tuple-element.13), channel_id=1, source_target_pairs={{0,4},{1,5},{2,6},{3,7},{4,0},{5,1},{6,2},{7,3},{8,12},{9,13},{10,... | collective-permute-start | bytes 1572872 | tf_op jit(solution)/shard_map/ppermute | solution.py:602
  69.5 6.0 %finish.1 = bf16[512,512]{1,0:T(8,128)(2,1)} custom-call(s32[2]{0:T(128)S(1)} %pad_add_fusion.table, bf16[512,512]{1,0:T(8,128)(2,1)} %collective-permute-done.2.refs_1_.refs_2_.refs_0_, bf16[512,512]{1,0:T(8,128)(2,1)} %collective-permute-done.3.refs_3_.refs_1_, bf16[512,512]{1,0:T(8,128)(2,1)} %collective-permute-done.6.refs_1_.refs_4_.refs_2_, ...), custom_call_target="tpu_custom_call" | custom-call | flops 1 | bytes 1 | tf_op jit(solution)/shard_map/finish/pallas_call | solution.py:560
  75.7 11.3 %stage.3 = (bf16[512,512]{1,0:T(8,128)(2,1)S(1)}, bf16[512,512]{1,0:T(8,128)(2,1)S(1)}) custom-call(s32[10]{0:T(128)S(1)} %stack.120.table, bf16[512,512]{1,0:T(8,128)(2,1)} %get-tuple-element.19.refs_0_, bf16[512,512]{1,0:T(8,128)(2,1)} %collective-permute-done.2.refs_1_.refs_2_.refs_0_, bf16[512,512]{1,0:T(8,128)(2,1)} %collective-permute-done.refs_2_, ...), custom_call_target="tpu_custom_call" | custom-call | tf_op jit(solution)/shard_map/stage/pallas_call | solution.py:463
  87.0 2.1 %collective-permute-start.9 = (bf16[512,512]{1,0:T(8,128)(2,1)S(1)}, bf16[512,512]{1,0:T(8,128)(2,1)S(1)}, u32[]{:S(2)}, u32[]{:S(2)}) collective-permute-start(bf16[512,512]{1,0:T(8,128)(2,1)S(1)} %get-tuple-element.16), channel_id=1, source_target_pairs={{0,2},{1,3},{2,0},{3,1},{4,6},{5,7},{6,4},{7,5},{8,10},{9,11},{10,... | collective-permute-start | bytes 1572872 | tf_op jit(solution)/shard_map/ppermute | solution.py:602
  89.2 12.3 %collective-permute-done.7 = bf16[512,512]{1,0:T(8,128)(2,1)} collective-permute-done((bf16[512,512]{1,0:T(8,128)(2,1)}, bf16[512,512]{1,0:T(8,128)(2,1)}, u32[]{:S(2)}, u32[]{:S(2)}) %collective-permute-start.7) | collective-permute-done | bytes 524320 | tf_op jit(solution)/shard_map/ppermute | solution.py:602
  101.7 1.1 constant_dynamic-update-slice_fusion.3
  102.9 11.9 %collective-permute-done.8 = bf16[512,512]{1,0:T(8,128)(2,1)} collective-permute-done((bf16[512,512]{1,0:T(8,128)(2,1)}, bf16[512,512]{1,0:T(8,128)(2,1)}, u32[]{:S(2)}, u32[]{:S(2)}) %collective-permute-start.8) | collective-permute-done | bytes 524320 | tf_op jit(solution)/shard_map/ppermute | solution.py:602
  114.8 1.1 constant_dynamic-update-slice_fusion.1
  115.9 1.3 %copy-done.2 = bf16[512,2048]{1,0:T(8,128)(2,1)} copy-done((bf16[512,2048]{1,0:T(8,128)(2,1)}, bf16[512,2048]{1,0:T(8,128)(2,1)S(1)}, u32[]{:S(2)}) %copy-start.2) | copy-done | bytes 2097176
  117.2 0.8 constant_dynamic-update-slice_fusion
  (27 shorter events, 1.4 us)
Async XLA Ops:
  0.0 4.7 %copy-start = (bf16[2048,16]{0,1:T(8,128)(2,1)S(1)}, bf16[2048,16]{0,1:T(8,128)(2,1)}, u32[]{:S(2)}) copy-start(bf16[2048,16]{0,1:T(8,128)(2,1)} %param.6) | copy-start | bytes 196612
  0.0 4.7 %copy-start.1 = (bf16[512,2048]{1,0:T(8,128)(2,1)S(1)}, bf16[512,2048]{1,0:T(8,128)(2,1)}, u32[]{:S(2)}) copy-start(bf16[512,2048]{1,0:T(8,128)(2,1)} %param.4) | copy-start | bytes 6291460
  1.4 15.0 %collective-permute-start = (bf16[512,512]{1,0:T(8,128)(2,1)S(1)}, bf16[512,512]{1,0:T(8,128)(2,1)}, u32[]{:S(2)}, u32[]{:S(2)}) collective-permute-start(bf16[512,512]{1,0:T(8,128)(2,1)S(1)} %get-tuple-element.18), channel_id=1, source_target_pairs={{0,2},{1,3},{2,0},{3,1},{4,6},{5,7},{6,4},{7,5},{8,10},{9,11},{10,... | collective-permute-start | bytes 1572872 | tf_op jit(solution)/shard_map/ppermute | solution.py:602
  1.5 29.4 %collective-permute-start.4 = (bf16[512,512]{1,0:T(8,128)(2,1)S(1)}, bf16[512,512]{1,0:T(8,128)(2,1)}, u32[]{:S(2)}, u32[]{:S(2)}) collective-permute-start(bf16[512,512]{1,0:T(8,128)(2,1)S(1)} %get-tuple-element.17), channel_id=1, source_target_pairs={{0,6},{1,7},{2,4},{3,5},{4,2},{5,3},{6,0},{7,1},{8,14},{9,15},{10,... | collective-permute-start | bytes 1572872 | tf_op jit(solution)/shard_map/ppermute | solution.py:602
  6.1 28.4 %all-to-all-start = ((f32[32,1,512]{2,1,0:T(1,128)}), f32[32,1,512]{2,1,0:T(1,128)S(1)}, u32[]{:S(2)}, u32[]{:S(2)}) async-start(f32[32,1,512]{2,1,0:T(1,128)} %all_to_all.6), calls=%async_computation | async-start | bytes 131072 | tf_op jit(solution)/shard_map/all_to_all | solution.py:614
  17.5 17.0 %collective-permute-start.2 = (bf16[512,512]{1,0:T(8,128)(2,1)}, bf16[512,512]{1,0:T(8,128)(2,1)}, u32[]{:S(2)}, u32[]{:S(2)}) collective-permute-start(bf16[512,512]{1,0:T(8,128)(2,1)} %get-tuple-element.19.refs_0_), channel_id=1, source_target_pairs={{0,1},{1,0},{2,3},{3,2},{4,5},{5,4},{6,7},{7,6},{8,9},{9,8},{10,11... | collective-permute-start | bytes 1572872 | tf_op jit(solution)/shard_map/ppermute | solution.py:602
  17.5 35.5 %collective-permute-start.1 = (bf16[512,512]{1,0:T(8,128)(2,1)}, bf16[512,512]{1,0:T(8,128)(2,1)}, u32[]{:S(2)}, u32[]{:S(2)}) collective-permute-start(bf16[512,512]{1,0:T(8,128)(2,1)} %get-tuple-element.20), channel_id=1, source_target_pairs={{0,4},{1,5},{2,6},{3,7},{4,0},{5,1},{6,2},{7,3},{8,12},{9,13},{10,... | collective-permute-start | bytes 1572872 | tf_op jit(solution)/shard_map/ppermute | solution.py:602
  30.7 3.8 %collective-permute-start.3 = (bf16[512,512]{1,0:T(8,128)(2,1)}, bf16[512,512]{1,0:T(8,128)(2,1)}, u32[]{:S(2)}, u32[]{:S(2)}) collective-permute-start(bf16[512,512]{1,0:T(8,128)(2,1)} %collective-permute-done.refs_2_), channel_id=1, source_target_pairs={{0,1},{1,0},{2,3},{3,2},{4,5},{5,4},{6,7},{7,6},{8,9},{9,8},{10,11... | collective-permute-start | bytes 1572872 | tf_op jit(solution)/shard_map/ppermute | solution.py:602
  30.9 3.6 %collective-permute-start.5 = (bf16[512,512]{1,0:T(8,128)(2,1)}, bf16[512,512]{1,0:T(8,128)(2,1)}, u32[]{:S(2)}, u32[]{:S(2)}) collective-permute-start(bf16[512,512]{1,0:T(8,128)(2,1)} %collective-permute-done.4.refs_4_), channel_id=1, source_target_pairs={{0,1},{1,0},{2,3},{3,2},{4,5},{5,4},{6,7},{7,6},{8,9},{9,8},{10,11... | collective-permute-start | bytes 1572872 | tf_op jit(solution)/shard_map/ppermute | solution.py:602
  53.0 2.3 %collective-permute-start.6 = (bf16[512,512]{1,0:T(8,128)(2,1)}, bf16[512,512]{1,0:T(8,128)(2,1)}, u32[]{:S(2)}, u32[]{:S(2)}) collective-permute-start(bf16[512,512]{1,0:T(8,128)(2,1)} %collective-permute-done.1.refs_0_), channel_id=1, source_target_pairs={{0,1},{1,0},{2,3},{3,2},{4,5},{5,4},{6,7},{7,6},{8,9},{9,8},{10,11... | collective-permute-start | bytes 1572872 | tf_op jit(solution)/shard_map/ppermute | solution.py:602
  67.6 33.8 %collective-permute-start.7 = (bf16[512,512]{1,0:T(8,128)(2,1)}, bf16[512,512]{1,0:T(8,128)(2,1)}, u32[]{:S(2)}, u32[]{:S(2)}) collective-permute-start(bf16[512,512]{1,0:T(8,128)(2,1)} %get-tuple-element.13), channel_id=1, source_target_pairs={{0,4},{1,5},{2,6},{3,7},{4,0},{5,1},{6,2},{7,3},{8,12},{9,13},{10,... | collective-permute-start | bytes 1572872 | tf_op jit(solution)/shard_map/ppermute | solution.py:602
  75.5 39.3 %collective-permute-start.8 = (bf16[512,512]{1,0:T(8,128)(2,1)}, bf16[512,512]{1,0:T(8,128)(2,1)}, u32[]{:S(2)}, u32[]{:S(2)}) collective-permute-start(bf16[512,512]{1,0:T(8,128)(2,1)} %finish.1), channel_id=1, source_target_pairs={{0,6},{1,7},{2,4},{3,5},{4,2},{5,3},{6,0},{7,1},{8,14},{9,15},{10,... | collective-permute-start | bytes 1572872 | tf_op jit(solution)/shard_map/ppermute | solution.py:602
  87.0 28.9 %collective-permute-start.9 = (bf16[512,512]{1,0:T(8,128)(2,1)S(1)}, bf16[512,512]{1,0:T(8,128)(2,1)S(1)}, u32[]{:S(2)}, u32[]{:S(2)}) collective-permute-start(bf16[512,512]{1,0:T(8,128)(2,1)S(1)} %get-tuple-element.16), channel_id=1, source_target_pairs={{0,2},{1,3},{2,0},{3,1},{4,6},{5,7},{6,4},{7,5},{8,10},{9,11},{10,... | collective-permute-start | bytes 1572872 | tf_op jit(solution)/shard_map/ppermute | solution.py:602
  115.9 1.3 %copy-start.2 = (bf16[512,2048]{1,0:T(8,128)(2,1)}, bf16[512,2048]{1,0:T(8,128)(2,1)S(1)}, u32[]{:S(2)}) copy-start(bf16[512,2048]{1,0:T(8,128)(2,1)S(1)} %constant_dynamic-update-slice_fusion.1) | copy-start | bytes 6291460
